TPU v7x, 32 devices: a whole 2x2x4 slice. The times are simulated.
32 devices in a mesh: row: 8 (over y, x, core), col: 4 (over z).
Axes of the slice: x: 2, y: 2, z: 4, core: 2. Of those that a mesh axis runs over, the one named last changes fastest.
Arguments:
- objects: float32 [4, 4096, 2048], P(None, 'row', 'col'), may hold values from -1 to 1, as said below
- probe: float32 [2, 256, 256], replicated, may hold values from -6 to 6
- kernel: float32 [2, 256, 256], replicated, may hold values from -1 to 1, as said below
- measured: float32 [8, 4, 9, 256, 256], P('row', 'col'), may hold values from 0.3 to 3
- offsets: int32 [8, 4, 9, 2], P('row', 'col'), may hold values from -64 to 320, as said below
Outputs:
- updated: float32 [4, 4096, 2048], P(None, 'row', 'col')
Inputs may be any that keep to these rules, and one draw needn't show every extreme that they name: Every window lies inside the object: tiles in the first row or column have offsets of 0 or more there, tiles in the last have offsets of at most 256 there. `objects`: real and imaginary parts of each slice give a magnitude between 0.6 and 1. `kernel`: each entry has magnitude 1.
All inputs are finite; a program needn't handle non-finite values.
Results may differ from a plain program's by a relative error of at most 0.012.
Values sent between devices are 32-bit elements; how exact they have to be, the bound alone decides.
No kernel may reach another device: no remote copies, remote signals or barrier semaphores. Data moves between devices by JAX's collectives and lax.ppermute only.
A program may use at most 128 MiB of HBM per device.

v0:
```python
import jax
import jax.numpy as jnp
from jax import lax
from jax.sharding import PartitionSpec as P

HALO = 64


RATE = 0.5


def padded_2(x, sides, width):
    for axis, dim in sides:
        devices, length = (lax.axis_size(axis), x.shape[dim])
        up = [(i, (i + 1) % devices) for i in range(devices - 1)]
        down = [(j, i) for i, j in up]
        last = lax.slice_in_dim(x, length - width, length, axis=dim)
        initial = lax.slice_in_dim(x, 0, width, axis=dim)
        before = lax.ppermute(last, axis, up)
        after = lax.ppermute(initial, axis, down)
        x = jnp.concatenate([before, x, after], axis=dim)
    return x


def make_tables(width):
    index = jnp.arange(width, dtype=jnp.int32)
    product = index[:, None] * index[None, :] % width
    angle = 2.0 * jnp.pi / width * product.astype(jnp.float32)
    norm = 1.0 / jnp.sqrt(jnp.float32(width))
    cosine = jnp.cos(angle) * norm
    sine = jnp.sin(angle) * norm

    def blocks(real_part, imag_part):
        left = jnp.concatenate(
            [
                jnp.concatenate([real_part, -imag_part], 1),
                jnp.concatenate([imag_part, real_part], 1),
            ],
            0,
        )
        right = jnp.concatenate(
            [
                jnp.concatenate([real_part, imag_part], 1),
                jnp.concatenate([-imag_part, real_part], 1),
            ],
            0,
        )
        return (left.astype(jnp.bfloat16), right.astype(jnp.bfloat16))

    return (blocks(cosine, -sine), blocks(cosine, sine))


def transform(real_part, imag_part, table):
    left, right = table
    width = real_part.shape[0]
    stacked = jnp.concatenate([real_part, imag_part], 0).astype(jnp.bfloat16)
    first = jnp.dot(left, stacked, preferred_element_type=jnp.float32)
    middle = jnp.concatenate([first[:width], first[width:]], 1).astype(jnp.bfloat16)
    result = jnp.dot(middle, right, preferred_element_type=jnp.float32)
    return (result[:, :width], result[:, width:])


def position_gradient(window, probe, kernel, amplitude, tables):
    forward, inverse = tables
    o1r, o1i, o2r, o2i = (window[0], window[1], window[2], window[3])
    pr, pim = (probe[0], probe[1])
    kr, kim = (kernel[0], kernel[1])
    ar = pr * o1r - pim * o1i
    ai = pr * o1i + pim * o1r
    fr, fi = transform(ar, ai, forward)
    br = kr * fr - kim * fi
    bi = kr * fi + kim * fr
    sr, si = transform(br, bi, inverse)
    er = sr * o2r - si * o2i
    ei = sr * o2i + si * o2r
    zr, zi = transform(er, ei, forward)
    factor = 1.0 - amplitude / jnp.sqrt(zr * zr + zi * zi + 1.0)
    gr, gi = transform(zr * factor, zi * factor, inverse)
    g2r = sr * gr + si * gi
    g2i = sr * gi - si * gr
    hr = o2r * gr + o2i * gi
    hi = o2r * gi - o2i * gr
    ur, ui = transform(hr, hi, forward)
    vr = kr * ur + kim * ui
    vi = kr * ui - kim * ur
    wr, wi = transform(vr, vi, inverse)
    g1r = pr * wr + pim * wi
    g1i = pr * wi - pim * wr
    return jnp.stack([g1r, g1i, g2r, g2i])


def per_device(objects, probe, kernel, measured, offsets):
    tile = objects.shape[1]
    width = probe.shape[1]
    margin = HALO
    extent = tile + 2 * margin
    tables = make_tables(width)
    zero = jnp.zeros((), jnp.int32)
    padded = padded_2(objects, (("row", 1), ("col", 2)), margin)
    source_cols = jnp.arange(width, dtype=jnp.int32)[:, None]
    target_cols = jnp.arange(extent, dtype=jnp.int32)[None, :]

    def accumulate(which, gradient):
        top = offsets[0, 0, which, 0] + margin
        left = offsets[0, 0, which, 1] + margin
        window = lax.dynamic_slice(padded, (zero, top, left), (4, width, width))
        piece = position_gradient(window, probe, kernel, measured[0, 0, which], tables)
        placer = (source_cols + left == target_cols).astype(jnp.float32)
        spread = jnp.dot(
            piece.reshape(4 * width, width),
            placer,
            precision=lax.Precision.HIGHEST,
            preferred_element_type=jnp.float32,
        )
        spread = spread.reshape(4, width, extent)
        current = lax.dynamic_slice(gradient, (zero, top, zero), (4, width, extent))
        return lax.dynamic_update_slice(gradient, current + spread, (zero, top, zero))

    gradient = lax.fori_loop(
        0, offsets.shape[2], accumulate, jnp.zeros((4, extent, extent), jnp.float32)
    )
    cycle = padded_2(gradient, (("row", 1), ("col", 2)), margin)
    inner = gradient[:, margin : margin + tile, margin : margin + tile]
    gap_rows = jnp.zeros((4, tile - 2 * margin, tile), jnp.float32)
    gap_cols = jnp.zeros((4, tile, tile - 2 * margin), jnp.float32)
    gap_corner = jnp.zeros((4, margin, tile - 2 * margin), jnp.float32)
    top = cycle[:, :margin, 2 * margin : 2 * margin + tile]
    bottom = cycle[:, extent + margin :, 2 * margin : 2 * margin + tile]
    left = cycle[:, 2 * margin : 2 * margin + tile, :margin]
    right = cycle[:, 2 * margin : 2 * margin + tile, extent + margin :]
    corner_top = jnp.concatenate(
        [cycle[:, :margin, :margin], gap_corner, cycle[:, :margin, extent + margin :]], 2
    )
    corner_bottom = jnp.concatenate(
        [
            cycle[:, extent + margin :, :margin],
            gap_corner,
            cycle[:, extent + margin :, extent + margin :],
        ],
        2,
    )
    vertical = jnp.concatenate([top + corner_top, gap_rows, bottom + corner_bottom], 1)
    horizontal = jnp.concatenate([left, gap_cols, right], 2)
    total = inner + vertical + horizontal
    return objects - RATE * total


def solution(mesh):
    return jax.shard_map(
        per_device,
        mesh=mesh,
        in_specs=(
            P(None, "row", "col"),
            P(),
            P(),
            P("row", "col", None, None, None),
            P("row", "col", None, None),
        ),
        out_specs=P(None, "row", "col"),
        check_vma=False,
    )
```

profile of v0, /device:TPU:2, one launch (start us, length us, event | category | flops | bytes accessed | tf_op | source)
XLA Modules:
  0.0 406.1 jit_solution(2098962630960405815)
XLA Ops:
  3.2 3.6 collective-permute-start.1
  6.9 5.2 %copy.18 = f32[4,512,512]{1,2,0:T(8,128)} copy(f32[4,512,512]{2,1,0:T(8,128)} %param.7) | data formatting | bytes 8388608 | tf_op args[0]
  12.5 4.0 collective-permute-done.1
  19.5 3.5 collective-permute-start.2
  27.3 10.3 %collective-permute-done.2 = f32[4,640,64]{1,2,0:T(8,128)S(1)} collective-permute-done((f32[4,640,64]{1,2,0:T(8,128)}, f32[4,640,64]{1,2,0:T(8,128)S(1)}, u32[]{:S(2)}, u32[]{:S(2)}) %collective-permute-start.2) | collective-permute-done | bytes 655392 | tf_op jit(solution)/shard_map/ppermute | solution.py:19
  37.7 4.8 %collective-permute-done.3 = f32[4,640,64]{1,2,0:T(8,128)} collective-permute-done((f32[4,640,64]{1,2,0:T(8,128)}, f32[4,640,64]{1,2,0:T(8,128)}, u32[]{:S(2)}, u32[]{:S(2)}) %collective-permute-start.3) | collective-permute-done | bytes 655392 | tf_op jit(solution)/shard_map/ppermute | solution.py:20
  42.4 5.9 %pad_maximum_fusion = f32[4,640,640]{1,2,0:T(8,128)} fusion(f32[4,640,64]{1,2,0:T(8,128)} %collective-permute-done.3, f32[4,64,512]{1,2,0:T(8,128)S(1)} %copy.19, f32[4,512,512]{1,2,0:T(8,128)} %copy.18, f32[4,64,512]{1,2,0:T(8,128)S(1)} %copy.17, f32[4,640,64]{1,2,0:T(8,128)S(1)} %collective-permute-done.2), kind=kLoop, calls=%fused_computation.138 | loop fusion | flops 6553600 | bytes 13107200 | tf_op jit(solution)/shard_map/concatenate | solution.py:21
  51.5 298.6 %while.17 = (s32[]{:T(128)}, f32[4,640,640]{2,1,0:T(8,128)}, s32[1,1,9,2]{2,3,1,0:T(2,128)S(1)}, f32[2,256,256]{2,1,0:T(8,128)}, f32[2,256,256]{2,1,0:T(8,128)},...) while((s32[]{:T(128)}, f32[4,640,640]{2,1,0:T(8,128)}, ...), condition=%wide.region_1.2_spmd.clone, body=%wide.region_0.1_spmd.clone.sunk | while | flops 3636625664 | bytes 43256140 | solution.py:119
  73.2 3.4 dynamic-slice_add_fusion.2
  76.6 8.2 %dynamic_update_slice.13 = f32[4,640,640]{2,1,0:T(8,128)} dynamic-update-slice(f32[4,640,640]{2,1,0:T(8,128)} %get-tuple-element.589, f32[4,256,640]{2,1,0:T(8,128)S(1)} %dynamic-slice_add_fusion.2, s32[]{:T(128)} %constant.93.clone.1..sunk, s32[]{:T(128)S(6)} %select_n.72, s32[]{:T(128)} %constant.93.clone.1..sunk) | dynamic-update-slice | bytes 5242884 | tf_op jit(solution)/shard_map/while/body/eval_jaxpr/dynamic_update_slice | solution.py:117
  109.8 8.2 %dynamic_update_slice.13 = f32[4,640,640]{2,1,0:T(8,128)} dynamic-update-slice(f32[4,640,640]{2,1,0:T(8,128)} %get-tuple-element.589, f32[4,256,640]{2,1,0:T(8,128)S(1)} %dynamic-slice_add_fusion.2, s32[]{:T(128)} %constant.93.clone.1..sunk, s32[]{:T(128)S(6)} %select_n.72, s32[]{:T(128)} %constant.93.clone.1..sunk) | dynamic-update-slice | bytes 5242884 | tf_op jit(solution)/shard_map/while/body/eval_jaxpr/dynamic_update_slice | solution.py:117
  143.0 8.2 %dynamic_update_slice.13 = f32[4,640,640]{2,1,0:T(8,128)} dynamic-update-slice(f32[4,640,640]{2,1,0:T(8,128)} %get-tuple-element.589, f32[4,256,640]{2,1,0:T(8,128)S(1)} %dynamic-slice_add_fusion.2, s32[]{:T(128)} %constant.93.clone.1..sunk, s32[]{:T(128)S(6)} %select_n.72, s32[]{:T(128)} %constant.93.clone.1..sunk) | dynamic-update-slice | bytes 5242884 | tf_op jit(solution)/shard_map/while/body/eval_jaxpr/dynamic_update_slice | solution.py:117
  176.2 8.2 %dynamic_update_slice.13 = f32[4,640,640]{2,1,0:T(8,128)} dynamic-update-slice(f32[4,640,640]{2,1,0:T(8,128)} %get-tuple-element.589, f32[4,256,640]{2,1,0:T(8,128)S(1)} %dynamic-slice_add_fusion.2, s32[]{:T(128)} %constant.93.clone.1..sunk, s32[]{:T(128)S(6)} %select_n.72, s32[]{:T(128)} %constant.93.clone.1..sunk) | dynamic-update-slice | bytes 5242884 | tf_op jit(solution)/shard_map/while/body/eval_jaxpr/dynamic_update_slice | solution.py:117
  209.5 8.2 %dynamic_update_slice.13 = f32[4,640,640]{2,1,0:T(8,128)} dynamic-update-slice(f32[4,640,640]{2,1,0:T(8,128)} %get-tuple-element.589, f32[4,256,640]{2,1,0:T(8,128)S(1)} %dynamic-slice_add_fusion.2, s32[]{:T(128)} %constant.93.clone.1..sunk, s32[]{:T(128)S(6)} %select_n.72, s32[]{:T(128)} %constant.93.clone.1..sunk) | dynamic-update-slice | bytes 5242884 | tf_op jit(solution)/shard_map/while/body/eval_jaxpr/dynamic_update_slice | solution.py:117
  242.7 8.2 %dynamic_update_slice.13 = f32[4,640,640]{2,1,0:T(8,128)} dynamic-update-slice(f32[4,640,640]{2,1,0:T(8,128)} %get-tuple-element.589, f32[4,256,640]{2,1,0:T(8,128)S(1)} %dynamic-slice_add_fusion.2, s32[]{:T(128)} %constant.93.clone.1..sunk, s32[]{:T(128)S(6)} %select_n.72, s32[]{:T(128)} %constant.93.clone.1..sunk) | dynamic-update-slice | bytes 5242884 | tf_op jit(solution)/shard_map/while/body/eval_jaxpr/dynamic_update_slice | solution.py:117
  275.9 8.0 %dynamic_update_slice.13 = f32[4,640,640]{2,1,0:T(8,128)} dynamic-update-slice(f32[4,640,640]{2,1,0:T(8,128)} %get-tuple-element.589, f32[4,256,640]{2,1,0:T(8,128)S(1)} %dynamic-slice_add_fusion.2, s32[]{:T(128)} %constant.93.clone.1..sunk, s32[]{:T(128)S(6)} %select_n.72, s32[]{:T(128)} %constant.93.clone.1..sunk) | dynamic-update-slice | bytes 5242884 | tf_op jit(solution)/shard_map/while/body/eval_jaxpr/dynamic_update_slice | solution.py:117
  309.0 8.1 %dynamic_update_slice.13 = f32[4,640,640]{2,1,0:T(8,128)} dynamic-update-slice(f32[4,640,640]{2,1,0:T(8,128)} %get-tuple-element.589, f32[4,256,640]{2,1,0:T(8,128)S(1)} %dynamic-slice_add_fusion.2, s32[]{:T(128)} %constant.93.clone.1..sunk, s32[]{:T(128)S(6)} %select_n.72, s32[]{:T(128)} %constant.93.clone.1..sunk) | dynamic-update-slice | bytes 5242884 | tf_op jit(solution)/shard_map/while/body/eval_jaxpr/dynamic_update_slice | solution.py:117
  342.1 8.0 %dynamic_update_slice.13 = f32[4,640,640]{2,1,0:T(8,128)} dynamic-update-slice(f32[4,640,640]{2,1,0:T(8,128)} %get-tuple-element.589, f32[4,256,640]{2,1,0:T(8,128)S(1)} %dynamic-slice_add_fusion.2, s32[]{:T(128)} %constant.93.clone.1..sunk, s32[]{:T(128)S(6)} %select_n.72, s32[]{:T(128)} %constant.93.clone.1..sunk) | dynamic-update-slice | bytes 5242884 | tf_op jit(solution)/shard_map/while/body/eval_jaxpr/dynamic_update_slice | solution.py:117
  353.8 3.5 collective-permute-start.5
  357.3 8.2 %copy.22 = f32[4,640,640]{1,2,0:T(8,128)} copy(f32[4,640,640]{2,1,0:T(8,128)} %get-tuple-element.337) | data formatting | bytes 13107200 | tf_op jit(solution)/shard_map/while | solution.py:119
  372.4 3.6 collective-permute-start.6
  377.4 14.0 %collective-permute-done.6 = f32[4,768,64]{1,2,0:T(8,128)S(1)} collective-permute-done((f32[4,768,64]{1,2,0:T(8,128)S(1)}, f32[4,768,64]{1,2,0:T(8,128)S(1)}, u32[]{:S(2)}, u32[]{:S(2)}) %collective-permute-start.6) | collective-permute-done | bytes 786464 | tf_op jit(solution)/shard_map/ppermute | solution.py:19
  391.6 4.2 %collective-permute-done.7 = f32[4,768,64]{1,2,0:T(8,128)S(1)} collective-permute-done((f32[4,768,64]{1,2,0:T(8,128)}, f32[4,768,64]{1,2,0:T(8,128)S(1)}, u32[]{:S(2)}, u32[]{:S(2)}) %collective-permute-start.7) | collective-permute-done | bytes 786464 | tf_op jit(solution)/shard_map/ppermute | solution.py:20
  399.9 6.1 %fusion.102 = f32[4,512,512]{2,1,0:T(8,128)} fusion(f32[4,512,512]{2,1,0:T(8,128)} %param.7, f32[4,64,512]{2,1,0:T(8,128)S(1)} %get-tuple-element.446, f32[4,64,512]{2,1,0:T(8,128)S(1)} %get-tuple-element.445, f32[4,512,64]{2,1,0:T(8,128)S(1)} %copy.29, f32[4,512,64]{2,1,0:T(8,128)S(1)} %copy.28, f32[4,640,640]{2,1,0:T(8,128)} %get-tuple-element.337, ...), kind=kLoop, calls=%fused_computation.142 | loop fusion | flops 8388608 | bytes 15732736 | tf_op jit(solution)/shard_map/sub | solution.py:145
  (334 shorter events, 227.4 us)
Async XLA Ops:
  1.3 10.8 %collective-permute-start = (f32[4,64,512]{2,1,0:T(8,128)S(1)}, f32[4,64,512]{2,1,0:T(8,128)S(1)}, u32[]{:S(2)}, u32[]{:S(2)}) collective-permute-start(f32[4,64,512]{2,1,0:T(8,128)S(1)} %get-tuple-element.437), channel_id=1, source_target_pairs={{0,4},{4,8},{8,12},{12,16},{16,20},{20,24},{24,28},{1,5},{5,9},{9,... | collective-permute-start | bytes 1572872 | tf_op jit(solution)/shard_map/ppermute | solution.py:19
  3.2 13.2 %collective-permute-start.1 = (f32[4,64,512]{2,1,0:T(8,128)S(1)}, f32[4,64,512]{2,1,0:T(8,128)S(1)}, u32[]{:S(2)}, u32[]{:S(2)}) collective-permute-start(f32[4,64,512]{2,1,0:T(8,128)S(1)} %get-tuple-element.438), channel_id=1, source_target_pairs={{4,0},{8,4},{12,8},{16,12},{20,16},{24,20},{28,24},{5,1},{9,5},{13... | collective-permute-start | bytes 1572872 | tf_op jit(solution)/shard_map/ppermute | solution.py:20
  19.5 18.1 %collective-permute-start.2 = (f32[4,640,64]{1,2,0:T(8,128)}, f32[4,640,64]{1,2,0:T(8,128)S(1)}, u32[]{:S(2)}, u32[]{:S(2)}) collective-permute-start(f32[4,640,64]{1,2,0:T(8,128)} %get-tuple-element.435), channel_id=1, source_target_pairs={{0,1},{1,2},{2,3},{4,5},{5,6},{6,7},{8,9},{9,10},{10,11},{12,13},{... | collective-permute-start | bytes 1966088 | tf_op jit(solution)/shard_map/ppermute | solution.py:19
  23.0 19.4 %collective-permute-start.3 = (f32[4,640,64]{1,2,0:T(8,128)}, f32[4,640,64]{1,2,0:T(8,128)}, u32[]{:S(2)}, u32[]{:S(2)}) collective-permute-start(f32[4,640,64]{1,2,0:T(8,128)} %get-tuple-element.436), channel_id=1, source_target_pairs={{1,0},{2,1},{3,2},{5,4},{6,5},{7,6},{9,8},{10,9},{11,10},{13,12},{... | collective-permute-start | bytes 1966088 | tf_op jit(solution)/shard_map/ppermute | solution.py:20
  48.3 3.2 copy-start.2
  351.5 13.9 %collective-permute-start.4 = (f32[4,64,640]{2,1,0:T(8,128)S(1)}, f32[4,64,640]{2,1,0:T(8,128)S(1)}, u32[]{:S(2)}, u32[]{:S(2)}) collective-permute-start(f32[4,64,640]{2,1,0:T(8,128)S(1)} %get-tuple-element.433), channel_id=1, source_target_pairs={{0,4},{4,8},{8,12},{12,16},{16,20},{20,24},{24,28},{1,5},{5,9},{9,... | collective-permute-start | bytes 1966088 | tf_op jit(solution)/shard_map/ppermute | solution.py:19
  353.8 14.4 %collective-permute-start.5 = (f32[4,64,640]{2,1,0:T(8,128)S(1)}, f32[4,64,640]{2,1,0:T(8,128)}, u32[]{:S(2)}, u32[]{:S(2)}) collective-permute-start(f32[4,64,640]{2,1,0:T(8,128)S(1)} %get-tuple-element.434), channel_id=1, source_target_pairs={{4,0},{8,4},{12,8},{16,12},{20,16},{24,20},{28,24},{5,1},{9,5},{13... | collective-permute-start | bytes 1966088 | tf_op jit(solution)/shard_map/ppermute | solution.py:20
  365.5 0.8 copy-start
  372.4 25.9 %copy-start.1 = (f32[4,64,640]{2,1,0:T(8,128)S(1)}, f32[4,64,640]{2,1,0:T(8,128)}, u32[]{:S(2)}) copy-start(f32[4,64,640]{2,1,0:T(8,128)} %copy-done) | copy-start | bytes 1966084
  372.4 19.0 %collective-permute-start.6 = (f32[4,768,64]{1,2,0:T(8,128)S(1)}, f32[4,768,64]{1,2,0:T(8,128)S(1)}, u32[]{:S(2)}, u32[]{:S(2)}) collective-permute-start(f32[4,768,64]{1,2,0:T(8,128)S(1)} %get-tuple-element.431), channel_id=1, source_target_pairs={{0,1},{1,2},{2,3},{4,5},{5,6},{6,7},{8,9},{9,10},{10,11},{12,13},{... | collective-permute-start | bytes 2359304 | tf_op jit(solution)/shard_map/ppermute | solution.py:19
  376.0 19.8 %collective-permute-start.7 = (f32[4,768,64]{1,2,0:T(8,128)}, f32[4,768,64]{1,2,0:T(8,128)S(1)}, u32[]{:S(2)}, u32[]{:S(2)}) collective-permute-start(f32[4,768,64]{1,2,0:T(8,128)} %get-tuple-element.432), channel_id=1, source_target_pairs={{1,0},{2,1},{3,2},{5,4},{6,5},{7,6},{9,8},{10,9},{11,10},{13,12},{... | collective-permute-start | bytes 2359304 | tf_op jit(solution)/shard_map/ppermute | solution.py:20
where the time goes:
time: 413 us; the launch traced here: 406 us
  local copies, waits for them, and re-layouts  125 us (30%)
  matrix products  122 us (30%)
  other arithmetic  73.4 us (18%)
  waiting for transfers between devices  39.2 us (9%)
  loops' own time  24.9 us (6%)
  starting transfers between devices  21 us (5%)
    dynamic_update_slice x9, local copies, waits for them, and re-layouts, accumulate(): lax.dynamic_update_slice(gradient, current + spread, (zero, top, zero))  73.2 us
    dot_general x54, matrix products, transform(): first = jnp.dot(left, stacked, preferred_element_type=jnp.float32)  46.8 us
    dot_general x54, matrix products, transform(): result = jnp.dot(middle, right, preferred_element_type=jnp.float32)  45.1 us
    another operation x56, other arithmetic  43.4 us
    dot_general x9, matrix products, accumulate(): jnp.dot(piece.reshape(4 * width, width), placer, precision=lax.Precision....  30.3 us
    another operation x1, loops' own time, per_device(): lax.fori_loop(0, offsets.shape[2], accumulate, jnp.zeros((4, extent, exte...  24.9 us
    ppermute x4, waiting for transfers between devices, padded_2(): before = lax.ppermute(last, axis, up)  24.4 us
    slice x9, local copies, waits for them, and re-layouts, position_gradient(): o1r, o1i, o2r, o2i = (window[0], window[1], window[2], window[3])  15.5 us
  transfers between devices with their start and end apart: 8, of which 6 were waited for; matrix products, arithmetic and copies ran while one was open for 4% of the time, Pallas kernels for 0%

commit v1 on v0

v1 whole, which is shorter than its diff:
```python
import functools
import jax
import jax.numpy as jnp
import numpy as np
from jax import lax
from jax.experimental import pallas as pl
from jax.experimental.pallas import tpu as pltpu
from jax.sharding import PartitionSpec as P

HALO = 64
RATE = 0.5
LANES = 128
ROWS = 8


def make_tables(width):
    half = width // 2
    index = np.arange(width)
    angle = 2.0 * np.pi / width * (index[:, None] * index[None, :] % width)
    cosine = np.cos(angle) / np.sqrt(width)
    sine = np.sin(angle) / np.sqrt(width)

    def block(parity):
        c, s = cosine[parity::2, :half], sine[parity::2, :half]
        return np.block([[c, s], [-s, c]])

    even, odd = block(0), block(1)
    order = np.zeros((width, width))
    order[index[0::2], np.arange(half)] = 1.0
    order[index[1::2], half + np.arange(half)] = 1.0
    return np.stack([even, odd, even.T, odd.T, order]).astype(jnp.bfloat16)


def dot(a, b):
    return jnp.dot(a, b, preferred_element_type=jnp.float32)


def forward(xr, xi, tables):
    half = xr.shape[0] // 2
    le, lo, re, ro = tables[0], tables[1], tables[2], tables[3]
    u = jnp.concatenate([xr[:half] + xr[half:], xi[:half] + xi[half:]], 0)
    v = jnp.concatenate([xr[:half] - xr[half:], xi[:half] - xi[half:]], 0)
    e = dot(le, u.astype(jnp.bfloat16))
    o = dot(lo, v.astype(jnp.bfloat16))

    def fold(parts):
        fr, fi = parts[:half], parts[half:]
        p = jnp.concatenate([fr[:, :half] + fr[:, half:], fi[:, :half] + fi[:, half:]], 1)
        m = jnp.concatenate([fr[:, :half] - fr[:, half:], fi[:, :half] - fi[:, half:]], 1)
        return p.astype(jnp.bfloat16), m.astype(jnp.bfloat16)

    pe, me = fold(e)
    po, mo = fold(o)
    y = dot(jnp.concatenate([pe, po], 0), re)
    z = dot(jnp.concatenate([me, mo], 0), ro)
    return (
        jnp.concatenate([y[:, :half], z[:, :half]], 1),
        jnp.concatenate([y[:, half:], z[:, half:]], 1),
    )


def inverse(xr, xi, tables):
    half = xr.shape[0] // 2
    le, lo, re, ro = tables[2], tables[3], tables[0], tables[1]
    e = dot(le, jnp.concatenate([xr[:half], xi[:half]], 0).astype(jnp.bfloat16))
    o = dot(lo, jnp.concatenate([xr[half:], xi[half:]], 0).astype(jnp.bfloat16))
    p = (e + o).astype(jnp.bfloat16)
    m = (e - o).astype(jnp.bfloat16)

    def pick(cols):
        return jnp.concatenate(
            [
                jnp.concatenate([p[:half, cols], p[half:, cols]], 1),
                jnp.concatenate([m[:half, cols], m[half:, cols]], 1),
            ],
            0,
        )

    y = dot(pick(slice(0, half)), re)
    z = dot(pick(slice(half, 2 * half)), ro)
    s, d = y + z, y - z
    return (
        jnp.concatenate([s[:, :half], d[:, :half]], 1),
        jnp.concatenate([s[:, half:], d[:, half:]], 1),
    )


def reorder(x, order, stage):
    half = x.shape[0] // 2
    high = x.astype(jnp.bfloat16)
    low = (x - high.astype(jnp.float32)).astype(jnp.bfloat16)
    columns = dot(high, order) + dot(low, order)
    parts = []
    for k in range(2):
        stage[k] = columns[:, k * LANES : (k + 1) * LANES]
        parts.append(
            jnp.concatenate([stage[k, pl.ds(0, half, 2), :], stage[k, pl.ds(1, half, 2), :]], 0)
        )
    return jnp.concatenate(parts, 1)


def rolled(x, down, right):
    return pltpu.roll(pltpu.roll(x, down, 0), right, 1)


def masks(down, right):
    sub = lax.broadcasted_iota(jnp.int32, (ROWS, LANES), 0) >= down
    lane = lax.broadcasted_iota(jnp.int32, (1, LANES), 1) >= right
    return sub, lane


def window(ref, channel, row, tile, down, right, width):
    sub, lane = masks(down, right)
    parts = []
    for k in range(3):
        at = ref[channel, tile + k, pl.ds(row, width), :]
        after = ref[channel, tile + k, pl.ds(row + width, ROWS), :]
        parts.append(jnp.concatenate([jnp.where(sub, at[:ROWS], after), at[ROWS:]], 0))
    return jnp.concatenate([jnp.where(lane, parts[0], parts[2]), parts[1]], 1)


def accumulate(ref, channel, row, tile, down, right, value):
    width = value.shape[0]
    sub, lane = masks(down, right)
    first = value[:, :LANES]
    for k, part in enumerate(
        (jnp.where(lane, first, 0.0), value[:, LANES:], jnp.where(lane, 0.0, first))
    ):
        head = part[:ROWS]
        ref[channel, tile + k, pl.ds(row, ROWS), :] += jnp.where(sub, head, 0.0)
        ref[channel, tile + k, pl.ds(row + ROWS, width - ROWS), :] += part[ROWS:]
        ref[channel, tile + k, pl.ds(row + width, ROWS), :] += jnp.where(sub, 0.0, head)


def body(offsets, padded, probe, kernel, measured, tables, gradient, spectrum, stage):
    width = probe.shape[1]
    position = pl.program_id(0)

    @pl.when(position == 0)
    def _():
        gradient[...] = jnp.zeros_like(gradient)
        for part in range(2):
            spectrum[part] = reorder(kernel[part], tables[4], stage)

    top = offsets[position, 0] + HALO
    left = offsets[position, 1] + LANES
    down, right = top % ROWS, left % LANES
    row, tile = pl.multiple_of(top - down, ROWS), left // LANES
    place = (row, tile, down, right)

    pr, pim = rolled(probe[0], down, right), rolled(probe[1], down, right)
    kr, kim = spectrum[0], spectrum[1]
    o1r = window(padded, 0, *place, width)
    o1i = window(padded, 1, *place, width)
    fr, fi = forward(pr * o1r - pim * o1i, pr * o1i + pim * o1r, tables)
    sr, si = inverse(kr * fr - kim * fi, kr * fi + kim * fr, tables)
    o2r = window(padded, 2, *place, width)
    o2i = window(padded, 3, *place, width)
    zr, zi = forward(sr * o2r - si * o2i, sr * o2i + si * o2r, tables)
    amplitude = reorder(measured[0], tables[4], stage)
    factor = 1.0 - amplitude * lax.rsqrt(zr * zr + zi * zi + 1.0)
    gr, gi = inverse(zr * factor, zi * factor, tables)
    accumulate(gradient, 2, *place, sr * gr + si * gi)
    accumulate(gradient, 3, *place, sr * gi - si * gr)
    ur, ui = forward(o2r * gr + o2i * gi, o2r * gi - o2i * gr, tables)
    wr, wi = inverse(kr * ur + kim * ui, kr * ui - kim * ur, tables)
    accumulate(gradient, 0, *place, pr * wr + pim * wi)
    accumulate(gradient, 1, *place, pr * wi - pim * wr)


def gradients(offsets, padded, probe, kernel, measured, tables):
    count, width = measured.shape[0], measured.shape[1]
    whole = pl.BlockSpec(memory_space=pltpu.VMEM)
    return pl.pallas_call(
        body,
        out_shape=jax.ShapeDtypeStruct(padded.shape, jnp.float32),
        grid_spec=pltpu.PrefetchScalarGridSpec(
            num_scalar_prefetch=1,
            grid=(count,),
            in_specs=[
                whole,
                whole,
                whole,
                pl.BlockSpec((1, width, width), lambda i, _: (i, 0, 0)),
                whole,
            ],
            out_specs=whole,
            scratch_shapes=[
                pltpu.VMEM((2, width, width), jnp.float32),
                pltpu.VMEM((2, width, LANES), jnp.float32),
            ],
        ),
        compiler_params=pltpu.CompilerParams(vmem_limit_bytes=56 * 1024 * 1024),
        name="positions",
    )(offsets, padded, probe, kernel, measured, tables)


def padded_2(x, sides, width):
    for axis, dim in sides:
        devices, length = (lax.axis_size(axis), x.shape[dim])
        up = [(i, (i + 1) % devices) for i in range(devices - 1)]
        down = [(j, i) for i, j in up]
        last = lax.slice_in_dim(x, length - width, length, axis=dim)
        initial = lax.slice_in_dim(x, 0, width, axis=dim)
        before = lax.ppermute(last, axis, up)
        after = lax.ppermute(initial, axis, down)
        x = jnp.concatenate([before, x, after], axis=dim)
    return x


def per_device(objects, probe, kernel, measured, offsets):
    tile = objects.shape[1]
    width = probe.shape[1]
    margin = HALO
    extent = tile + 2 * margin
    tables = jnp.asarray(make_tables(width))
    padded = padded_2(objects, (("row", 1), ("col", 2)), margin)
    padded = jnp.pad(padded, ((0, 0), (0, ROWS), (LANES - margin, LANES - margin)))
    tiles = padded.shape[2] // LANES
    padded = padded.reshape(4, extent + ROWS, tiles, LANES).transpose(0, 2, 1, 3)
    gradient = gradients(offsets[0, 0], padded, probe, kernel, measured[0, 0], tables)
    gradient = gradient.transpose(0, 2, 1, 3).reshape(4, extent + ROWS, tiles * LANES)
    gradient = gradient[:, :extent, LANES - margin : LANES - margin + extent]
    cycle = padded_2(gradient, (("row", 1), ("col", 2)), margin)
    inner = gradient[:, margin : margin + tile, margin : margin + tile]
    gap_rows = jnp.zeros((4, tile - 2 * margin, tile), jnp.float32)
    gap_cols = jnp.zeros((4, tile, tile - 2 * margin), jnp.float32)
    gap_corner = jnp.zeros((4, margin, tile - 2 * margin), jnp.float32)
    top = cycle[:, :margin, 2 * margin : 2 * margin + tile]
    bottom = cycle[:, extent + margin :, 2 * margin : 2 * margin + tile]
    left = cycle[:, 2 * margin : 2 * margin + tile, :margin]
    right = cycle[:, 2 * margin : 2 * margin + tile, extent + margin :]
    corner_top = jnp.concatenate(
        [cycle[:, :margin, :margin], gap_corner, cycle[:, :margin, extent + margin :]], 2
    )
    corner_bottom = jnp.concatenate(
        [
            cycle[:, extent + margin :, :margin],
            gap_corner,
            cycle[:, extent + margin :, extent + margin :],
        ],
        2,
    )
    vertical = jnp.concatenate([top + corner_top, gap_rows, bottom + corner_bottom], 1)
    horizontal = jnp.concatenate([left, gap_cols, right], 2)
    total = inner + vertical + horizontal
    return objects - RATE * total


def solution(mesh):
    return jax.shard_map(
        per_device,
        mesh=mesh,
        in_specs=(
            P(None, "row", "col"),
            P(),
            P(),
            P("row", "col", None, None, None),
            P("row", "col", None, None),
        ),
        out_specs=P(None, "row", "col"),
        check_vma=False,
    )
```

time: 413 us -> 162 us (0.39)
  the two profiles are of different devices: /device:TPU:2 before, /device:TPU:11 now
where the time goes in v1:
time: 162 us; the launch traced here: 159 us
  local copies, waits for them, and re-layouts  42.7 us (26%)
  waiting for transfers between devices  41.9 us (26%)
  Pallas kernels  36.3 us (22%)
  starting transfers between devices  20.8 us (13%)
  other arithmetic  17.4 us (11%)
    pallas_call x1, Pallas kernels, gradients(): pl.pallas_call(body, out_shape=jax.ShapeDtypeStruct(padded.shape, jnp.flo...  36.3 us
    ppermute x4, waiting for transfers between devices, padded_2(): before = lax.ppermute(last, axis, up)  28.8 us
    ppermute x4, waiting for transfers between devices, padded_2(): after = lax.ppermute(initial, axis, down)  13.1 us
    ppermute x4, starting transfers between devices, padded_2(): before = lax.ppermute(last, axis, up)  12.3 us
    transpose x1, local copies, waits for them, and re-layouts, per_device(): gradient.transpose(0, 2, 1, 3).reshape(4, extent + ROWS, tiles * LANES)  9.19 us
    reshape x1, local copies, waits for them, and re-layouts, per_device(): padded.reshape(4, extent + ROWS, tiles, LANES).transpose(0, 2, 1, 3)  9.15 us
    ppermute x4, starting transfers between devices, padded_2(): after = lax.ppermute(initial, axis, down)  8.54 us
    concatenate x1, other arithmetic, padded_2(): x = jnp.concatenate([before, x, after], axis=dim)  7.23 us
  transfers between devices with their start and end apart: 8, of which 8 were waited for; matrix products, arithmetic and copies ran while one was open for 8% of the time, Pallas kernels for 0%

profile of v1, /device:TPU:11, one launch (start us, length us, event | category | flops | bytes accessed | tf_op | source)
XLA Modules:
  0.0 159.3 jit_solution(2981892548418009142)
XLA Ops:
  1.3 3.7 %collective-permute-start = (f32[4,64,512]{2,1,0:T(8,128)S(1)}, f32[4,64,512]{2,1,0:T(8,128)S(1)}, u32[]{:S(2)}, u32[]{:S(2)}) collective-permute-start(f32[4,64,512]{2,1,0:T(8,128)S(1)} %get-tuple-element.11), channel_id=1, source_target_pairs={{0,4},{4,8},{8,12},{12,16},{16,20},{20,24},{24,28},{1,5},{5,9},{9,... | collective-permute-start | bytes 1572872 | tf_op jit(solution)/shard_map/ppermute | solution.py:205
  5.0 1.9 %collective-permute-start.1 = (f32[4,64,512]{2,1,0:T(8,128)S(1)}, f32[4,64,512]{2,1,0:T(8,128)S(1)}, u32[]{:S(2)}, u32[]{:S(2)}) collective-permute-start(f32[4,64,512]{2,1,0:T(8,128)S(1)} %get-tuple-element.12), channel_id=1, source_target_pairs={{4,0},{8,4},{12,8},{16,12},{20,16},{24,20},{28,24},{5,1},{9,5},{13... | collective-permute-start | bytes 1572872 | tf_op jit(solution)/shard_map/ppermute | solution.py:206
  6.9 5.2 %copy.40 = f32[4,512,512]{1,2,0:T(8,128)} copy(f32[4,512,512]{2,1,0:T(8,128)} %param.6) | data formatting | bytes 8388608 | tf_op args[0]
  14.2 4.1 %collective-permute-done.1 = f32[4,64,512]{2,1,0:T(8,128)S(1)} collective-permute-done((f32[4,64,512]{2,1,0:T(8,128)S(1)}, f32[4,64,512]{2,1,0:T(8,128)S(1)}, u32[]{:S(2)}, u32[]{:S(2)}) %collective-permute-start.1) | collective-permute-done | bytes 524320 | tf_op jit(solution)/shard_map/ppermute | solution.py:206
  18.7 2.8 %pad_maximum_fusion.5 = (f32[4,640,64]{1,2,0:T(8,128)}, f32[4,640,64]{1,2,0:T(8,128)}) fusion(f32[4,64,512]{1,2,0:T(8,128)S(1)} %copy.30, f32[4,512,512]{1,2,0:T(8,128)} %copy.40, f32[4,64,512]{1,2,0:T(8,128)S(1)} %copy.28), kind=kLoop, calls=%fused_computation.26 | loop fusion | flops 655360 | bytes 6553600 | tf_op jit(solution)/shard_map/slice | solution.py:203
  21.5 3.2 %collective-permute-start.2 = (f32[4,640,64]{1,2,0:T(8,128)}, f32[4,640,64]{1,2,0:T(8,128)S(1)}, u32[]{:S(2)}, u32[]{:S(2)}) collective-permute-start(f32[4,640,64]{1,2,0:T(8,128)} %get-tuple-element.9), channel_id=1, source_target_pairs={{0,1},{1,2},{2,3},{4,5},{5,6},{6,7},{8,9},{9,10},{10,11},{12,13},{... | collective-permute-start | bytes 1966088 | tf_op jit(solution)/shard_map/ppermute | solution.py:205
  24.7 2.1 %collective-permute-start.3 = (f32[4,640,64]{1,2,0:T(8,128)}, f32[4,640,64]{1,2,0:T(8,128)S(1)}, u32[]{:S(2)}, u32[]{:S(2)}) collective-permute-start(f32[4,640,64]{1,2,0:T(8,128)} %get-tuple-element.10), channel_id=1, source_target_pairs={{1,0},{2,1},{3,2},{5,4},{6,5},{7,6},{9,8},{10,9},{11,10},{13,12},{... | collective-permute-start | bytes 1966088 | tf_op jit(solution)/shard_map/ppermute | solution.py:206
  27.5 12.0 %collective-permute-done.2 = f32[4,640,64]{1,2,0:T(8,128)S(1)} collective-permute-done((f32[4,640,64]{1,2,0:T(8,128)}, f32[4,640,64]{1,2,0:T(8,128)S(1)}, u32[]{:S(2)}, u32[]{:S(2)}) %collective-permute-start.2) | collective-permute-done | bytes 655392 | tf_op jit(solution)/shard_map/ppermute | solution.py:205
  39.5 3.2 %collective-permute-done.3 = f32[4,640,64]{1,2,0:T(8,128)S(1)} collective-permute-done((f32[4,640,64]{1,2,0:T(8,128)}, f32[4,640,64]{1,2,0:T(8,128)S(1)}, u32[]{:S(2)}, u32[]{:S(2)}) %collective-permute-start.3) | collective-permute-done | bytes 655392 | tf_op jit(solution)/shard_map/ppermute | solution.py:206
  42.7 7.2 %select_maximum_fusion = f32[4,648,768]{1,2,0:T(8,128)} fusion(f32[4,640,64]{1,2,0:T(8,128)S(1)} %collective-permute-done.3, f32[4,640,64]{1,2,0:T(8,128)S(1)} %collective-permute-done.2, f32[4,64,512]{1,2,0:T(8,128)S(1)} %copy.30, f32[4,512,512]{1,2,0:T(8,128)} %copy.40, f32[4,64,512]{1,2,0:T(8,128)S(1)} %copy.28), kind=kLoop, calls=%fused_computation.2 | loop fusion | flops 37822464 | bytes 14516224 | tf_op jit(solution)/shard_map/concatenate | solution.py:207
  50.0 9.1 %copy.31 = f32[4,648,6,128]{3,1,2,0:T(8,128)} copy(f32[4,648,6,128]{1,3,2,0:T(8,128)} %bitcast.9) | data formatting | bytes 15925248 | tf_op jit(solution)/shard_map/reshape | solution.py:220
  59.1 36.3 %positions.1 = f32[4,6,648,128]{3,2,1,0:T(8,128)} custom-call(s32[9,2]{1,0:T(8,128)} %copy.32.offsets, f32[4,6,648,128]{3,2,1,0:T(8,128)} %bitcast.10, f32[2,256,256]{2,1,0:T(8,128)} %probe.1, f32[2,256,256]{2,1,0:T(8,128)} %kernel.1, f32[9,256,256]{2,1,0:T(8,128)} %bitcast.12, bf16[5,256,256]{2,1,0:T(8,128)(2,1)} %constant.5.clone.tables), custom_call_target="tpu_custom_call" | custom-call | tf_op jit(solution)/shard_map/positions/pallas_call | solution.py:174
  95.4 9.2 %copy.33 = f32[4,648,6,128]{1,3,2,0:T(8,128)} copy(f32[4,648,6,128]{3,1,2,0:T(8,128)} %bitcast.11) | data formatting | bytes 15925248 | tf_op jit(solution)/shard_map/transpose | solution.py:222
  104.6 2.2 %fusion.13 = (f32[4,64,640]{1,2,0:T(8,128)S(1)}, f32[4,64,640]{1,2,0:T(8,128)S(1)}) fusion(f32[4,648,768]{1,2,0:T(8,128)} %bitcast.6), kind=kLoop, calls=%fused_computation.27 | loop fusion | bytes 2621440 | tf_op jit(solution)/shard_map/slice | solution.py:203
  107.2 1.9 %collective-permute-start.4 = (f32[4,64,640]{2,1,0:T(8,128)S(1)}, f32[4,64,640]{2,1,0:T(8,128)S(1)}, u32[]{:S(2)}, u32[]{:S(2)}) collective-permute-start(f32[4,64,640]{2,1,0:T(8,128)S(1)} %copy.34), channel_id=1, source_target_pairs={{0,4},{4,8},{8,12},{12,16},{16,20},{20,24},{24,28},{1,5},{5,9},{9,... | collective-permute-start | bytes 1966088 | tf_op jit(solution)/shard_map/ppermute | solution.py:205
  109.5 2.4 %collective-permute-start.5 = (f32[4,64,640]{2,1,0:T(8,128)S(1)}, f32[4,64,640]{2,1,0:T(8,128)}, u32[]{:S(2)}, u32[]{:S(2)}) collective-permute-start(f32[4,64,640]{2,1,0:T(8,128)S(1)} %copy.36), channel_id=1, source_target_pairs={{4,0},{8,4},{12,8},{16,12},{20,16},{24,20},{28,24},{5,1},{9,5},{13... | collective-permute-start | bytes 1966088 | tf_op jit(solution)/shard_map/ppermute | solution.py:206
  111.9 6.0 %slice.78 = f32[4,640,640]{1,2,0:T(8,128)} slice(f32[4,648,768]{1,2,0:T(8,128)} %bitcast.7), slice={[0:4], [0:640], [64:704]} | slice | bytes 13107200 | tf_op jit(solution)/shard_map/slice | solution.py:223
  119.5 2.9 %collective-permute-done.5 = f32[4,64,640]{2,1,0:T(8,128)} collective-permute-done((f32[4,64,640]{2,1,0:T(8,128)S(1)}, f32[4,64,640]{2,1,0:T(8,128)}, u32[]{:S(2)}, u32[]{:S(2)}) %collective-permute-start.5) | collective-permute-done | bytes 655392 | tf_op jit(solution)/shard_map/ppermute | solution.py:206
  125.7 3.5 %collective-permute-start.6 = (f32[4,768,64]{1,2,0:T(8,128)S(1)}, f32[4,768,64]{1,2,0:T(8,128)S(1)}, u32[]{:S(2)}, u32[]{:S(2)}) collective-permute-start(f32[4,768,64]{1,2,0:T(8,128)S(1)} %get-tuple-element.7), channel_id=1, source_target_pairs={{0,1},{1,2},{2,3},{4,5},{5,6},{6,7},{8,9},{9,10},{10,11},{12,13},{... | collective-permute-start | bytes 2359304 | tf_op jit(solution)/shard_map/ppermute | solution.py:205
  129.2 2.1 %collective-permute-start.7 = (f32[4,768,64]{1,2,0:T(8,128)S(1)}, f32[4,768,64]{1,2,0:T(8,128)S(1)}, u32[]{:S(2)}, u32[]{:S(2)}) collective-permute-start(f32[4,768,64]{1,2,0:T(8,128)S(1)} %get-tuple-element.8), channel_id=1, source_target_pairs={{1,0},{2,1},{3,2},{5,4},{6,5},{7,6},{9,8},{10,9},{11,10},{13,12},{... | collective-permute-start | bytes 2359304 | tf_op jit(solution)/shard_map/ppermute | solution.py:206
  131.4 13.9 %collective-permute-done.6 = f32[4,768,64]{1,2,0:T(8,128)S(1)} collective-permute-done((f32[4,768,64]{1,2,0:T(8,128)S(1)}, f32[4,768,64]{1,2,0:T(8,128)S(1)}, u32[]{:S(2)}, u32[]{:S(2)}) %collective-permute-start.6) | collective-permute-done | bytes 786464 | tf_op jit(solution)/shard_map/ppermute | solution.py:205
  145.4 2.9 %collective-permute-done.7 = f32[4,768,64]{1,2,0:T(8,128)S(1)} collective-permute-done((f32[4,768,64]{1,2,0:T(8,128)S(1)}, f32[4,768,64]{1,2,0:T(8,128)S(1)}, u32[]{:S(2)}, u32[]{:S(2)}) %collective-permute-start.7) | collective-permute-done | bytes 786464 | tf_op jit(solution)/shard_map/ppermute | solution.py:206
  148.7 5.3 %fusion.12 = f32[4,512,512]{1,2,0:T(8,128)} fusion(f32[4,512,512]{1,2,0:T(8,128)S(1)} %copy-done, f32[4,648,768]{1,2,0:T(8,128)} %bitcast.8, f32[4,64,512]{1,2,0:T(8,128)S(1)} %get-tuple-element.18, f32[4,64,512]{1,2,0:T(8,128)S(1)} %get-tuple-element.17, f32[4,512,64]{1,2,0:T(8,128)S(1)} %slice.86, f32[4,512,64]{1,2,0:T(8,128)S(1)} %slice.85, ...), kind=kLoop, calls=%fused_computation.18 | loop fusion | flops 8388608 | bytes 15732736 | tf_op jit(solution)/shard_map/sub | solution.py:247
  154.0 5.2 %copy.41 = f32[4,512,512]{2,1,0:T(8,128)} copy(f32[4,512,512]{1,2,0:T(8,128)} %fusion.12) | data formatting | bytes 8388608 | tf_op jit(solution)/shard_map/sub | solution.py:247
  (22 shorter events, 10.7 us)
Async XLA Ops:
  1.3 12.6 %collective-permute-start = (f32[4,64,512]{2,1,0:T(8,128)S(1)}, f32[4,64,512]{2,1,0:T(8,128)S(1)}, u32[]{:S(2)}, u32[]{:S(2)}) collective-permute-start(f32[4,64,512]{2,1,0:T(8,128)S(1)} %get-tuple-element.11), channel_id=1, source_target_pairs={{0,4},{4,8},{8,12},{12,16},{16,20},{20,24},{24,28},{1,5},{5,9},{9,... | collective-permute-start | bytes 1572872 | tf_op jit(solution)/shard_map/ppermute | solution.py:205
  5.0 13.4 %collective-permute-start.1 = (f32[4,64,512]{2,1,0:T(8,128)S(1)}, f32[4,64,512]{2,1,0:T(8,128)S(1)}, u32[]{:S(2)}, u32[]{:S(2)}) collective-permute-start(f32[4,64,512]{2,1,0:T(8,128)S(1)} %get-tuple-element.12), channel_id=1, source_target_pairs={{4,0},{8,4},{12,8},{16,12},{20,16},{24,20},{28,24},{5,1},{9,5},{13... | collective-permute-start | bytes 1572872 | tf_op jit(solution)/shard_map/ppermute | solution.py:206
  18.7 8.1 %copy-start.1 = (s32[1,1,9,2]{2,3,1,0:T(2,128)S(1)}, s32[1,1,9,2]{2,3,1,0:T(2,128)}, u32[]{:S(2)}) copy-start(s32[1,1,9,2]{2,3,1,0:T(2,128)} %param.10) | copy-start | bytes 220
  21.5 18.0 %collective-permute-start.2 = (f32[4,640,64]{1,2,0:T(8,128)}, f32[4,640,64]{1,2,0:T(8,128)S(1)}, u32[]{:S(2)}, u32[]{:S(2)}) collective-permute-start(f32[4,640,64]{1,2,0:T(8,128)} %get-tuple-element.9), channel_id=1, source_target_pairs={{0,1},{1,2},{2,3},{4,5},{5,6},{6,7},{8,9},{9,10},{10,11},{12,13},{... | collective-permute-start | bytes 1966088 | tf_op jit(solution)/shard_map/ppermute | solution.py:205
  24.7 18.0 %collective-permute-start.3 = (f32[4,640,64]{1,2,0:T(8,128)}, f32[4,640,64]{1,2,0:T(8,128)S(1)}, u32[]{:S(2)}, u32[]{:S(2)}) collective-permute-start(f32[4,640,64]{1,2,0:T(8,128)} %get-tuple-element.10), channel_id=1, source_target_pairs={{1,0},{2,1},{3,2},{5,4},{6,5},{7,6},{9,8},{10,9},{11,10},{13,12},{... | collective-permute-start | bytes 1966088 | tf_op jit(solution)/shard_map/ppermute | solution.py:206
  107.2 11.9 %collective-permute-start.4 = (f32[4,64,640]{2,1,0:T(8,128)S(1)}, f32[4,64,640]{2,1,0:T(8,128)S(1)}, u32[]{:S(2)}, u32[]{:S(2)}) collective-permute-start(f32[4,64,640]{2,1,0:T(8,128)S(1)} %copy.34), channel_id=1, source_target_pairs={{0,4},{4,8},{8,12},{12,16},{16,20},{20,24},{24,28},{1,5},{5,9},{9,... | collective-permute-start | bytes 1966088 | tf_op jit(solution)/shard_map/ppermute | solution.py:205
  109.5 12.9 %collective-permute-start.5 = (f32[4,64,640]{2,1,0:T(8,128)S(1)}, f32[4,64,640]{2,1,0:T(8,128)}, u32[]{:S(2)}, u32[]{:S(2)}) collective-permute-start(f32[4,64,640]{2,1,0:T(8,128)S(1)} %copy.36), channel_id=1, source_target_pairs={{4,0},{8,4},{12,8},{16,12},{20,16},{24,20},{28,24},{5,1},{9,5},{13... | collective-permute-start | bytes 1966088 | tf_op jit(solution)/shard_map/ppermute | solution.py:206
  125.7 23.0 %copy-start = (f32[4,512,512]{1,2,0:T(8,128)S(1)}, f32[4,512,512]{1,2,0:T(8,128)}, u32[]{:S(2)}) copy-start(f32[4,512,512]{1,2,0:T(8,128)} %copy.40) | copy-start | bytes 12582916
  125.7 19.6 %collective-permute-start.6 = (f32[4,768,64]{1,2,0:T(8,128)S(1)}, f32[4,768,64]{1,2,0:T(8,128)S(1)}, u32[]{:S(2)}, u32[]{:S(2)}) collective-permute-start(f32[4,768,64]{1,2,0:T(8,128)S(1)} %get-tuple-element.7), channel_id=1, source_target_pairs={{0,1},{1,2},{2,3},{4,5},{5,6},{6,7},{8,9},{9,10},{10,11},{12,13},{... | collective-permute-start | bytes 2359304 | tf_op jit(solution)/shard_map/ppermute | solution.py:205
  129.2 19.0 %collective-permute-start.7 = (f32[4,768,64]{1,2,0:T(8,128)S(1)}, f32[4,768,64]{1,2,0:T(8,128)S(1)}, u32[]{:S(2)}, u32[]{:S(2)}) collective-permute-start(f32[4,768,64]{1,2,0:T(8,128)S(1)} %get-tuple-element.8), channel_id=1, source_target_pairs={{1,0},{2,1},{3,2},{5,4},{6,5},{7,6},{9,8},{10,9},{11,10},{13,12},{... | collective-permute-start | bytes 2359304 | tf_op jit(solution)/shard_map/ppermute | solution.py:206

commit v2 on v1

--- a/solution.py
+++ b/solution.py
@@ -132,119 +132,334 @@
         ref[channel, tile + k, pl.ds(row + width, ROWS), :] += jnp.where(sub, 0.0, head)
 
 
-def body(offsets, padded, probe, kernel, measured, tables, gradient, spectrum, stage):
+def fold_pair(a, b, low_first):
+    lane = lax.broadcasted_iota(jnp.int32, (1, LANES), 1) < HALO
+    if low_first:
+        return jnp.where(lane, a, pltpu.roll(b, HALO, 1))
+    return jnp.where(lane, pltpu.roll(a, HALO, 1), b)
+
+
+def pack_body(place, left, right, outer, inner, ze, zo, de, do, ro):
+    tile = left.shape[1]
+    half = ze.shape[1]
+    corner = HALO // 2
+    even = place[1] == 0
+    for ch in range(left.shape[0]):
+        strips, corners = [], []
+        for ref, lanes, low in (
+            (left, slice(0, LANES), True),
+            (right, slice(tile - LANES, tile), False),
+        ):
+            below = jnp.concatenate([ref[ch, half:], inner[ch, :, lanes]], 0)
+            strips.append(fold_pair(ref[ch, :half], below, low))
+            corners.append(
+                fold_pair(outer[ch, :corner, lanes], outer[ch, corner:, lanes], low)
+            )
+        ze[ch] = jnp.where(even, strips[1], strips[0])
+        zo[ch] = jnp.where(even, strips[0], strips[1])
+        de[ch] = jnp.where(even, corners[1], corners[0])
+        do[ch] = jnp.where(even, corners[0], corners[1])
+        ro[ch] = outer[ch]
+
+
+def pack(place, objects, inner):
+    channels, tile = objects.shape[:2]
+    half = (tile + HALO) // 2
+    last = tile // LANES - 1
+    strip = jax.ShapeDtypeStruct((channels, half, LANES), jnp.float32)
+    corner = jax.ShapeDtypeStruct((channels, HALO // 2, LANES), jnp.float32)
+    whole = pl.BlockSpec(memory_space=pltpu.VMEM)
+    return pl.pallas_call(
+        pack_body,
+        out_shape=(strip, strip, corner, corner, jax.ShapeDtypeStruct(inner.shape, jnp.float32)),
+        grid_spec=pltpu.PrefetchScalarGridSpec(
+            num_scalar_prefetch=1,
+            grid=(1,),
+            in_specs=[
+                pl.BlockSpec((channels, tile, LANES), lambda i, _: (0, 0, 0)),
+                pl.BlockSpec((channels, tile, LANES), lambda i, _: (0, 0, last)),
+                pl.BlockSpec(
+                    (channels, HALO, tile),
+                    lambda i, place: (0, place[0] * (tile // HALO - 1), 0),
+                ),
+                whole,
+            ],
+            out_specs=[whole] * 5,
+        ),
+        compiler_params=pltpu.CompilerParams(vmem_limit_bytes=48 * 1024 * 1024),
+        name="pack",
+    )(place, objects, objects, objects, inner)
+
+
+def assemble(place, padded, ze, zo, de, do, re, ro):
+    tile = re.shape[2]
+    tiles = tile // LANES
+    half = ze.shape[1]
+    corner = HALO // 2
+    even = place[1] == 0
+    outer = pl.multiple_of(place[0] * (tile + HALO), HALO)
+    inner = pl.multiple_of((1 - place[0]) * (tile + HALO), HALO)
+    for ch in range(re.shape[0]):
+        for side, at in ((0, 0), (1, tiles + 1)):
+            strip = jnp.where(even, (zo, ze)[side][ch], (ze, zo)[side][ch])
+            piece = jnp.where(even, (do, de)[side][ch], (de, do)[side][ch])
+            turned, turned_piece = pltpu.roll(strip, HALO, 1), pltpu.roll(piece, HALO, 1)
+            first, second = (turned, strip) if side == 0 else (strip, turned)
+            near, far = (turned_piece, piece) if side == 0 else (piece, turned_piece)
+            padded[ch, at, HALO : HALO + half] = first
+            padded[ch, at, HALO + half : HALO + tile] = second[: tile - half]
+            padded[ch, at, pl.ds(inner, HALO)] = second[tile - half :]
+            padded[ch, at, pl.ds(outer, corner)] = near
+            padded[ch, at, pl.ds(outer + corner, corner)] = far
+        for k in range(tiles):
+            padded[ch, k + 1, pl.ds(inner, HALO)] = re[ch, :, k * LANES : (k + 1) * LANES]
+            padded[ch, k + 1, pl.ds(outer, HALO)] = ro[ch, :, k * LANES : (k + 1) * LANES]
+
+
+def finish(place, padded, gradient, updated, ze, zo, de, do, re, ro):
+    tile = re.shape[2]
+    tiles = tile // LANES
+    half = ze.shape[1]
+    corner = HALO // 2
+    even = place[1] == 0
+    outer = pl.multiple_of(place[0] * (tile + HALO), HALO)
+    inner = pl.multiple_of((1 - place[0]) * (tile + HALO), HALO)
+    for ch in range(re.shape[0]):
+        strips, corners = [], []
+        for at, low in ((0, False), (tiles + 1, True)):
+            first = gradient[ch, at, HALO : HALO + half]
+            second = jnp.concatenate(
+                [gradient[ch, at, HALO + half : HALO + tile], gradient[ch, at, pl.ds(inner, HALO)]],
+                0,
+            )
+            strips.append(-RATE * fold_pair(first, second, low))
+            near = gradient[ch, at, pl.ds(outer, corner)]
+            far = gradient[ch, at, pl.ds(outer + corner, corner)]
+            corners.append(-RATE * fold_pair(near, far, low))
+        ze[ch] = jnp.where(even, strips[1], strips[0])
+        zo[ch] = jnp.where(even, strips[0], strips[1])
+        de[ch] = jnp.where(even, corners[1], corners[0])
+        do[ch] = jnp.where(even, corners[0], corners[1])
+        for k in range(tiles):
+            lanes = slice(k * LANES, (k + 1) * LANES)
+            re[ch, :, lanes] = -RATE * gradient[ch, k + 1, pl.ds(inner, HALO)]
+            ro[ch, :, lanes] = -RATE * gradient[ch, k + 1, pl.ds(outer, HALO)]
+            updated[ch, :, lanes] = (
+                padded[ch, k + 1, HALO : HALO + tile]
+                - RATE * gradient[ch, k + 1, HALO : HALO + tile]
+            )
+
+
+def body(
+    offsets,
+    place,
+    objects,
+    ze,
+    zo,
+    de,
+    do,
+    re,
+    ro,
+    probe,
+    kernel,
+    measured,
+    tables,
+    updated,
+    gze,
+    gzo,
+    gde,
+    gdo,
+    gre,
+    gro,
+    padded,
+    gradient,
+    spectrum,
+    stage,
+    sems,
+):
     width = probe.shape[1]
+    tile = re.shape[2]
     position = pl.program_id(0)
 
     @pl.when(position == 0)
     def _():
+        copies = [
+            pltpu.make_async_copy(
+                objects.at[:, :, pl.ds(k * LANES, LANES)],
+                padded.at[:, k + 1, pl.ds(HALO, tile), :],
+                sems.at[k],
+            )
+            for k in range(tile // LANES)
+        ]
+        for copy in copies:
+            copy.start()
         gradient[...] = jnp.zeros_like(gradient)
         for part in range(2):
             spectrum[part] = reorder(kernel[part], tables[4], stage)
+        assemble(place, padded, ze, zo, de, do, re, ro)
+        for copy in copies:
+            copy.wait()
 
     top = offsets[position, 0] + HALO
     left = offsets[position, 1] + LANES
     down, right = top % ROWS, left % LANES
-    row, tile = pl.multiple_of(top - down, ROWS), left // LANES
-    place = (row, tile, down, right)
+    row, column = pl.multiple_of(top - down, ROWS), left // LANES
+    spot = (row, column, down, right)
 
     pr, pim = rolled(probe[0], down, right), rolled(probe[1], down, right)
     kr, kim = spectrum[0], spectrum[1]
-    o1r = window(padded, 0, *place, width)
-    o1i = window(padded, 1, *place, width)
+    o1r = window(padded, 0, *spot, width)
+    o1i = window(padded, 1, *spot, width)
     fr, fi = forward(pr * o1r - pim * o1i, pr * o1i + pim * o1r, tables)
     sr, si = inverse(kr * fr - kim * fi, kr * fi + kim * fr, tables)
-    o2r = window(padded, 2, *place, width)
-    o2i = window(padded, 3, *place, width)
+    o2r = window(padded, 2, *spot, width)
+    o2i = window(padded, 3, *spot, width)
     zr, zi = forward(sr * o2r - si * o2i, sr * o2i + si * o2r, tables)
     amplitude = reorder(measured[0], tables[4], stage)
     factor = 1.0 - amplitude * lax.rsqrt(zr * zr + zi * zi + 1.0)
     gr, gi = inverse(zr * factor, zi * factor, tables)
-    accumulate(gradient, 2, *place, sr * gr + si * gi)
-    accumulate(gradient, 3, *place, sr * gi - si * gr)
+    accumulate(gradient, 2, *spot, sr * gr + si * gi)
+    accumulate(gradient, 3, *spot, sr * gi - si * gr)
     ur, ui = forward(o2r * gr + o2i * gi, o2r * gi - o2i * gr, tables)
     wr, wi = inverse(kr * ur + kim * ui, kr * ui - kim * ur, tables)
-    accumulate(gradient, 0, *place, pr * wr + pim * wi)
-    accumulate(gradient, 1, *place, pr * wi - pim * wr)
-
-
-def gradients(offsets, padded, probe, kernel, measured, tables):
+    accumulate(gradient, 0, *spot, pr * wr + pim * wi)
+    accumulate(gradient, 1, *spot, pr * wi - pim * wr)
+
+    @pl.when(position == pl.num_programs(0) - 1)
+    def _():
+        finish(place, padded, gradient, updated, gze, gzo, gde, gdo, gre, gro)
+
+
+def step(offsets, place, objects, halo, probe, kernel, measured, tables):
     count, width = measured.shape[0], measured.shape[1]
+    channels, tile = objects.shape[:2]
     whole = pl.BlockSpec(memory_space=pltpu.VMEM)
+    shapes = [jax.ShapeDtypeStruct(x.shape, jnp.float32) for x in (objects,) + halo]
+    extended = (channels, tile // LANES + 2, tile + 2 * HALO + ROWS, LANES)
     return pl.pallas_call(
         body,
-        out_shape=jax.ShapeDtypeStruct(padded.shape, jnp.float32),
+        out_shape=shapes,
         grid_spec=pltpu.PrefetchScalarGridSpec(
-            num_scalar_prefetch=1,
+            num_scalar_prefetch=2,
             grid=(count,),
-            in_specs=[
-                whole,
-                whole,
-                whole,
-                pl.BlockSpec((1, width, width), lambda i, _: (i, 0, 0)),
-                whole,
-            ],
-            out_specs=whole,
+            in_specs=[pl.BlockSpec(memory_space=pl.ANY)]
+            + [whole] * 8
+            + [pl.BlockSpec((1, width, width), lambda i, *_: (i, 0, 0)), whole],
+            out_specs=[whole] * 7,
             scratch_shapes=[
+                pltpu.VMEM(extended, jnp.float32),
+                pltpu.VMEM(extended, jnp.float32),
                 pltpu.VMEM((2, width, width), jnp.float32),
                 pltpu.VMEM((2, width, LANES), jnp.float32),
+                pltpu.SemaphoreType.DMA((tile // LANES,)),
             ],
         ),
         compiler_params=pltpu.CompilerParams(vmem_limit_bytes=56 * 1024 * 1024),
         name="positions",
-    )(offsets, padded, probe, kernel, measured, tables)
-
-
-def padded_2(x, sides, width):
-    for axis, dim in sides:
-        devices, length = (lax.axis_size(axis), x.shape[dim])
-        up = [(i, (i + 1) % devices) for i in range(devices - 1)]
-        down = [(j, i) for i, j in up]
-        last = lax.slice_in_dim(x, length - width, length, axis=dim)
-        initial = lax.slice_in_dim(x, 0, width, axis=dim)
-        before = lax.ppermute(last, axis, up)
-        after = lax.ppermute(initial, axis, down)
-        x = jnp.concatenate([before, x, after], axis=dim)
-    return x
+    )(offsets, place, objects, *halo, probe, kernel, measured, tables)
+
+
+def relay_body(place, re, ze, zo, out):
+    tile = re.shape[2]
+    even = place[1] == 0
+    lane = lax.broadcasted_iota(jnp.int32, (1, LANES), 1) < HALO
+    for ch in range(re.shape[0]):
+        low = jnp.where(even, zo[ch, -HALO:], ze[ch, -HALO:])
+        high = jnp.where(even, ze[ch, -HALO:], zo[ch, -HALO:])
+        out[ch, :, :LANES] = re[ch, :, :LANES] + jnp.where(lane, pltpu.roll(low, HALO, 1), 0.0)
+        out[ch, :, LANES : tile - LANES] = re[ch, :, LANES : tile - LANES]
+        out[ch, :, tile - LANES :] = re[ch, :, tile - LANES :] + jnp.where(lane, 0.0, high)
+
+
+def relay(place, re, ze, zo):
+    whole = pl.BlockSpec(memory_space=pltpu.VMEM)
+    return pl.pallas_call(
+        relay_body,
+        out_shape=jax.ShapeDtypeStruct(re.shape, jnp.float32),
+        in_specs=[pl.BlockSpec(memory_space=pltpu.SMEM)] + [whole] * 3,
+        out_specs=whole,
+        name="relay",
+    )(place, re, ze, zo)
+
+
+def settle_body(place, updated, ze, zo, de, do, re, ro, out):
+    tile = re.shape[2]
+    half = ze.shape[1]
+    corner = HALO // 2
+    even = place[1] == 0
+    outer = pl.multiple_of(place[0] * (tile - HALO), HALO)
+    inner = pl.multiple_of((1 - place[0]) * (tile - HALO), HALO)
+    lane = lax.broadcasted_iota(jnp.int32, (1, LANES), 1) < HALO
+    out[...] = updated[...]
+    out[0, pl.ds(inner, HALO)] += re[0]
+    out[0, pl.ds(outer, HALO)] += ro[0]
+    for side in range(2):
+        lanes = slice(0, LANES) if side == 0 else slice(tile - LANES, tile)
+        mask = lane if side == 0 else jnp.logical_not(lane)
+        strip = jnp.where(even, (zo, ze)[side][0], (ze, zo)[side][0])
+        piece = jnp.where(even, (do, de)[side][0], (de, do)[side][0])
+        turned, turned_piece = pltpu.roll(strip, HALO, 1), pltpu.roll(piece, HALO, 1)
+        first, second = (strip, turned) if side == 0 else (turned, strip)
+        near, far = (piece, turned_piece) if side == 0 else (turned_piece, piece)
+        out[0, :half, lanes] += jnp.where(mask, first, 0.0)
+        out[0, half:, lanes] += jnp.where(mask, second[: tile - half], 0.0)
+        out[0, pl.ds(outer, corner), lanes] += jnp.where(mask, near, 0.0)
+        out[0, pl.ds(outer + corner, corner), lanes] += jnp.where(mask, far, 0.0)
+
+
+def settle(place, updated, shares):
+    channels = updated.shape[0]
+
+    def spec(x):
+        return pl.BlockSpec((1,) + x.shape[1:], lambda i, _: (i, 0, 0))
+
+    return pl.pallas_call(
+        settle_body,
+        out_shape=jax.ShapeDtypeStruct(updated.shape, jnp.float32),
+        grid_spec=pltpu.PrefetchScalarGridSpec(
+            num_scalar_prefetch=1,
+            grid=(channels,),
+            in_specs=[spec(updated)] + [spec(x) for x in shares],
+            out_specs=spec(updated),
+        ),
+        name="settle",
+    )(place, updated, *shares)
+
+
+def swap(x, row, col):
+    rows, cols = lax.axis_size("row"), lax.axis_size("col")
+
+    def partner(i, kind):
+        return i + kind * (1 - 2 * (i % 2))
+
+    pairs = [
+        (r * cols + c, partner(r, row) * cols + partner(c, col))
+        for r in range(rows)
+        for c in range(cols)
+        if 0 <= partner(r, row) < rows and 0 <= partner(c, col) < cols
+    ]
+    return lax.ppermute(x, ("row", "col"), pairs)
+
+
+def exchange(ze, zo, de, do):
+    return swap(ze, 0, 1), swap(zo, 0, -1), swap(de, -1, 1), swap(do, -1, -1)
 
 
 def per_device(objects, probe, kernel, measured, offsets):
     tile = objects.shape[1]
-    width = probe.shape[1]
-    margin = HALO
-    extent = tile + 2 * margin
-    tables = jnp.asarray(make_tables(width))
-    padded = padded_2(objects, (("row", 1), ("col", 2)), margin)
-    padded = jnp.pad(padded, ((0, 0), (0, ROWS), (LANES - margin, LANES - margin)))
-    tiles = padded.shape[2] // LANES
-    padded = padded.reshape(4, extent + ROWS, tiles, LANES).transpose(0, 2, 1, 3)
-    gradient = gradients(offsets[0, 0], padded, probe, kernel, measured[0, 0], tables)
-    gradient = gradient.transpose(0, 2, 1, 3).reshape(4, extent + ROWS, tiles * LANES)
-    gradient = gradient[:, :extent, LANES - margin : LANES - margin + extent]
-    cycle = padded_2(gradient, (("row", 1), ("col", 2)), margin)
-    inner = gradient[:, margin : margin + tile, margin : margin + tile]
-    gap_rows = jnp.zeros((4, tile - 2 * margin, tile), jnp.float32)
-    gap_cols = jnp.zeros((4, tile, tile - 2 * margin), jnp.float32)
-    gap_corner = jnp.zeros((4, margin, tile - 2 * margin), jnp.float32)
-    top = cycle[:, :margin, 2 * margin : 2 * margin + tile]
-    bottom = cycle[:, extent + margin :, 2 * margin : 2 * margin + tile]
-    left = cycle[:, 2 * margin : 2 * margin + tile, :margin]
-    right = cycle[:, 2 * margin : 2 * margin + tile, extent + margin :]
-    corner_top = jnp.concatenate(
-        [cycle[:, :margin, :margin], gap_corner, cycle[:, :margin, extent + margin :]], 2
+    tables = jnp.asarray(make_tables(probe.shape[1]))
+    place = jnp.stack([lax.axis_index("row") % 2, lax.axis_index("col") % 2]).astype(jnp.int32)
+    rows = lax.dynamic_slice_in_dim(objects, (1 - place[0]) * (tile - HALO), HALO, axis=1)
+    re = swap(rows, 1, 0)
+    *sides, ro = pack(place, objects, re)
+    halo = (*exchange(*sides), re, swap(ro, -1, 0))
+    updated, *sides, gre, gro = step(
+        offsets[0, 0], place, objects, halo, probe, kernel, measured[0, 0], tables
     )
-    corner_bottom = jnp.concatenate(
-        [
-            cycle[:, extent + margin :, :margin],
-            gap_corner,
-            cycle[:, extent + margin :, extent + margin :],
-        ],
-        2,
-    )
-    vertical = jnp.concatenate([top + corner_top, gap_rows, bottom + corner_bottom], 1)
-    horizontal = jnp.concatenate([left, gap_cols, right], 2)
-    total = inner + vertical + horizontal
-    return objects - RATE * total
+    ze, zo, de, do = exchange(*sides)
+    ro = swap(gro, -1, 0)
+    re = swap(relay(place, gre, ze, zo), 1, 0)
+    return settle(place, updated, (ze, zo, de, do, re, ro))
 
 
 def solution(mesh):

time: 162 us -> 105 us (0.65); the launches traced: 159 us -> 104 us
  local copies, waits for them, and re-layouts: 42.7 us -> 4.77 us
  other arithmetic: 17.4 us -> 0.07 us
  waiting for transfers between devices: 41.9 us -> 25.7 us
  Pallas kernels: 36.3 us -> 48.7 us
  starting transfers between devices: 20.8 us -> 25 us
    ppermute x8 -> x12, waiting for transfers between devices: 41.9 us -> 25.7 us  [swap(): return lax.ppermute(x, ('row', 'col'), pairs)]
    pallas_call x1 -> x4, Pallas kernels: 36.3 us -> 48.7 us  [the longest x1 37.4 us: step(): pl.pallas_call(body, out_shape=shapes, grid_spec=pltpu.PrefetchScalarGrid...]
    slice x9 -> x0, local copies, waits for them, and re-layouts: 10.6 us -> none  [the longest x1 6.04 us: per_device(): gradient = gradient[:, :extent, LANES - margin:LANES - margin + extent]]
    transpose x1 -> x0, local copies, waits for them, and re-layouts: 9.19 us -> none  [per_device(): gradient.transpose(0, 2, 1, 3).reshape(4, extent + ROWS, tiles * LANES)]
    reshape x1 -> x0, local copies, waits for them, and re-layouts: 9.15 us -> none  [per_device(): padded.reshape(4, extent + ROWS, tiles, LANES).transpose(0, 2, 1, 3)]
    concatenate x1 -> x0, other arithmetic: 7.23 us -> none  [padded_2(): x = jnp.concatenate([before, x, after], axis=dim)]
    sub x1 -> x0, other arithmetic: 5.29 us -> none  [per_device(): return objects - RATE * total]
    sub x1 -> x0, local copies, waits for them, and re-layouts: 5.22 us -> none  [per_device(): return objects - RATE * total]
  transfers between devices with their start and end apart: 8 -> 12, of which waited for: 8 -> 8; matrix products, arithmetic and copies ran while one was open for 8% -> 1% of each run, Pallas kernels for 0% -> 2%
where the time goes in v2:
time: 105 us; the launch traced here: 104 us
  Pallas kernels  48.7 us (46%)
  waiting for transfers between devices  25.7 us (24%)
  starting transfers between devices  25 us (24%)
  local copies, waits for them, and re-layouts  4.77 us (5%)
    pallas_call x1, Pallas kernels, step(): pl.pallas_call(body, out_shape=shapes, grid_spec=pltpu.PrefetchScalarGrid...  37.4 us
    ppermute x12, waiting for transfers between devices, swap(): return lax.ppermute(x, ('row', 'col'), pairs)  25.7 us
    ppermute x12, starting transfers between devices, swap(): return lax.ppermute(x, ('row', 'col'), pairs)  25 us
    pallas_call x1, Pallas kernels, settle(): pl.pallas_call(settle_body, out_shape=jax.ShapeDtypeStruct(updated.shape,...  6.28 us
    unnamed x24, local copies, waits for them, and re-layouts  3.01 us
    pallas_call x1, Pallas kernels, pack(): pl.pallas_call(pack_body, out_shape=(strip, strip, corner, corner, jax.Sh...  2.68 us
    pallas_call x1, Pallas kernels, relay(): pl.pallas_call(relay_body, out_shape=jax.ShapeDtypeStruct(re.shape, jnp.f...  2.31 us
  transfers between devices with their start and end apart: 12, of which 8 were waited for; matrix products, arithmetic and copies ran while one was open for 1% of the time, Pallas kernels for 2%

profile of v2, /device:TPU:11, one launch (start us, length us, event | category | flops | bytes accessed | tf_op | source)
XLA Modules:
  0.0 104.3 jit_solution(1201570359367193580)
XLA Ops:
  0.0 1.1 %constant_dynamic-slice_fusion = f32[4,64,512]{2,1,0:T(8,128)S(1)} fusion(f32[4,512,512]{2,1,0:T(8,128)} %objects.1, s32[]{:T(128)S(6)} %select_n.16), kind=kLoop, calls=%fused_computation.1 | loop fusion | bytes 1048580 | tf_op jit(solution)/shard_map/dynamic_slice | solution.py:452
  1.1 0.7 collective-permute-start
  1.9 1.5 %collective-permute-done.inner.re = f32[4,64,512]{2,1,0:T(8,128)S(1)} collective-permute-done((f32[4,64,512]{2,1,0:T(8,128)S(1)}, f32[4,64,512]{2,1,0:T(8,128)S(1)}, u32[]{:S(2)}, u32[]{:S(2)}) %collective-permute-start) | collective-permute-done | bytes 524320 | tf_op jit(solution)/shard_map/ppermute | solution.py:441
  3.4 2.7 %pack.1 = (f32[4,288,128]{2,1,0:T(8,128)S(1)}, f32[4,288,128]{2,1,0:T(8,128)S(1)}, f32[4,32,128]{2,1,0:T(8,128)S(1)}, f32[4,32,128]{2,1,0:T(8,128)S(1)}, f32[4,64,512]{2,1,0:T(8,128)S(1)}) custom-call(s32[2]{0:T(128)S(1)} %pad_add_fusion.place, f32[4,512,512]{2,1,0:T(8,128)} %objects.1, f32[4,512,512]{2,1,0:T(8,128)} %objects.1, f32[4,512,512]{2,1,0:T(8,128)} %objects.1, ...), custom_call_target="tpu_custom_call" | custom-call | tf_op jit(solution)/shard_map/pack/pallas_call | solution.py:172
  6.3 4.3 %collective-permute-start.2 = (f32[4,288,128]{2,1,0:T(8,128)S(1)}, f32[4,288,128]{2,1,0:T(8,128)S(1)}, u32[]{:S(2)}, u32[]{:S(2)}) collective-permute-start(f32[4,288,128]{2,1,0:T(8,128)S(1)} %get-tuple-element.18), channel_id=1, source_target_pairs={{1,2},{2,1},{5,6},{6,5},{9,10},{10,9},{13,14},{14,13},{17,18},{18,... | collective-permute-start | bytes 1769480 | tf_op jit(solution)/shard_map/ppermute | solution.py:441
  10.6 3.9 %collective-permute-start.5 = (f32[4,64,512]{2,1,0:T(8,128)S(1)}, f32[4,64,512]{2,1,0:T(8,128)S(1)}, u32[]{:S(2)}, u32[]{:S(2)}) collective-permute-start(f32[4,64,512]{2,1,0:T(8,128)S(1)} %get-tuple-element.21), channel_id=1, source_target_pairs={{4,8},{5,9},{6,10},{7,11},{8,4},{9,5},{10,6},{11,7},{12,16},{13,17... | collective-permute-start | bytes 1572872 | tf_op jit(solution)/shard_map/ppermute | solution.py:441
  14.6 1.9 %collective-permute-start.3 = (f32[4,32,128]{2,1,0:T(8,128)S(1)}, f32[4,32,128]{2,1,0:T(8,128)}, u32[]{:S(2)}, u32[]{:S(2)}) collective-permute-start(f32[4,32,128]{2,1,0:T(8,128)S(1)} %get-tuple-element.19), channel_id=1, source_target_pairs={{4,9},{5,8},{6,11},{7,10},{8,5},{9,4},{10,7},{11,6},{12,17},{13,16... | collective-permute-start | bytes 196616 | tf_op jit(solution)/shard_map/ppermute | solution.py:441
  16.5 2.7 %collective-permute-start.4 = (f32[4,32,128]{2,1,0:T(8,128)S(1)}, f32[4,32,128]{2,1,0:T(8,128)}, u32[]{:S(2)}, u32[]{:S(2)}) collective-permute-start(f32[4,32,128]{2,1,0:T(8,128)S(1)} %get-tuple-element.20), channel_id=1, source_target_pairs={{5,10},{6,9},{9,6},{10,5},{13,18},{14,17},{17,14},{18,13},{21,26},... | collective-permute-start | bytes 196616 | tf_op jit(solution)/shard_map/ppermute | solution.py:441
  19.9 3.9 %collective-permute-done.3.de = f32[4,32,128]{2,1,0:T(8,128)} collective-permute-done((f32[4,32,128]{2,1,0:T(8,128)S(1)}, f32[4,32,128]{2,1,0:T(8,128)}, u32[]{:S(2)}, u32[]{:S(2)}) %collective-permute-start.3) | collective-permute-done | bytes 65568 | tf_op jit(solution)/shard_map/ppermute | solution.py:441
  23.7 3.0 %collective-permute-done.4.do = f32[4,32,128]{2,1,0:T(8,128)} collective-permute-done((f32[4,32,128]{2,1,0:T(8,128)S(1)}, f32[4,32,128]{2,1,0:T(8,128)}, u32[]{:S(2)}, u32[]{:S(2)}) %collective-permute-start.4) | collective-permute-done | bytes 65568 | tf_op jit(solution)/shard_map/ppermute | solution.py:441
  26.7 3.4 %collective-permute-done.5.ro = f32[4,64,512]{2,1,0:T(8,128)S(1)} collective-permute-done((f32[4,64,512]{2,1,0:T(8,128)S(1)}, f32[4,64,512]{2,1,0:T(8,128)S(1)}, u32[]{:S(2)}, u32[]{:S(2)}) %collective-permute-start.5) | collective-permute-done | bytes 524320 | tf_op jit(solution)/shard_map/ppermute | solution.py:441
  30.2 0.8 copy-done.6
  31.4 37.4 %positions.1 = (f32[4,512,512]{2,1,0:T(8,128)}, f32[4,288,128]{2,1,0:T(8,128)}, f32[4,288,128]{2,1,0:T(8,128)}, f32[4,32,128]{2,1,0:T(8,128)}, f32[4,32,128]{2,1...) custom-call(s32[9,2]{1,0:T(8,128)} %copy.7.offsets, s32[2]{0:T(128)} %copy-done.1, f32[4,512,512]{2,1,0:T(8,128)} %objects.1, ...), custom_call_target="tpu_custom_call" | custom-call | tf_op jit(solution)/shard_map/positions/pallas_call | solution.py:339
  68.8 2.1 %collective-permute-start.7 = (f32[4,288,128]{2,1,0:T(8,128)}, f32[4,288,128]{2,1,0:T(8,128)S(1)}, u32[]{:S(2)}, u32[]{:S(2)}) collective-permute-start(f32[4,288,128]{2,1,0:T(8,128)} %get-tuple-element.24), channel_id=1, source_target_pairs={{1,2},{2,1},{5,6},{6,5},{9,10},{10,9},{13,14},{14,13},{17,18},{18,... | collective-permute-start | bytes 1769480 | tf_op jit(solution)/shard_map/ppermute | solution.py:441
  70.9 3.1 %collective-permute-start.11 = (f32[4,64,512]{2,1,0:T(8,128)}, f32[4,64,512]{2,1,0:T(8,128)S(1)}, u32[]{:S(2)}, u32[]{:S(2)}) collective-permute-start(f32[4,64,512]{2,1,0:T(8,128)} %get-tuple-element.28), channel_id=1, source_target_pairs={{4,8},{5,9},{6,10},{7,11},{8,4},{9,5},{10,6},{11,7},{12,16},{13,17... | collective-permute-start | bytes 1572872 | tf_op jit(solution)/shard_map/ppermute | solution.py:441
  74.0 8.3 %collective-permute-done.6.ze = f32[4,288,128]{2,1,0:T(8,128)S(1)} collective-permute-done((f32[4,288,128]{2,1,0:T(8,128)}, f32[4,288,128]{2,1,0:T(8,128)S(1)}, u32[]{:S(2)}, u32[]{:S(2)}) %collective-permute-start.6) | collective-permute-done | bytes 589856 | tf_op jit(solution)/shard_map/ppermute | solution.py:441
  82.3 1.7 %collective-permute-done.7.zo = f32[4,288,128]{2,1,0:T(8,128)S(1)} collective-permute-done((f32[4,288,128]{2,1,0:T(8,128)}, f32[4,288,128]{2,1,0:T(8,128)S(1)}, u32[]{:S(2)}, u32[]{:S(2)}) %collective-permute-start.7) | collective-permute-done | bytes 589856 | tf_op jit(solution)/shard_map/ppermute | solution.py:441
  84.0 0.8 copy-done.3
  84.9 2.3 %relay.1 = f32[4,64,512]{2,1,0:T(8,128)} custom-call(s32[2]{0:T(128)} %copy-done.1, f32[4,64,512]{2,1,0:T(8,128)} %get-tuple-element.27.re, f32[4,288,128]{2,1,0:T(8,128)} %copy-done.2, f32[4,288,128]{2,1,0:T(8,128)} %copy-done.3), custom_call_target="tpu_custom_call" | custom-call | tf_op jit(solution)/shard_map/relay/pallas_call | solution.py:376
  87.2 2.3 %collective-permute-start.8 = (f32[4,32,128]{2,1,0:T(8,128)}, f32[4,32,128]{2,1,0:T(8,128)S(1)}, u32[]{:S(2)}, u32[]{:S(2)}) collective-permute-start(f32[4,32,128]{2,1,0:T(8,128)} %get-tuple-element.25), channel_id=1, source_target_pairs={{4,9},{5,8},{6,11},{7,10},{8,5},{9,4},{10,7},{11,6},{12,17},{13,16... | collective-permute-start | bytes 196616 | tf_op jit(solution)/shard_map/ppermute | solution.py:441
  89.5 3.7 %collective-permute-start.9 = (f32[4,32,128]{2,1,0:T(8,128)}, f32[4,32,128]{2,1,0:T(8,128)S(1)}, u32[]{:S(2)}, u32[]{:S(2)}) collective-permute-start(f32[4,32,128]{2,1,0:T(8,128)} %get-tuple-element.26), channel_id=1, source_target_pairs={{5,10},{6,9},{9,6},{10,5},{13,18},{14,17},{17,14},{18,13},{21,26},... | collective-permute-start | bytes 196616 | tf_op jit(solution)/shard_map/ppermute | solution.py:441
  93.1 1.6 %collective-permute-done.8.de = f32[4,32,128]{2,1,0:T(8,128)S(1)} collective-permute-done((f32[4,32,128]{2,1,0:T(8,128)}, f32[4,32,128]{2,1,0:T(8,128)S(1)}, u32[]{:S(2)}, u32[]{:S(2)}) %collective-permute-start.8) | collective-permute-done | bytes 65568 | tf_op jit(solution)/shard_map/ppermute | solution.py:441
  94.8 2.3 %collective-permute-done.9.do = f32[4,32,128]{2,1,0:T(8,128)S(1)} collective-permute-done((f32[4,32,128]{2,1,0:T(8,128)}, f32[4,32,128]{2,1,0:T(8,128)S(1)}, u32[]{:S(2)}, u32[]{:S(2)}) %collective-permute-start.9) | collective-permute-done | bytes 65568 | tf_op jit(solution)/shard_map/ppermute | solution.py:441
  98.1 6.3 %settle.1 = f32[4,512,512]{2,1,0:T(8,128)} custom-call(s32[2]{0:T(128)} %copy-done.1, f32[4,512,512]{2,1,0:T(8,128)} %get-tuple-element.22.updated, f32[4,288,128]{2,1,0:T(8,128)} %copy-done.2, f32[4,288,128]{2,1,0:T(8,128)} %copy-done.3, f32[4,32,128]{2,1,0:T(8,128)} %copy-done.9, f32[4,32,128]{2,1,0:T(8,128)} %copy-done.10, f32[4,64,512]{2,1,0:T(8,128)} %copy-done.8, ...), custom_call_target="tpu_custom_call" | custom-call | tf_op jit(solution)/shard_map/settle/pallas_call | solution.py:416
  (31 shorter events, 2.4 us)
Async XLA Ops:
  1.1 2.3 %collective-permute-start = (f32[4,64,512]{2,1,0:T(8,128)S(1)}, f32[4,64,512]{2,1,0:T(8,128)S(1)}, u32[]{:S(2)}, u32[]{:S(2)}) collective-permute-start(f32[4,64,512]{2,1,0:T(8,128)S(1)} %constant_dynamic-slice_fusion), channel_id=1, source_target_pairs={{0,4},{1,5},{2,6},{3,7},{4,0},{5,1},{6,2},{7,3},{8,12},{9,13},{10,... | collective-permute-start | bytes 1572872 | tf_op jit(solution)/shard_map/ppermute | solution.py:441
  1.9 4.2 %copy-start.1 = (s32[2]{0:T(128)}, s32[2]{0:T(128)S(1)}, u32[]{:S(2)}) copy-start(s32[2]{0:T(128)S(1)} %pad_add_fusion.place) | copy-start | bytes 28
  1.9 17.3 %copy-start.11 = (s32[1,1,9,2]{2,3,1,0:T(2,128)S(1)}, s32[1,1,9,2]{2,3,1,0:T(2,128)}, u32[]{:S(2)}) copy-start(s32[1,1,9,2]{2,3,1,0:T(2,128)} %param.10) | copy-start | bytes 220
  3.4 2.7 %copy-start = (f32[4,64,512]{2,1,0:T(8,128)}, f32[4,64,512]{2,1,0:T(8,128)S(1)}, u32[]{:S(2)}) copy-start(f32[4,64,512]{2,1,0:T(8,128)S(1)} %collective-permute-done.inner.re) | copy-start | bytes 1572868
  6.1 24.1 %collective-permute-start.1 = (f32[4,288,128]{2,1,0:T(8,128)S(1)}, f32[4,288,128]{2,1,0:T(8,128)S(1)}, u32[]{:S(2)}, u32[]{:S(2)}) collective-permute-start(f32[4,288,128]{2,1,0:T(8,128)S(1)} %get-tuple-element.17), channel_id=1, source_target_pairs={{0,1},{1,0},{2,3},{3,2},{4,5},{5,4},{6,7},{7,6},{8,9},{9,8},{10,11... | collective-permute-start | bytes 1769480 | tf_op jit(solution)/shard_map/ppermute | solution.py:441
  6.3 23.9 %collective-permute-start.2 = (f32[4,288,128]{2,1,0:T(8,128)S(1)}, f32[4,288,128]{2,1,0:T(8,128)S(1)}, u32[]{:S(2)}, u32[]{:S(2)}) collective-permute-start(f32[4,288,128]{2,1,0:T(8,128)S(1)} %get-tuple-element.18), channel_id=1, source_target_pairs={{1,2},{2,1},{5,6},{6,5},{9,10},{10,9},{13,14},{14,13},{17,18},{18,... | collective-permute-start | bytes 1769480 | tf_op jit(solution)/shard_map/ppermute | solution.py:441
  10.6 19.5 %collective-permute-start.5 = (f32[4,64,512]{2,1,0:T(8,128)S(1)}, f32[4,64,512]{2,1,0:T(8,128)S(1)}, u32[]{:S(2)}, u32[]{:S(2)}) collective-permute-start(f32[4,64,512]{2,1,0:T(8,128)S(1)} %get-tuple-element.21), channel_id=1, source_target_pairs={{4,8},{5,9},{6,10},{7,11},{8,4},{9,5},{10,6},{11,7},{12,16},{13,17... | collective-permute-start | bytes 1572872 | tf_op jit(solution)/shard_map/ppermute | solution.py:441
  14.6 9.1 %collective-permute-start.3 = (f32[4,32,128]{2,1,0:T(8,128)S(1)}, f32[4,32,128]{2,1,0:T(8,128)}, u32[]{:S(2)}, u32[]{:S(2)}) collective-permute-start(f32[4,32,128]{2,1,0:T(8,128)S(1)} %get-tuple-element.19), channel_id=1, source_target_pairs={{4,9},{5,8},{6,11},{7,10},{8,5},{9,4},{10,7},{11,6},{12,17},{13,16... | collective-permute-start | bytes 196616 | tf_op jit(solution)/shard_map/ppermute | solution.py:441
  16.5 10.2 %collective-permute-start.4 = (f32[4,32,128]{2,1,0:T(8,128)S(1)}, f32[4,32,128]{2,1,0:T(8,128)}, u32[]{:S(2)}, u32[]{:S(2)}) collective-permute-start(f32[4,32,128]{2,1,0:T(8,128)S(1)} %get-tuple-element.20), channel_id=1, source_target_pairs={{5,10},{6,9},{9,6},{10,5},{13,18},{14,17},{17,14},{18,13},{21,26},... | collective-permute-start | bytes 196616 | tf_op jit(solution)/shard_map/ppermute | solution.py:441
  30.2 0.8 copy-start.6
  30.2 1.0 copy-start.4
  30.2 1.2 %copy-start.5 = (f32[4,288,128]{2,1,0:T(8,128)}, f32[4,288,128]{2,1,0:T(8,128)S(1)}, u32[]{:S(2)}) copy-start(f32[4,288,128]{2,1,0:T(8,128)S(1)} %collective-permute-done.2.zo) | copy-start | bytes 1769476
  68.7 13.6 %collective-permute-start.6 = (f32[4,288,128]{2,1,0:T(8,128)}, f32[4,288,128]{2,1,0:T(8,128)S(1)}, u32[]{:S(2)}, u32[]{:S(2)}) collective-permute-start(f32[4,288,128]{2,1,0:T(8,128)} %get-tuple-element.23), channel_id=1, source_target_pairs={{0,1},{1,0},{2,3},{3,2},{4,5},{5,4},{6,7},{7,6},{8,9},{9,8},{10,11... | collective-permute-start | bytes 1769480 | tf_op jit(solution)/shard_map/ppermute | solution.py:441
  68.8 15.2 %collective-permute-start.7 = (f32[4,288,128]{2,1,0:T(8,128)}, f32[4,288,128]{2,1,0:T(8,128)S(1)}, u32[]{:S(2)}, u32[]{:S(2)}) collective-permute-start(f32[4,288,128]{2,1,0:T(8,128)} %get-tuple-element.24), channel_id=1, source_target_pairs={{1,2},{2,1},{5,6},{6,5},{9,10},{10,9},{13,14},{14,13},{17,18},{18,... | collective-permute-start | bytes 1769480 | tf_op jit(solution)/shard_map/ppermute | solution.py:441
  70.9 26.2 %collective-permute-start.11 = (f32[4,64,512]{2,1,0:T(8,128)}, f32[4,64,512]{2,1,0:T(8,128)S(1)}, u32[]{:S(2)}, u32[]{:S(2)}) collective-permute-start(f32[4,64,512]{2,1,0:T(8,128)} %get-tuple-element.28), channel_id=1, source_target_pairs={{4,8},{5,9},{6,10},{7,11},{8,4},{9,5},{10,6},{11,7},{12,16},{13,17... | collective-permute-start | bytes 1572872 | tf_op jit(solution)/shard_map/ppermute | solution.py:441
  82.3 1.7 %copy-start.2 = (f32[4,288,128]{2,1,0:T(8,128)}, f32[4,288,128]{2,1,0:T(8,128)S(1)}, u32[]{:S(2)}) copy-start(f32[4,288,128]{2,1,0:T(8,128)S(1)} %collective-permute-done.6.ze) | copy-start | bytes 1769476
  84.0 0.8 copy-start.3
  87.2 9.9 %collective-permute-start.10 = (f32[4,64,512]{2,1,0:T(8,128)}, f32[4,64,512]{2,1,0:T(8,128)S(1)}, u32[]{:S(2)}, u32[]{:S(2)}) collective-permute-start(f32[4,64,512]{2,1,0:T(8,128)} %relay.1), channel_id=1, source_target_pairs={{0,4},{1,5},{2,6},{3,7},{4,0},{5,1},{6,2},{7,3},{8,12},{9,13},{10,... | collective-permute-start | bytes 1572872 | tf_op jit(solution)/shard_map/ppermute | solution.py:441
  87.2 7.6 %collective-permute-start.8 = (f32[4,32,128]{2,1,0:T(8,128)}, f32[4,32,128]{2,1,0:T(8,128)S(1)}, u32[]{:S(2)}, u32[]{:S(2)}) collective-permute-start(f32[4,32,128]{2,1,0:T(8,128)} %get-tuple-element.25), channel_id=1, source_target_pairs={{4,9},{5,8},{6,11},{7,10},{8,5},{9,4},{10,7},{11,6},{12,17},{13,16... | collective-permute-start | bytes 196616 | tf_op jit(solution)/shard_map/ppermute | solution.py:441
  89.5 7.6 %collective-permute-start.9 = (f32[4,32,128]{2,1,0:T(8,128)}, f32[4,32,128]{2,1,0:T(8,128)S(1)}, u32[]{:S(2)}, u32[]{:S(2)}) collective-permute-start(f32[4,32,128]{2,1,0:T(8,128)} %get-tuple-element.26), channel_id=1, source_target_pairs={{5,10},{6,9},{9,6},{10,5},{13,18},{14,17},{17,14},{18,13},{21,26},... | collective-permute-start | bytes 196616 | tf_op jit(solution)/shard_map/ppermute | solution.py:441
  94.8 2.3 %copy-start.9 = (f32[4,32,128]{2,1,0:T(8,128)}, f32[4,32,128]{2,1,0:T(8,128)S(1)}, u32[]{:S(2)}) copy-start(f32[4,32,128]{2,1,0:T(8,128)S(1)} %collective-permute-done.8.de) | copy-start | bytes 196612
  97.0 0.6 copy-start.10
  97.1 0.8 copy-start.7
  97.1 1.0 copy-start.8

commit v3 on v2

v3 whole, which is shorter than its diff:
```python
import itertools
import jax
import jax.numpy as jnp
import numpy as np
from jax import lax
from jax.experimental import pallas as pl
from jax.experimental.pallas import tpu as pltpu
from jax.sharding import PartitionSpec as P

HALO = 64
RATE = 0.5
LANES = 128
ROWS = 8
GROUPS = (3, 2, 1)
VMEM = 24 * 1024 * 1024


def make_tables(width):
    half = width // 2
    index = np.arange(width)
    angle = 2.0 * np.pi / width * (index[:, None] * index[None, :] % width)
    cosine = np.cos(angle) / np.sqrt(width)
    sine = np.sin(angle) / np.sqrt(width)

    def block(parity):
        c, s = cosine[parity::2, :half], sine[parity::2, :half]
        return np.block([[c, s], [-s, c]])

    even, odd = block(0), block(1)
    order = np.zeros((width, width))
    order[index[0::2], np.arange(half)] = 1.0
    order[index[1::2], half + np.arange(half)] = 1.0
    return np.stack([even, odd, even.T, odd.T, order, RATE * order]).astype(jnp.bfloat16)


def dot(a, b):
    return jnp.dot(a, b, preferred_element_type=jnp.float32)


def forward(xr, xi, tables):
    half = xr.shape[0] // 2
    le, lo, re, ro = tables[0], tables[1], tables[2], tables[3]
    u = jnp.concatenate([xr[:half] + xr[half:], xi[:half] + xi[half:]], 0)
    v = jnp.concatenate([xr[:half] - xr[half:], xi[:half] - xi[half:]], 0)
    e = dot(le, u.astype(jnp.bfloat16))
    o = dot(lo, v.astype(jnp.bfloat16))
    yield

    def fold(parts):
        fr, fi = parts[:half], parts[half:]
        p = jnp.concatenate([fr[:, :half] + fr[:, half:], fi[:, :half] + fi[:, half:]], 1)
        m = jnp.concatenate([fr[:, :half] - fr[:, half:], fi[:, :half] - fi[:, half:]], 1)
        return p.astype(jnp.bfloat16), m.astype(jnp.bfloat16)

    pe, me = fold(e)
    po, mo = fold(o)
    y = dot(jnp.concatenate([pe, po], 0), re)
    z = dot(jnp.concatenate([me, mo], 0), ro)
    yield
    return (
        jnp.concatenate([y[:, :half], z[:, :half]], 1),
        jnp.concatenate([y[:, half:], z[:, half:]], 1),
    )


def inverse(xr, xi, tables):
    half = xr.shape[0] // 2
    le, lo, re, ro = tables[2], tables[3], tables[0], tables[1]
    e = dot(le, jnp.concatenate([xr[:half], xi[:half]], 0).astype(jnp.bfloat16))
    o = dot(lo, jnp.concatenate([xr[half:], xi[half:]], 0).astype(jnp.bfloat16))
    yield
    p = (e + o).astype(jnp.bfloat16)
    m = (e - o).astype(jnp.bfloat16)

    def pick(cols):
        return jnp.concatenate(
            [
                jnp.concatenate([p[:half, cols], p[half:, cols]], 1),
                jnp.concatenate([m[:half, cols], m[half:, cols]], 1),
            ],
            0,
        )

    y = dot(pick(slice(0, half)), re)
    z = dot(pick(slice(half, 2 * half)), ro)
    yield
    s, d = y + z, y - z
    return (
        jnp.concatenate([s[:, :half], d[:, :half]], 1),
        jnp.concatenate([s[:, half:], d[:, half:]], 1),
    )


def reorder(x, order, stage):
    half = x.shape[0] // 2
    high = x.astype(jnp.bfloat16)
    low = (x - high.astype(jnp.float32)).astype(jnp.bfloat16)
    columns = dot(high, order) + dot(low, order)
    parts = []
    for k in range(2):
        stage[k] = columns[:, k * LANES : (k + 1) * LANES]
        parts.append(
            jnp.concatenate([stage[k, pl.ds(0, half, 2), :], stage[k, pl.ds(1, half, 2), :]], 0)
        )
    return jnp.concatenate(parts, 1)


def rolled(x, down, right):
    return pltpu.roll(pltpu.roll(x, down, 0), right, 1)


def masks(down, right):
    sub = lax.broadcasted_iota(jnp.int32, (ROWS, LANES), 0) >= down
    lane = lax.broadcasted_iota(jnp.int32, (1, LANES), 1) >= right
    return sub, lane


def window(ref, channel, row, tile, down, right, width):
    sub, lane = masks(down, right)
    parts = []
    for k in range(3):
        at = ref[channel, tile + k, pl.ds(row, width), :]
        after = ref[channel, tile + k, pl.ds(row + width, ROWS), :]
        parts.append(jnp.concatenate([jnp.where(sub, at[:ROWS], after), at[ROWS:]], 0))
    return jnp.concatenate([jnp.where(lane, parts[0], parts[2]), parts[1]], 1)


def accumulate(ref, channel, row, tile, down, right, value):
    width = value.shape[0]
    sub, lane = masks(down, right)
    first = value[:, :LANES]
    for k, part in enumerate(
        (jnp.where(lane, first, 0.0), value[:, LANES:], jnp.where(lane, 0.0, first))
    ):
        head = part[:ROWS]
        ref[channel, tile + k, pl.ds(row, ROWS), :] += jnp.where(sub, head, 0.0)
        ref[channel, tile + k, pl.ds(row + ROWS, width - ROWS), :] += part[ROWS:]
        ref[channel, tile + k, pl.ds(row + width, ROWS), :] += jnp.where(sub, 0.0, head)


def fold_pair(a, b, low_first):
    lane = lax.broadcasted_iota(jnp.int32, (1, LANES), 1) < HALO
    if low_first:
        return jnp.where(lane, a, pltpu.roll(b, HALO, 1))
    return jnp.where(lane, pltpu.roll(a, HALO, 1), b)


def pack_body(place, left, right, outer, inner, ze, zo, de, do):
    tile = left.shape[1]
    half = ze.shape[1]
    corner = HALO // 2
    even = place[1] == 0
    for ch in range(left.shape[0]):
        strips, corners = [], []
        for ref, lanes, low in (
            (left, slice(0, LANES), True),
            (right, slice(tile - LANES, tile), False),
        ):
            below = jnp.concatenate([ref[ch, half:], inner[ch, :, lanes]], 0)
            strips.append(fold_pair(ref[ch, :half], below, low))
            corners.append(
                fold_pair(outer[ch, :corner, lanes], outer[ch, corner:, lanes], low)
            )
        ze[ch] = jnp.where(even, strips[1], strips[0])
        zo[ch] = jnp.where(even, strips[0], strips[1])
        de[ch] = jnp.where(even, corners[1], corners[0])
        do[ch] = jnp.where(even, corners[0], corners[1])


def pack(place, objects, inner):
    channels, tile = objects.shape[:2]
    half = (tile + HALO) // 2
    last = tile // LANES - 1
    strip = jax.ShapeDtypeStruct((channels, half, LANES), jnp.float32)
    corner = jax.ShapeDtypeStruct((channels, HALO // 2, LANES), jnp.float32)
    whole = pl.BlockSpec(memory_space=pltpu.VMEM)
    return pl.pallas_call(
        pack_body,
        out_shape=(strip, strip, corner, corner),
        grid_spec=pltpu.PrefetchScalarGridSpec(
            num_scalar_prefetch=1,
            grid=(1,),
            in_specs=[
                pl.BlockSpec((channels, tile, LANES), lambda i, _: (0, 0, 0)),
                pl.BlockSpec((channels, tile, LANES), lambda i, _: (0, 0, last)),
                pl.BlockSpec(
                    (channels, HALO, tile),
                    lambda i, place: (0, place[0] * (tile // HALO - 1), 0),
                ),
                whole,
            ],
            out_specs=[whole] * 4,
        ),
        compiler_params=pltpu.CompilerParams(vmem_limit_bytes=VMEM),
        name="pack",
    )(place, objects, objects, objects, inner)


def chain(top, left, padded, probe, spectrum, measured, tables, gradient, stage):
    width = probe.shape[1]
    down, right = top % ROWS, left % LANES
    row, column = pl.multiple_of(top - down, ROWS), left // LANES
    spot = (row, column, down, right)
    pr, pim = rolled(probe[0], down, right), rolled(probe[1], down, right)
    kr, kim = spectrum[0], spectrum[1]
    o1r = window(padded, 0, *spot, width)
    o1i = window(padded, 1, *spot, width)
    fr, fi = yield from forward(pr * o1r - pim * o1i, pr * o1i + pim * o1r, tables)
    sr, si = yield from inverse(kr * fr - kim * fi, kr * fi + kim * fr, tables)
    o2r = window(padded, 2, *spot, width)
    o2i = window(padded, 3, *spot, width)
    zr, zi = yield from forward(sr * o2r - si * o2i, sr * o2i + si * o2r, tables)
    amplitude = reorder(measured[...], tables[5], stage)
    factor = amplitude * lax.rsqrt(zr * zr + zi * zi + 1.0) - RATE
    gr, gi = yield from inverse(zr * factor, zi * factor, tables)
    accumulate(gradient, 2, *spot, sr * gr + si * gi)
    accumulate(gradient, 3, *spot, sr * gi - si * gr)
    ur, ui = yield from forward(o2r * gr + o2i * gi, o2r * gi - o2i * gr, tables)
    wr, wi = yield from inverse(kr * ur + kim * ui, kr * ui - kim * ur, tables)
    accumulate(gradient, 0, *spot, pr * wr + pim * wi)
    accumulate(gradient, 1, *spot, pr * wi - pim * wr)


def rows_of(place, tile):
    outer = pl.multiple_of(place[0] * (tile + HALO), HALO)
    inner = pl.multiple_of((1 - place[0]) * (tile + HALO), HALO)
    return outer, inner


def assemble(place, padded, ze, zo, de, do, tile):
    half = ze.shape[1]
    corner = HALO // 2
    even = place[1] == 0
    outer, inner = rows_of(place, tile)
    for ch in range(ze.shape[0]):
        for side, at in ((0, 0), (1, padded.shape[1] - 1)):
            strip = jnp.where(even, (zo, ze)[side][ch], (ze, zo)[side][ch])
            piece = jnp.where(even, (do, de)[side][ch], (de, do)[side][ch])
            turned, turned_piece = pltpu.roll(strip, HALO, 1), pltpu.roll(piece, HALO, 1)
            first, second = (turned, strip) if side == 0 else (strip, turned)
            near, far = (turned_piece, piece) if side == 0 else (piece, turned_piece)
            padded[ch, at, HALO : HALO + half] = first
            padded[ch, at, HALO + half : HALO + tile] = second[: tile - half]
            padded[ch, at, pl.ds(inner, HALO)] = second[tile - half :]
            padded[ch, at, pl.ds(outer, corner)] = near
            padded[ch, at, pl.ds(outer + corner, corner)] = far


def harvest(place, gradient, ze, zo, de, do, re, ro):
    tile = re.shape[2]
    tiles = tile // LANES
    half = ze.shape[1]
    corner = HALO // 2
    even = place[1] == 0
    outer, inner = rows_of(place, tile)
    for ch in range(re.shape[0]):
        strips, corners = [], []
        for at, low in ((0, False), (tiles + 1, True)):
            first = gradient[ch, at, HALO : HALO + half]
            second = jnp.concatenate(
                [gradient[ch, at, HALO + half : HALO + tile], gradient[ch, at, pl.ds(inner, HALO)]],
                0,
            )
            strips.append(fold_pair(first, second, low))
            near = gradient[ch, at, pl.ds(outer, corner)]
            far = gradient[ch, at, pl.ds(outer + corner, corner)]
            corners.append(fold_pair(near, far, low))
        ze[ch] = jnp.where(even, strips[1], strips[0])
        zo[ch] = jnp.where(even, strips[0], strips[1])
        de[ch] = jnp.where(even, corners[1], corners[0])
        do[ch] = jnp.where(even, corners[0], corners[1])
        for k in range(tiles):
            lanes = slice(k * LANES, (k + 1) * LANES)
            re[ch, :, lanes] = gradient[ch, k + 1, pl.ds(inner, HALO)]
            ro[ch, :, lanes] = gradient[ch, k + 1, pl.ds(outer, HALO)]


def sort_positions(offsets, order, inside):
    count = offsets.shape[0]
    needs = [(offsets[i, 1] >= 0) & (offsets[i, 1] <= inside) for i in range(count)]
    at = jnp.int32(0)
    for i in range(count):
        order[at] = i
        at += needs[i].astype(jnp.int32)
    first = at
    for i in range(count):
        order[at] = i
        at += 1 - needs[i].astype(jnp.int32)
    return first


def run_groups(begin, end, group, offsets, order, padded, probe, spectrum, measured, tables, gradient, stage):
    def one(g, carry):
        chains = []
        for k in range(group):
            which = order[g * group + k]
            chains.append(
                chain(
                    offsets[which, 0] + HALO,
                    offsets[which, 1] + LANES,
                    padded,
                    probe,
                    spectrum,
                    measured.at[which],
                    tables,
                    gradient,
                    stage.at[k],
                )
            )
        for _ in itertools.zip_longest(*chains):
            pass
        return carry

    lax.fori_loop(begin, end, one, 0)


def early_body(
    offsets, place, objects, re, ro, probe, kernel, measured, tables,
    padded, gradient, spectrum, order, stage, sems,
):
    tile, width = re.shape[2], probe.shape[1]
    tiles = tile // LANES
    outer, inner = rows_of(place, tile)
    copies = [
        pltpu.make_async_copy(
            objects.at[:, :, pl.ds(k * LANES, LANES)],
            target.at[:, k + 1, pl.ds(HALO, tile), :],
            sems.at[n, k],
        )
        for n, target in enumerate((padded, gradient))
        for k in range(tiles)
    ]
    for copy in copies:
        copy.start()
    first = sort_positions(offsets, order, tile - width)
    for part in range(2):
        spectrum[part] = reorder(kernel[part], tables[4], stage.at[0])
    bottom = gradient.shape[2] - HALO - tile
    for ch in range(gradient.shape[0]):
        for at in (0, tiles + 1):
            gradient[ch, at] = jnp.zeros(gradient.shape[2:], jnp.float32)
        for k in range(tiles):
            gradient[ch, k + 1, :HALO] = jnp.zeros((HALO, LANES), jnp.float32)
            gradient[ch, k + 1, HALO + tile :] = jnp.zeros((bottom, LANES), jnp.float32)
            lanes = slice(k * LANES, (k + 1) * LANES)
            padded[ch, k + 1, pl.ds(inner, HALO)] = re[ch, :, lanes]
            padded[ch, k + 1, pl.ds(outer, HALO)] = ro[ch, :, lanes]
    for copy in copies:
        copy.wait()
    group = stage.shape[0]
    run_groups(
        0, first // group, group, offsets, order,
        padded, probe, spectrum, measured, tables, gradient, stage,
    )


def late_body(
    offsets, place, padded_in, gradient_in, ze, zo, de, do, probe, spectrum, measured, tables,
    padded, gradient, gze, gzo, gde, gdo, gre, gro, order, stage,
):
    tile, width = gre.shape[2], probe.shape[1]
    first = sort_positions(offsets, order, tile - width)
    assemble(place, padded, ze, zo, de, do, tile)
    group = stage.shape[0]
    run_groups(
        first // group, offsets.shape[0] // group, group, offsets, order,
        padded, probe, spectrum, measured, tables, gradient, stage,
    )
    harvest(place, gradient, gze, gzo, gde, gdo, gre, gro)


WHOLE = pl.BlockSpec(memory_space=pltpu.VMEM)
SCALARS = pl.BlockSpec(memory_space=pltpu.SMEM)


def scratch(count, width):
    group = next(k for k in GROUPS if count % k == 0)
    return [
        pltpu.SMEM((count + 1,), jnp.int32),
        pltpu.VMEM((group, 2, width, LANES), jnp.float32),
    ]


def cost(positions, width):
    return pl.CostEstimate(
        flops=positions * 6 * 8 * width**3, bytes_accessed=positions * 4 * width * width, transcendentals=0
    )


def early(offsets, place, objects, re, ro, probe, kernel, measured, tables):
    count, width = measured.shape[0], measured.shape[1]
    channels, tile = objects.shape[:2]
    extended = (channels, tile // LANES + 2, tile + 2 * HALO + ROWS, LANES)
    return pl.pallas_call(
        early_body,
        out_shape=[
            jax.ShapeDtypeStruct(extended, jnp.float32),
            jax.ShapeDtypeStruct(extended, jnp.float32),
            jax.ShapeDtypeStruct(kernel.shape, jnp.float32),
        ],
        in_specs=[SCALARS, SCALARS, pl.BlockSpec(memory_space=pl.ANY)] + [WHOLE] * 6,
        out_specs=[WHOLE] * 3,
        scratch_shapes=scratch(count, width) + [pltpu.SemaphoreType.DMA((2, tile // LANES))],
        compiler_params=pltpu.CompilerParams(vmem_limit_bytes=VMEM),
        cost_estimate=cost(count, width),
        name="early",
    )(offsets, place, objects, re, ro, probe, kernel, measured, tables)


def late(offsets, place, padded, gradient, sides, rows, probe, spectrum, measured, tables):
    count, width = measured.shape[0], measured.shape[1]
    shapes = (padded, gradient) + tuple(sides) + (rows, rows)
    return pl.pallas_call(
        late_body,
        out_shape=[jax.ShapeDtypeStruct(x.shape, jnp.float32) for x in shapes],
        in_specs=[SCALARS, SCALARS] + [WHOLE] * 10,
        out_specs=[WHOLE] * 8,
        scratch_shapes=scratch(count, width),
        input_output_aliases={2: 0, 3: 1},
        compiler_params=pltpu.CompilerParams(vmem_limit_bytes=VMEM),
        cost_estimate=cost(count, width),
        name="late",
    )(offsets, place, padded, gradient, *sides, probe, spectrum, measured, tables)


def relay_body(place, ze, zo, out):
    even = place[1] == 0
    lane = lax.broadcasted_iota(jnp.int32, (1, LANES), 1) < HALO
    for ch in range(out.shape[0]):
        low = jnp.where(even, zo[ch, -HALO:], ze[ch, -HALO:])
        high = jnp.where(even, ze[ch, -HALO:], zo[ch, -HALO:])
        out[ch] = jnp.where(lane, pltpu.roll(low, HALO, 1), high)


def relay(place, ze, zo):
    channels, half = ze.shape[:2]
    return pl.pallas_call(
        relay_body,
        out_shape=jax.ShapeDtypeStruct((channels, HALO, LANES), jnp.float32),
        in_specs=[SCALARS, WHOLE, WHOLE],
        out_specs=WHOLE,
        name="relay",
    )(place, ze, zo)


def settle_body(place, gradient_in, ze, zo, de, do, re, ro, ce, gradient, out, sems):
    tile = re.shape[2]
    tiles = tile // LANES
    half = ze.shape[1]
    corner = HALO // 2
    even = place[1] == 0
    outer = pl.multiple_of(HALO + place[0] * (tile - HALO), HALO)
    inner = pl.multiple_of(HALO + (1 - place[0]) * (tile - HALO), HALO)
    lane = lax.broadcasted_iota(jnp.int32, (1, LANES), 1) < HALO

    def copy(k):
        return pltpu.make_async_copy(
            gradient.at[:, k + 1, pl.ds(HALO, tile), :],
            out.at[:, :, pl.ds(k * LANES, LANES)],
            sems.at[k],
        )

    for k in list(range(1, tiles - 1)) + [0, tiles - 1]:
        for ch in range(re.shape[0]):
            lanes = slice(k * LANES, (k + 1) * LANES)
            gradient[ch, k + 1, pl.ds(inner, HALO)] += re[ch, :, lanes]
            gradient[ch, k + 1, pl.ds(outer, HALO)] += ro[ch, :, lanes]
        for side in range(2):
            if k != (0, tiles - 1)[side]:
                continue
            mask = lane if side == 0 else jnp.logical_not(lane)
            for ch in range(re.shape[0]):
                strip = jnp.where(even, (zo, ze)[side][ch], (ze, zo)[side][ch])
                piece = jnp.where(even, (do, de)[side][ch], (de, do)[side][ch])
                turned, turned_piece = pltpu.roll(strip, HALO, 1), pltpu.roll(piece, HALO, 1)
                first, second = (strip, turned) if side == 0 else (turned, strip)
                near, far = (piece, turned_piece) if side == 0 else (turned_piece, piece)
                gradient[ch, k + 1, HALO : HALO + half] += jnp.where(mask, first, 0.0)
                gradient[ch, k + 1, HALO + half : HALO + tile] += jnp.where(
                    mask, second[: tile - half], 0.0
                )
                gradient[ch, k + 1, pl.ds(outer, corner)] += jnp.where(mask, near, 0.0)
                gradient[ch, k + 1, pl.ds(outer + corner, corner)] += jnp.where(mask, far, 0.0)
                gradient[ch, k + 1, pl.ds(inner, HALO)] += jnp.where(mask, ce[ch], 0.0)
        copy(k).start()
    for k in range(tiles):
        copy(k).wait()


def settle(place, gradient, shares, tile):
    channels = gradient.shape[0]
    return pl.pallas_call(
        settle_body,
        out_shape=[
            jax.ShapeDtypeStruct(gradient.shape, jnp.float32),
            jax.ShapeDtypeStruct((channels, tile, tile), jnp.float32),
        ],
        in_specs=[SCALARS] + [WHOLE] * 8,
        out_specs=[WHOLE, pl.BlockSpec(memory_space=pl.ANY)],
        input_output_aliases={1: 0},
        scratch_shapes=[pltpu.SemaphoreType.DMA((tile // LANES,))],
        compiler_params=pltpu.CompilerParams(vmem_limit_bytes=VMEM),
        name="settle",
    )(place, gradient, *shares)[1]


def swap(x, row, col):
    rows, cols = lax.axis_size("row"), lax.axis_size("col")

    def partner(i, kind):
        return i + kind * (1 - 2 * (i % 2))

    pairs = [
        (r * cols + c, partner(r, row) * cols + partner(c, col))
        for r in range(rows)
        for c in range(cols)
        if 0 <= partner(r, row) < rows and 0 <= partner(c, col) < cols
    ]
    return lax.ppermute(x, ("row", "col"), pairs)


def exchange(ze, zo, de, do):
    return swap(ze, 0, 1), swap(zo, 0, -1), swap(de, -1, 1), swap(do, -1, -1)


def per_device(objects, probe, kernel, measured, offsets):
    tile = objects.shape[1]
    tables = jnp.asarray(make_tables(probe.shape[1]))
    place = jnp.stack([lax.axis_index("row") % 2, lax.axis_index("col") % 2]).astype(jnp.int32)
    offsets, measured = offsets[0, 0], measured[0, 0]
    rows = [
        lax.dynamic_slice_in_dim(objects, at * (tile - HALO), HALO, axis=1)
        for at in (place[0], 1 - place[0])
    ]
    ro = swap(rows[0], -1, 0)
    re = swap(rows[1], 1, 0)
    sides = exchange(*pack(place, objects, re))
    padded, gradient, spectrum = early(
        offsets, place, objects, re, ro, probe, kernel, measured, tables
    )
    _, gradient, *sides, gre, gro = late(
        offsets, place, padded, gradient, sides, re, probe, spectrum, measured, tables
    )
    re, ro = swap(gre, 1, 0), swap(gro, -1, 0)
    ze, zo, de, do = exchange(*sides)
    ze, zo, de, do, re, ro = lax.optimization_barrier((ze, zo, de, do, re, ro))
    ce = swap(relay(place, ze, zo), 1, 0)
    return settle(place, gradient, (ze, zo, de, do, re, ro, ce), tile)


def solution(mesh):
    return jax.shard_map(
        per_device,
        mesh=mesh,
        in_specs=(
            P(None, "row", "col"),
            P(),
            P(),
            P("row", "col", None, None, None),
            P("row", "col", None, None),
        ),
        out_specs=P(None, "row", "col"),
        check_vma=False,
    )
```

time: 105 us -> 89.9 us (0.86)
  the two profiles are of different devices: /device:TPU:11 before, /device:TPU:13 now
where the time goes in v3:
time: 89.9 us; the launch traced here: 89.3 us
  starting transfers between devices  34.6 us (38%)
  Pallas kernels  26.3 us (29%)
  local copies, waits for them, and re-layouts  16 us (18%)
  waiting for transfers between devices  12 us (13%)
    ppermute x13, starting transfers between devices, swap(): return lax.ppermute(x, ('row', 'col'), pairs)  34.6 us
    unnamed x28, local copies, waits for them, and re-layouts  13 us
    pallas_call x1, Pallas kernels, late(): pl.pallas_call(late_body, out_shape=[jax.ShapeDtypeStruct(x.shape, jnp.fl...  12.5 us
    ppermute x13, waiting for transfers between devices, swap(): return lax.ppermute(x, ('row', 'col'), pairs)  12 us
    pallas_call x1, Pallas kernels, early(): pl.pallas_call(early_body, out_shape=[jax.ShapeDtypeStruct(extended, jnp....  8.27 us
    pallas_call x1, Pallas kernels, settle(): pl.pallas_call(settle_body, out_shape=[jax.ShapeDtypeStruct(gradient.shap...  2.63 us
    dynamic_slice x1, local copies, waits for them, and re-layouts, per_device(): lax.dynamic_slice_in_dim(objects, at * (tile - HALO), HALO, axis=1)  2.15 us
    pallas_call x1, Pallas kernels, relay(): pl.pallas_call(relay_body, out_shape=jax.ShapeDtypeStruct((channels, HALO...  2.01 us
  transfers between devices with their start and end apart: 13, of which 6 were waited for; matrix products, arithmetic and copies ran while one was open for 1% of the time, Pallas kernels for 10%

profile of v3, /device:TPU:13, one launch (start us, length us, event | category | flops | bytes accessed | tf_op | source)
XLA Modules:
  0.0 89.3 jit_solution(16062254078852918364)
XLA Ops:
  0.0 2.1 %constant_dynamic-slice_fusion = (f32[4,64,512]{2,1,0:T(8,128)}, f32[4,64,512]{2,1,0:T(8,128)S(1)}) fusion(f32[4,512,512]{2,1,0:T(8,128)} %outer.1, s32[]{:T(128)S(6)} %select_n.20, s32[]{:T(128)S(6)} %select_n.19), kind=kLoop, calls=%fused_computation.1 | loop fusion | bytes 2097160 | tf_op jit(solution)/shard_map/dynamic_slice | solution.py:532
  2.8 3.0 %collective-permute-start.1 = (f32[4,64,512]{2,1,0:T(8,128)}, f32[4,64,512]{2,1,0:T(8,128)}, u32[]{:S(2)}, u32[]{:S(2)}) collective-permute-start(f32[4,64,512]{2,1,0:T(8,128)} %get-tuple-element.47), channel_id=1, source_target_pairs={{4,8},{5,9},{6,10},{7,11},{8,4},{9,5},{10,6},{11,7},{12,16},{13,17... | collective-permute-start | bytes 1572872 | tf_op jit(solution)/shard_map/ppermute | solution.py:519
  6.7 2.2 %copy-done = f32[4,512,512]{2,1,0:T(8,128)S(1)} copy-done((f32[4,512,512]{2,1,0:T(8,128)S(1)}, f32[4,512,512]{2,1,0:T(8,128)}, u32[]{:S(2)}) %copy-start) | copy-done | bytes 4194328
  9.8 2.7 %collective-permute-start.4 = (f32[4,32,128]{2,1,0:T(8,128)S(1)}, f32[4,32,128]{2,1,0:T(8,128)S(1)}, u32[]{:S(2)}, u32[]{:S(2)}) collective-permute-start(f32[4,32,128]{2,1,0:T(8,128)S(1)} %get-tuple-element.30), channel_id=1, source_target_pairs={{4,9},{5,8},{6,11},{7,10},{8,5},{9,4},{10,7},{11,6},{12,17},{13,16... | collective-permute-start | bytes 196616 | tf_op jit(solution)/shard_map/ppermute | solution.py:519
  12.6 5.1 %collective-permute-start.5 = (f32[4,32,128]{2,1,0:T(8,128)S(1)}, f32[4,32,128]{2,1,0:T(8,128)S(1)}, u32[]{:S(2)}, u32[]{:S(2)}) collective-permute-start(f32[4,32,128]{2,1,0:T(8,128)S(1)} %get-tuple-element.31), channel_id=1, source_target_pairs={{5,10},{6,9},{9,6},{10,5},{13,18},{14,17},{17,14},{18,13},{21,26},... | collective-permute-start | bytes 196616 | tf_op jit(solution)/shard_map/ppermute | solution.py:519
  17.8 1.9 %collective-permute-start.3 = (f32[4,288,128]{2,1,0:T(8,128)S(1)}, f32[4,288,128]{2,1,0:T(8,128)S(1)}, u32[]{:S(2)}, u32[]{:S(2)}) collective-permute-start(f32[4,288,128]{2,1,0:T(8,128)S(1)} %get-tuple-element.29), channel_id=1, source_target_pairs={{1,2},{2,1},{5,6},{6,5},{9,10},{10,9},{13,14},{14,13},{17,18},{18,... | collective-permute-start | bytes 1769480 | tf_op jit(solution)/shard_map/ppermute | solution.py:519
  20.0 8.3 %early.1 = (f32[4,6,648,128]{3,2,1,0:T(8,128)S(1)}, f32[4,6,648,128]{3,2,1,0:T(8,128)S(1)}, f32[2,256,256]{2,1,0:T(8,128)S(1)}) custom-call(s32[9,2]{1,0:T(8,128)S(1)} %copy.11.offsets, s32[2]{0:T(128)S(1)} %pad_add_fusion.place, f32[4,512,512]{2,1,0:T(8,128)S(1)} %copy-done.1, f32[4,64,512]{2,1,0:T(8,128)S(1)} %collective-permute-done.re.inner, ...), custom_call_target="tpu_custom_call" | custom-call | flops 7247757312 | bytes 2359296 | tf_op jit(solution)/shard_map/early/pallas_call | solution.py:394
  28.3 3.0 %collective-permute-done.2.ze = f32[4,288,128]{2,1,0:T(8,128)S(1)} collective-permute-done((f32[4,288,128]{2,1,0:T(8,128)S(1)}, f32[4,288,128]{2,1,0:T(8,128)S(1)}, u32[]{:S(2)}, u32[]{:S(2)}) %collective-permute-start.2) | collective-permute-done | bytes 589856 | tf_op jit(solution)/shard_map/ppermute | solution.py:519
  31.3 1.9 %collective-permute-done.3.zo = f32[4,288,128]{2,1,0:T(8,128)S(1)} collective-permute-done((f32[4,288,128]{2,1,0:T(8,128)S(1)}, f32[4,288,128]{2,1,0:T(8,128)S(1)}, u32[]{:S(2)}, u32[]{:S(2)}) %collective-permute-start.3) | collective-permute-done | bytes 589856 | tf_op jit(solution)/shard_map/ppermute | solution.py:519
  33.2 12.5 %late.1 = (f32[4,6,648,128]{3,2,1,0:T(8,128)S(1)}, f32[4,6,648,128]{3,2,1,0:T(8,128)S(1)}, f32[4,288,128]{2,1,0:T(8,128)S(1)}, f32[4,288,128]{2,1,0:T(8,128)S(1)...) custom-call(s32[9,2]{1,0:T(8,128)S(1)} %copy.11.offsets, ...), custom_call_target="tpu_custom_call", output_to_operand_aliasing={{0}: (2, {}), {1}: (3, {})} | custom-call | flops 7247757312 | bytes 2359296 | tf_op jit(solution)/shard_map/late/pallas_call | solution.py:413
  45.6 3.1 %copy-done.2 = f32[4,6,648,128]{3,2,1,0:T(8,128)} copy-done((f32[4,6,648,128]{3,2,1,0:T(8,128)}, f32[4,6,648,128]{3,2,1,0:T(8,128)S(1)}, u32[]{:S(2)}) %copy-start.2) | copy-done | bytes 7962648
  48.7 2.6 %collective-permute-start.7 = (f32[4,288,128]{2,1,0:T(8,128)S(1)}, f32[4,288,128]{2,1,0:T(8,128)S(1)}, u32[]{:S(2)}, u32[]{:S(2)}) collective-permute-start(f32[4,288,128]{2,1,0:T(8,128)S(1)} %get-tuple-element.35), channel_id=1, source_target_pairs={{1,2},{2,1},{5,6},{6,5},{9,10},{10,9},{13,14},{14,13},{17,18},{18,... | collective-permute-start | bytes 1769480 | tf_op jit(solution)/shard_map/ppermute | solution.py:519
  51.3 2.1 %collective-permute-start.10 = (f32[4,64,512]{2,1,0:T(8,128)S(1)}, f32[4,64,512]{2,1,0:T(8,128)S(1)}, u32[]{:S(2)}, u32[]{:S(2)}) collective-permute-start(f32[4,64,512]{2,1,0:T(8,128)S(1)} %get-tuple-element.38), channel_id=1, source_target_pairs={{0,4},{1,5},{2,6},{3,7},{4,0},{5,1},{6,2},{7,3},{8,12},{9,13},{10,... | collective-permute-start | bytes 1572872 | tf_op jit(solution)/shard_map/ppermute | solution.py:519
  53.5 1.9 %collective-permute-start.11 = (f32[4,64,512]{2,1,0:T(8,128)S(1)}, f32[4,64,512]{2,1,0:T(8,128)S(1)}, u32[]{:S(2)}, u32[]{:S(2)}) collective-permute-start(f32[4,64,512]{2,1,0:T(8,128)S(1)} %get-tuple-element.39), channel_id=1, source_target_pairs={{4,8},{5,9},{6,10},{7,11},{8,4},{9,5},{10,6},{11,7},{12,16},{13,17... | collective-permute-start | bytes 1572872 | tf_op jit(solution)/shard_map/ppermute | solution.py:519
  55.4 3.3 %collective-permute-start.8 = (f32[4,32,128]{2,1,0:T(8,128)S(1)}, f32[4,32,128]{2,1,0:T(8,128)S(1)}, u32[]{:S(2)}, u32[]{:S(2)}) collective-permute-start(f32[4,32,128]{2,1,0:T(8,128)S(1)} %get-tuple-element.36), channel_id=1, source_target_pairs={{4,9},{5,8},{6,11},{7,10},{8,5},{9,4},{10,7},{11,6},{12,17},{13,16... | collective-permute-start | bytes 196616 | tf_op jit(solution)/shard_map/ppermute | solution.py:519
  58.7 3.4 %collective-permute-done.8.de = f32[4,32,128]{2,1,0:T(8,128)S(1)} collective-permute-done((f32[4,32,128]{2,1,0:T(8,128)S(1)}, f32[4,32,128]{2,1,0:T(8,128)S(1)}, u32[]{:S(2)}, u32[]{:S(2)}) %collective-permute-start.8) | collective-permute-done | bytes 65568 | tf_op jit(solution)/shard_map/ppermute | solution.py:519
  62.1 5.0 %collective-permute-start.9 = (f32[4,32,128]{2,1,0:T(8,128)S(1)}, f32[4,32,128]{2,1,0:T(8,128)S(1)}, u32[]{:S(2)}, u32[]{:S(2)}) collective-permute-start(f32[4,32,128]{2,1,0:T(8,128)S(1)} %get-tuple-element.37), channel_id=1, source_target_pairs={{5,10},{6,9},{9,6},{10,5},{13,18},{14,17},{17,14},{18,13},{21,26},... | collective-permute-start | bytes 196616 | tf_op jit(solution)/shard_map/ppermute | solution.py:519
  67.2 2.2 %collective-permute-done.9.do = f32[4,32,128]{2,1,0:T(8,128)S(1)} collective-permute-done((f32[4,32,128]{2,1,0:T(8,128)S(1)}, f32[4,32,128]{2,1,0:T(8,128)S(1)}, u32[]{:S(2)}, u32[]{:S(2)}) %collective-permute-start.9) | collective-permute-done | bytes 65568 | tf_op jit(solution)/shard_map/ppermute | solution.py:519
  71.1 2.0 %relay.1 = f32[4,64,128]{2,1,0:T(8,128)} custom-call(s32[2]{0:T(128)} %copy-done.8, f32[4,288,128]{2,1,0:T(8,128)} %copy-done.4, f32[4,288,128]{2,1,0:T(8,128)} %copy-done.6), custom_call_target="tpu_custom_call" | custom-call | tf_op jit(solution)/shard_map/relay/pallas_call | solution.py:437
  73.1 6.2 %collective-permute-start.12 = (f32[4,64,128]{2,1,0:T(8,128)}, f32[4,64,128]{2,1,0:T(8,128)S(1)}, u32[]{:S(2)}, u32[]{:S(2)}) collective-permute-start(f32[4,64,128]{2,1,0:T(8,128)} %relay.1), channel_id=1, source_target_pairs={{0,4},{1,5},{2,6},{3,7},{4,0},{5,1},{6,2},{7,3},{8,12},{9,13},{10,... | collective-permute-start | bytes 393224 | tf_op jit(solution)/shard_map/ppermute | solution.py:519
  79.3 1.2 %collective-permute-done.12.ce = f32[4,64,128]{2,1,0:T(8,128)S(1)} collective-permute-done((f32[4,64,128]{2,1,0:T(8,128)}, f32[4,64,128]{2,1,0:T(8,128)S(1)}, u32[]{:S(2)}, u32[]{:S(2)}) %collective-permute-start.12) | collective-permute-done | bytes 131104 | tf_op jit(solution)/shard_map/ppermute | solution.py:519
  80.5 3.3 %copy-done.3 = f32[4,6,648,128]{3,2,1,0:T(8,128)S(1)} copy-done((f32[4,6,648,128]{3,2,1,0:T(8,128)S(1)}, f32[4,6,648,128]{3,2,1,0:T(8,128)}, u32[]{:S(2)}) %copy-start.3) | copy-done | bytes 7962648
  84.8 1.1 %copy-done.7 = f32[4,288,128]{2,1,0:T(8,128)S(1)} copy-done((f32[4,288,128]{2,1,0:T(8,128)S(1)}, f32[4,288,128]{2,1,0:T(8,128)}, u32[]{:S(2)}) %copy-start.7) | copy-done | bytes 589848
  86.5 2.6 %settle.1 = (f32[4,6,648,128]{3,2,1,0:T(8,128)S(1)}, f32[4,512,512]{2,1,0:T(8,128)}) custom-call(s32[2]{0:T(128)S(1)} %copy-done.9, f32[4,6,648,128]{3,2,1,0:T(8,128)S(1)} %copy-done.3, f32[4,288,128]{2,1,0:T(8,128)S(1)} %copy-done.5, f32[4,288,128]{2,1,0:T(8,128)S(1)} %copy-done.7, ...), custom_call_target="tpu_custom_call", output_to_operand_aliasing={{0}: (1, {})} | custom-call | tf_op jit(solution)/shard_map/settle/pallas_call | solution.py:492
  (38 shorter events, 6.2 us)
Async XLA Ops:
  0.0 20.0 %copy-start.12 = (f32[2,256,256]{2,1,0:T(8,128)S(1)}, f32[2,256,256]{2,1,0:T(8,128)}, u32[]{:S(2)}) copy-start(f32[2,256,256]{2,1,0:T(8,128)} %probe.3) | copy-start | bytes 1572868
  0.0 20.0 %copy-start.11 = (f32[2,256,256]{2,1,0:T(8,128)S(1)}, f32[2,256,256]{2,1,0:T(8,128)}, u32[]{:S(2)}) copy-start(f32[2,256,256]{2,1,0:T(8,128)} %kernel.1) | copy-start | bytes 1572868
  2.2 4.5 %collective-permute-start = (f32[4,64,512]{2,1,0:T(8,128)S(1)}, f32[4,64,512]{2,1,0:T(8,128)S(1)}, u32[]{:S(2)}, u32[]{:S(2)}) collective-permute-start(f32[4,64,512]{2,1,0:T(8,128)S(1)} %get-tuple-element.48), channel_id=1, source_target_pairs={{0,4},{1,5},{2,6},{3,7},{4,0},{5,1},{6,2},{7,3},{8,12},{9,13},{10,... | collective-permute-start | bytes 1572872 | tf_op jit(solution)/shard_map/ppermute | solution.py:519
  2.8 17.1 %collective-permute-start.1 = (f32[4,64,512]{2,1,0:T(8,128)}, f32[4,64,512]{2,1,0:T(8,128)}, u32[]{:S(2)}, u32[]{:S(2)}) collective-permute-start(f32[4,64,512]{2,1,0:T(8,128)} %get-tuple-element.47), channel_id=1, source_target_pairs={{4,8},{5,9},{6,10},{7,11},{8,4},{9,5},{10,6},{11,7},{12,16},{13,17... | collective-permute-start | bytes 1572872 | tf_op jit(solution)/shard_map/ppermute | solution.py:519
  6.7 26.5 %copy-start.8 = (s32[2]{0:T(128)}, s32[2]{0:T(128)S(1)}, u32[]{:S(2)}) copy-start(s32[2]{0:T(128)S(1)} %pad_add_fusion.place) | copy-start | bytes 28
  6.7 2.2 %copy-start = (f32[4,512,512]{2,1,0:T(8,128)S(1)}, f32[4,512,512]{2,1,0:T(8,128)}, u32[]{:S(2)}) copy-start(f32[4,512,512]{2,1,0:T(8,128)} %outer.1) | copy-start | bytes 12582916
  8.9 11.1 %copy-start.1 = (f32[4,512,512]{2,1,0:T(8,128)S(1)}, f32[4,512,512]{2,1,0:T(8,128)}, u32[]{:S(2)}) copy-start(f32[4,512,512]{2,1,0:T(8,128)} %outer.1) | copy-start | bytes 12582916
  8.9 11.1 %copy-start.10 = (f32[1,1,9,256,256]{4,3,2,1,0:T(8,128)S(1)}, f32[1,1,9,256,256]{4,3,2,1,0:T(8,128)}, u32[]{:S(2)}) copy-start(f32[1,1,9,256,256]{4,3,2,1,0:T(8,128)} %param.9) | copy-start | bytes 7077892
  8.9 11.1 %copy-start.13 = (bf16[6,256,256]{2,1,0:T(8,128)(2,1)S(1)}, bf16[6,256,256]{2,1,0:T(8,128)(2,1)}, u32[]{:S(2)}) copy-start(bf16[6,256,256]{2,1,0:T(8,128)(2,1)} %constant.34.clone.tables) | copy-start | bytes 2359300
  9.8 18.4 %collective-permute-start.4 = (f32[4,32,128]{2,1,0:T(8,128)S(1)}, f32[4,32,128]{2,1,0:T(8,128)S(1)}, u32[]{:S(2)}, u32[]{:S(2)}) collective-permute-start(f32[4,32,128]{2,1,0:T(8,128)S(1)} %get-tuple-element.30), channel_id=1, source_target_pairs={{4,9},{5,8},{6,11},{7,10},{8,5},{9,4},{10,7},{11,6},{12,17},{13,16... | collective-permute-start | bytes 196616 | tf_op jit(solution)/shard_map/ppermute | solution.py:519
  12.6 15.7 %collective-permute-start.5 = (f32[4,32,128]{2,1,0:T(8,128)S(1)}, f32[4,32,128]{2,1,0:T(8,128)S(1)}, u32[]{:S(2)}, u32[]{:S(2)}) collective-permute-start(f32[4,32,128]{2,1,0:T(8,128)S(1)} %get-tuple-element.31), channel_id=1, source_target_pairs={{5,10},{6,9},{9,6},{10,5},{13,18},{14,17},{17,14},{18,13},{21,26},... | collective-permute-start | bytes 196616 | tf_op jit(solution)/shard_map/ppermute | solution.py:519
  17.7 13.5 %collective-permute-start.2 = (f32[4,288,128]{2,1,0:T(8,128)S(1)}, f32[4,288,128]{2,1,0:T(8,128)S(1)}, u32[]{:S(2)}, u32[]{:S(2)}) collective-permute-start(f32[4,288,128]{2,1,0:T(8,128)S(1)} %get-tuple-element.28), channel_id=1, source_target_pairs={{0,1},{1,0},{2,3},{3,2},{4,5},{5,4},{6,7},{7,6},{8,9},{9,8},{10,11... | collective-permute-start | bytes 1769480 | tf_op jit(solution)/shard_map/ppermute | solution.py:519
  17.8 15.4 %collective-permute-start.3 = (f32[4,288,128]{2,1,0:T(8,128)S(1)}, f32[4,288,128]{2,1,0:T(8,128)S(1)}, u32[]{:S(2)}, u32[]{:S(2)}) collective-permute-start(f32[4,288,128]{2,1,0:T(8,128)S(1)} %get-tuple-element.29), channel_id=1, source_target_pairs={{1,2},{2,1},{5,6},{6,5},{9,10},{10,9},{13,14},{14,13},{17,18},{18,... | collective-permute-start | bytes 1769480 | tf_op jit(solution)/shard_map/ppermute | solution.py:519
  45.6 3.1 %copy-start.2 = (f32[4,6,648,128]{3,2,1,0:T(8,128)}, f32[4,6,648,128]{3,2,1,0:T(8,128)S(1)}, u32[]{:S(2)}) copy-start(f32[4,6,648,128]{3,2,1,0:T(8,128)S(1)} %get-tuple-element.33.gradient_in) | copy-start | bytes 23887876
  48.7 20.7 %collective-permute-start.6 = (f32[4,288,128]{2,1,0:T(8,128)S(1)}, f32[4,288,128]{2,1,0:T(8,128)S(1)}, u32[]{:S(2)}, u32[]{:S(2)}) collective-permute-start(f32[4,288,128]{2,1,0:T(8,128)S(1)} %get-tuple-element.34), channel_id=1, source_target_pairs={{0,1},{1,0},{2,3},{3,2},{4,5},{5,4},{6,7},{7,6},{8,9},{9,8},{10,11... | collective-permute-start | bytes 1769480 | tf_op jit(solution)/shard_map/ppermute | solution.py:519
  48.7 20.7 %collective-permute-start.7 = (f32[4,288,128]{2,1,0:T(8,128)S(1)}, f32[4,288,128]{2,1,0:T(8,128)S(1)}, u32[]{:S(2)}, u32[]{:S(2)}) collective-permute-start(f32[4,288,128]{2,1,0:T(8,128)S(1)} %get-tuple-element.35), channel_id=1, source_target_pairs={{1,2},{2,1},{5,6},{6,5},{9,10},{10,9},{13,14},{14,13},{17,18},{18,... | collective-permute-start | bytes 1769480 | tf_op jit(solution)/shard_map/ppermute | solution.py:519
  51.3 18.1 %collective-permute-start.10 = (f32[4,64,512]{2,1,0:T(8,128)S(1)}, f32[4,64,512]{2,1,0:T(8,128)S(1)}, u32[]{:S(2)}, u32[]{:S(2)}) collective-permute-start(f32[4,64,512]{2,1,0:T(8,128)S(1)} %get-tuple-element.38), channel_id=1, source_target_pairs={{0,4},{1,5},{2,6},{3,7},{4,0},{5,1},{6,2},{7,3},{8,12},{9,13},{10,... | collective-permute-start | bytes 1572872 | tf_op jit(solution)/shard_map/ppermute | solution.py:519
  53.5 15.9 %collective-permute-start.11 = (f32[4,64,512]{2,1,0:T(8,128)S(1)}, f32[4,64,512]{2,1,0:T(8,128)S(1)}, u32[]{:S(2)}, u32[]{:S(2)}) collective-permute-start(f32[4,64,512]{2,1,0:T(8,128)S(1)} %get-tuple-element.39), channel_id=1, source_target_pairs={{4,8},{5,9},{6,10},{7,11},{8,4},{9,5},{10,6},{11,7},{12,16},{13,17... | collective-permute-start | bytes 1572872 | tf_op jit(solution)/shard_map/ppermute | solution.py:519
  55.4 6.8 %collective-permute-start.8 = (f32[4,32,128]{2,1,0:T(8,128)S(1)}, f32[4,32,128]{2,1,0:T(8,128)S(1)}, u32[]{:S(2)}, u32[]{:S(2)}) collective-permute-start(f32[4,32,128]{2,1,0:T(8,128)S(1)} %get-tuple-element.36), channel_id=1, source_target_pairs={{4,9},{5,8},{6,11},{7,10},{8,5},{9,4},{10,7},{11,6},{12,17},{13,16... | collective-permute-start | bytes 196616 | tf_op jit(solution)/shard_map/ppermute | solution.py:519
  62.1 7.2 %collective-permute-start.9 = (f32[4,32,128]{2,1,0:T(8,128)S(1)}, f32[4,32,128]{2,1,0:T(8,128)S(1)}, u32[]{:S(2)}, u32[]{:S(2)}) collective-permute-start(f32[4,32,128]{2,1,0:T(8,128)S(1)} %get-tuple-element.37), channel_id=1, source_target_pairs={{5,10},{6,9},{9,6},{10,5},{13,18},{14,17},{17,14},{18,13},{21,26},... | collective-permute-start | bytes 196616 | tf_op jit(solution)/shard_map/ppermute | solution.py:519
  73.1 7.4 %collective-permute-start.12 = (f32[4,64,128]{2,1,0:T(8,128)}, f32[4,64,128]{2,1,0:T(8,128)S(1)}, u32[]{:S(2)}, u32[]{:S(2)}) collective-permute-start(f32[4,64,128]{2,1,0:T(8,128)} %relay.1), channel_id=1, source_target_pairs={{0,4},{1,5},{2,6},{3,7},{4,0},{5,1},{6,2},{7,3},{8,12},{9,13},{10,... | collective-permute-start | bytes 393224 | tf_op jit(solution)/shard_map/ppermute | solution.py:519
  80.5 3.3 %copy-start.3 = (f32[4,6,648,128]{3,2,1,0:T(8,128)S(1)}, f32[4,6,648,128]{3,2,1,0:T(8,128)}, u32[]{:S(2)}) copy-start(f32[4,6,648,128]{3,2,1,0:T(8,128)} %copy-done.2) | copy-start | bytes 23887876
  83.7 1.1 %copy-start.5 = (f32[4,288,128]{2,1,0:T(8,128)S(1)}, f32[4,288,128]{2,1,0:T(8,128)}, u32[]{:S(2)}) copy-start(f32[4,288,128]{2,1,0:T(8,128)} %copy-done.4) | copy-start | bytes 1769476
  84.8 1.1 %copy-start.7 = (f32[4,288,128]{2,1,0:T(8,128)S(1)}, f32[4,288,128]{2,1,0:T(8,128)}, u32[]{:S(2)}) copy-start(f32[4,288,128]{2,1,0:T(8,128)} %copy-done.6) | copy-start | bytes 1769476
  (3 other events, 2.4 us)

commit v4 on v3

--- a/solution.py
+++ b/solution.py
@@ -13,6 +13,10 @@
 ROWS = 8
 GROUPS = (3, 2, 1)
 VMEM = 24 * 1024 * 1024
+SMALL = 12 * 1024 * 1024
+LARGE = 58 * 1024 * 1024
+WHOLE = pl.BlockSpec(memory_space=pltpu.VMEM)
+SCALARS = pl.BlockSpec(memory_space=pltpu.SMEM)
 
 
 def make_tables(width):
@@ -145,55 +149,90 @@
     return jnp.where(lane, pltpu.roll(a, HALO, 1), b)
 
 
-def pack_body(place, left, right, outer, inner, ze, zo, de, do):
-    tile = left.shape[1]
+def pack_body(place, objects, ze, zo, re, ro, left, right, sems):
+    tile = objects.shape[2]
     half = ze.shape[1]
-    corner = HALO // 2
     even = place[1] == 0
+    outer = pl.multiple_of(place[0] * (tile - HALO), HALO)
+    inner = pl.multiple_of((1 - place[0]) * (tile - HALO), HALO)
+    copies = [
+        pltpu.make_async_copy(source, target, sems.at[n])
+        for n, (source, target) in enumerate(
+            (
+                (objects.at[:, :, pl.ds(0, LANES)], left),
+                (objects.at[:, :, pl.ds(tile - LANES, LANES)], right),
+                (objects.at[:, pl.ds(outer, HALO), :], ro),
+                (objects.at[:, pl.ds(inner, HALO), :], re),
+            )
+        )
+    ]
+    for copy in copies:
+        copy.start()
+    for copy in copies[:2]:
+        copy.wait()
     for ch in range(left.shape[0]):
-        strips, corners = [], []
-        for ref, lanes, low in (
-            (left, slice(0, LANES), True),
-            (right, slice(tile - LANES, tile), False),
-        ):
-            below = jnp.concatenate([ref[ch, half:], inner[ch, :, lanes]], 0)
-            strips.append(fold_pair(ref[ch, :half], below, low))
-            corners.append(
-                fold_pair(outer[ch, :corner, lanes], outer[ch, corner:, lanes], low)
-            )
-        ze[ch] = jnp.where(even, strips[1], strips[0])
-        zo[ch] = jnp.where(even, strips[0], strips[1])
-        de[ch] = jnp.where(even, corners[1], corners[0])
-        do[ch] = jnp.where(even, corners[0], corners[1])
-
-
-def pack(place, objects, inner):
+        low = fold_pair(left[ch, :half], left[ch, half:], True)
+        high = fold_pair(right[ch, :half], right[ch, half:], False)
+        ze[ch] = jnp.where(even, high, low)
+        zo[ch] = jnp.where(even, low, high)
+    for copy in copies[2:]:
+        copy.wait()
+
+
+def pack(place, objects):
     channels, tile = objects.shape[:2]
-    half = (tile + HALO) // 2
-    last = tile // LANES - 1
-    strip = jax.ShapeDtypeStruct((channels, half, LANES), jnp.float32)
-    corner = jax.ShapeDtypeStruct((channels, HALO // 2, LANES), jnp.float32)
-    whole = pl.BlockSpec(memory_space=pltpu.VMEM)
+    strip = jax.ShapeDtypeStruct((channels, tile // 2, LANES), jnp.float32)
+    rows = jax.ShapeDtypeStruct((channels, HALO, tile), jnp.float32)
     return pl.pallas_call(
         pack_body,
-        out_shape=(strip, strip, corner, corner),
-        grid_spec=pltpu.PrefetchScalarGridSpec(
-            num_scalar_prefetch=1,
-            grid=(1,),
-            in_specs=[
-                pl.BlockSpec((channels, tile, LANES), lambda i, _: (0, 0, 0)),
-                pl.BlockSpec((channels, tile, LANES), lambda i, _: (0, 0, last)),
-                pl.BlockSpec(
-                    (channels, HALO, tile),
-                    lambda i, place: (0, place[0] * (tile // HALO - 1), 0),
-                ),
-                whole,
-            ],
-            out_specs=[whole] * 4,
-        ),
-        compiler_params=pltpu.CompilerParams(vmem_limit_bytes=VMEM),
+        out_shape=(strip, strip, rows, rows),
+        in_specs=[SCALARS, pl.BlockSpec(memory_space=pltpu.HBM)],
+        out_specs=[WHOLE] * 4,
+        scratch_shapes=[
+            pltpu.VMEM((channels, tile, LANES), jnp.float32),
+            pltpu.VMEM((channels, tile, LANES), jnp.float32),
+            pltpu.SemaphoreType.DMA((4,)),
+        ],
+        compiler_params=pltpu.CompilerParams(vmem_limit_bytes=LARGE),
         name="pack",
-    )(place, objects, objects, objects, inner)
+    )(place, objects)
+
+
+def corners_body(place, ze, zo, ce, co):
+    below, even = place[0] == 0, place[1] == 0
+    lane = lax.broadcasted_iota(jnp.int32, (1, LANES), 1) < HALO
+    for ch in range(ze.shape[0]):
+        left = jnp.where(even, zo[ch, :HALO], ze[ch, :HALO])
+        right = jnp.where(even, ze[ch, :HALO], zo[ch, :HALO])
+        top = jnp.where(lane, right, pltpu.roll(left, HALO, 1))
+        left = jnp.where(even, zo[ch, -HALO:], ze[ch, -HALO:])
+        right = jnp.where(even, ze[ch, -HALO:], zo[ch, -HALO:])
+        bottom = jnp.where(lane, pltpu.roll(right, HALO, 1), left)
+        ce[ch] = jnp.where(below, bottom, top)
+        co[ch] = jnp.where(below, top, bottom)
+
+
+def shares_body(place, ze, zo, ce, co):
+    even = place[1] == 0
+    lane = lax.broadcasted_iota(jnp.int32, (1, LANES), 1) < HALO
+    for out, rows in ((ce, slice(-2 * HALO, -HALO)), (co, slice(-HALO, None))):
+        for ch in range(out.shape[0]):
+            low = jnp.where(even, zo[ch, rows], ze[ch, rows])
+            high = jnp.where(even, ze[ch, rows], zo[ch, rows])
+            out[ch] = jnp.where(lane, pltpu.roll(low, HALO, 1), high)
+
+
+def relay(place, ze, zo, relay_body):
+    shape = jax.ShapeDtypeStruct((ze.shape[0], HALO, LANES), jnp.float32)
+    ce, co = pl.pallas_call(
+        relay_body,
+        out_shape=(shape, shape),
+        in_specs=[SCALARS, WHOLE, WHOLE],
+        out_specs=[WHOLE] * 2,
+        compiler_params=pltpu.CompilerParams(vmem_limit_bytes=SMALL),
+        name=relay_body.__name__[:-5],
+    )(place, ze, zo)
+    return swap(ce, 1, 0), swap(co, -1, 0)
 
 
 def chain(top, left, padded, probe, spectrum, measured, tables, gradient, stage):
@@ -227,48 +266,41 @@
     return outer, inner
 
 
-def assemble(place, padded, ze, zo, de, do, tile):
+def assemble(place, padded, ze, zo, ce, co, tile):
     half = ze.shape[1]
-    corner = HALO // 2
     even = place[1] == 0
     outer, inner = rows_of(place, tile)
     for ch in range(ze.shape[0]):
         for side, at in ((0, 0), (1, padded.shape[1] - 1)):
             strip = jnp.where(even, (zo, ze)[side][ch], (ze, zo)[side][ch])
-            piece = jnp.where(even, (do, de)[side][ch], (de, do)[side][ch])
-            turned, turned_piece = pltpu.roll(strip, HALO, 1), pltpu.roll(piece, HALO, 1)
+            turned = pltpu.roll(strip, HALO, 1)
             first, second = (turned, strip) if side == 0 else (strip, turned)
-            near, far = (turned_piece, piece) if side == 0 else (piece, turned_piece)
             padded[ch, at, HALO : HALO + half] = first
-            padded[ch, at, HALO + half : HALO + tile] = second[: tile - half]
-            padded[ch, at, pl.ds(inner, HALO)] = second[tile - half :]
-            padded[ch, at, pl.ds(outer, corner)] = near
-            padded[ch, at, pl.ds(outer + corner, corner)] = far
-
-
-def harvest(place, gradient, ze, zo, de, do, re, ro):
+            padded[ch, at, HALO + half : HALO + tile] = second
+            padded[ch, at, pl.ds(inner, HALO)] = ce[ch]
+            padded[ch, at, pl.ds(outer, HALO)] = co[ch]
+
+
+def harvest(place, gradient, ze, zo, re, ro):
     tile = re.shape[2]
     tiles = tile // LANES
     half = ze.shape[1]
-    corner = HALO // 2
     even = place[1] == 0
     outer, inner = rows_of(place, tile)
     for ch in range(re.shape[0]):
-        strips, corners = [], []
+        strips = []
         for at, low in ((0, False), (tiles + 1, True)):
-            first = gradient[ch, at, HALO : HALO + half]
             second = jnp.concatenate(
-                [gradient[ch, at, HALO + half : HALO + tile], gradient[ch, at, pl.ds(inner, HALO)]],
+                [
+                    gradient[ch, at, HALO + half : HALO + tile],
+                    gradient[ch, at, pl.ds(inner, HALO)],
+                    gradient[ch, at, pl.ds(outer, HALO)],
+                ],
                 0,
             )
-            strips.append(fold_pair(first, second, low))
-            near = gradient[ch, at, pl.ds(outer, corner)]
-            far = gradient[ch, at, pl.ds(outer + corner, corner)]
-            corners.append(fold_pair(near, far, low))
+            strips.append(fold_pair(gradient[ch, at, HALO : HALO + half], second, low))
         ze[ch] = jnp.where(even, strips[1], strips[0])
         zo[ch] = jnp.where(even, strips[0], strips[1])
-        de[ch] = jnp.where(even, corners[1], corners[0])
-        do[ch] = jnp.where(even, corners[0], corners[1])
         for k in range(tiles):
             lanes = slice(k * LANES, (k + 1) * LANES)
             re[ch, :, lanes] = gradient[ch, k + 1, pl.ds(inner, HALO)]
@@ -355,22 +387,18 @@
 
 
 def late_body(
-    offsets, place, padded_in, gradient_in, ze, zo, de, do, probe, spectrum, measured, tables,
-    padded, gradient, gze, gzo, gde, gdo, gre, gro, order, stage,
+    offsets, place, padded_in, gradient_in, ze, zo, ce, co, probe, spectrum, measured, tables,
+    padded, gradient, gze, gzo, gre, gro, order, stage,
 ):
     tile, width = gre.shape[2], probe.shape[1]
     first = sort_positions(offsets, order, tile - width)
-    assemble(place, padded, ze, zo, de, do, tile)
+    assemble(place, padded, ze, zo, ce, co, tile)
     group = stage.shape[0]
     run_groups(
         first // group, offsets.shape[0] // group, group, offsets, order,
         padded, probe, spectrum, measured, tables, gradient, stage,
     )
-    harvest(place, gradient, gze, gzo, gde, gdo, gre, gro)
-
-
-WHOLE = pl.BlockSpec(memory_space=pltpu.VMEM)
-SCALARS = pl.BlockSpec(memory_space=pltpu.SMEM)
+    harvest(place, gradient, gze, gzo, gre, gro)
 
 
 def scratch(count, width):
@@ -407,14 +435,16 @@
     )(offsets, place, objects, re, ro, probe, kernel, measured, tables)
 
 
-def late(offsets, place, padded, gradient, sides, rows, probe, spectrum, measured, tables):
+def late(offsets, place, padded, gradient, sides, probe, spectrum, measured, tables):
     count, width = measured.shape[0], measured.shape[1]
-    shapes = (padded, gradient) + tuple(sides) + (rows, rows)
+    channels, half = sides[0].shape[:2]
+    strip, rows = (channels, half + HALO, LANES), (channels, HALO, 2 * half)
+    shapes = (padded.shape, gradient.shape, strip, strip, rows, rows)
     return pl.pallas_call(
         late_body,
-        out_shape=[jax.ShapeDtypeStruct(x.shape, jnp.float32) for x in shapes],
+        out_shape=[jax.ShapeDtypeStruct(x, jnp.float32) for x in shapes],
         in_specs=[SCALARS, SCALARS] + [WHOLE] * 10,
-        out_specs=[WHOLE] * 8,
+        out_specs=[WHOLE] * 6,
         scratch_shapes=scratch(count, width),
         input_output_aliases={2: 0, 3: 1},
         compiler_params=pltpu.CompilerParams(vmem_limit_bytes=VMEM),
@@ -423,31 +453,10 @@
     )(offsets, place, padded, gradient, *sides, probe, spectrum, measured, tables)
 
 
-def relay_body(place, ze, zo, out):
-    even = place[1] == 0
-    lane = lax.broadcasted_iota(jnp.int32, (1, LANES), 1) < HALO
-    for ch in range(out.shape[0]):
-        low = jnp.where(even, zo[ch, -HALO:], ze[ch, -HALO:])
-        high = jnp.where(even, ze[ch, -HALO:], zo[ch, -HALO:])
-        out[ch] = jnp.where(lane, pltpu.roll(low, HALO, 1), high)
-
-
-def relay(place, ze, zo):
-    channels, half = ze.shape[:2]
-    return pl.pallas_call(
-        relay_body,
-        out_shape=jax.ShapeDtypeStruct((channels, HALO, LANES), jnp.float32),
-        in_specs=[SCALARS, WHOLE, WHOLE],
-        out_specs=WHOLE,
-        name="relay",
-    )(place, ze, zo)
-
-
-def settle_body(place, gradient_in, ze, zo, de, do, re, ro, ce, gradient, out, sems):
+def settle_body(place, gradient_in, ze, zo, re, ro, ce, co, gradient, out, sems):
     tile = re.shape[2]
     tiles = tile // LANES
     half = ze.shape[1]
-    corner = HALO // 2
     even = place[1] == 0
     outer = pl.multiple_of(HALO + place[0] * (tile - HALO), HALO)
     inner = pl.multiple_of(HALO + (1 - place[0]) * (tile - HALO), HALO)
@@ -471,17 +480,14 @@
             mask = lane if side == 0 else jnp.logical_not(lane)
             for ch in range(re.shape[0]):
                 strip = jnp.where(even, (zo, ze)[side][ch], (ze, zo)[side][ch])
-                piece = jnp.where(even, (do, de)[side][ch], (de, do)[side][ch])
-                turned, turned_piece = pltpu.roll(strip, HALO, 1), pltpu.roll(piece, HALO, 1)
+                turned = pltpu.roll(strip, HALO, 1)
                 first, second = (strip, turned) if side == 0 else (turned, strip)
-                near, far = (piece, turned_piece) if side == 0 else (turned_piece, piece)
                 gradient[ch, k + 1, HALO : HALO + half] += jnp.where(mask, first, 0.0)
                 gradient[ch, k + 1, HALO + half : HALO + tile] += jnp.where(
                     mask, second[: tile - half], 0.0
                 )
-                gradient[ch, k + 1, pl.ds(outer, corner)] += jnp.where(mask, near, 0.0)
-                gradient[ch, k + 1, pl.ds(outer + corner, corner)] += jnp.where(mask, far, 0.0)
                 gradient[ch, k + 1, pl.ds(inner, HALO)] += jnp.where(mask, ce[ch], 0.0)
+                gradient[ch, k + 1, pl.ds(outer, HALO)] += jnp.where(mask, co[ch], 0.0)
         copy(k).start()
     for k in range(tiles):
         copy(k).wait()
@@ -495,7 +501,7 @@
             jax.ShapeDtypeStruct(gradient.shape, jnp.float32),
             jax.ShapeDtypeStruct((channels, tile, tile), jnp.float32),
         ],
-        in_specs=[SCALARS] + [WHOLE] * 8,
+        in_specs=[SCALARS] + [WHOLE] * 7,
         out_specs=[WHOLE, pl.BlockSpec(memory_space=pl.ANY)],
         input_output_aliases={1: 0},
         scratch_shapes=[pltpu.SemaphoreType.DMA((tile // LANES,))],
@@ -519,33 +525,24 @@
     return lax.ppermute(x, ("row", "col"), pairs)
 
 
-def exchange(ze, zo, de, do):
-    return swap(ze, 0, 1), swap(zo, 0, -1), swap(de, -1, 1), swap(do, -1, -1)
-
-
 def per_device(objects, probe, kernel, measured, offsets):
     tile = objects.shape[1]
     tables = jnp.asarray(make_tables(probe.shape[1]))
     place = jnp.stack([lax.axis_index("row") % 2, lax.axis_index("col") % 2]).astype(jnp.int32)
     offsets, measured = offsets[0, 0], measured[0, 0]
-    rows = [
-        lax.dynamic_slice_in_dim(objects, at * (tile - HALO), HALO, axis=1)
-        for at in (place[0], 1 - place[0])
-    ]
-    ro = swap(rows[0], -1, 0)
-    re = swap(rows[1], 1, 0)
-    sides = exchange(*pack(place, objects, re))
+    ze, zo, re, ro = pack(place, objects)
+    ze, zo, re, ro = swap(ze, 0, 1), swap(zo, 0, -1), swap(re, 1, 0), swap(ro, -1, 0)
     padded, gradient, spectrum = early(
         offsets, place, objects, re, ro, probe, kernel, measured, tables
     )
-    _, gradient, *sides, gre, gro = late(
-        offsets, place, padded, gradient, sides, re, probe, spectrum, measured, tables
-    )
-    re, ro = swap(gre, 1, 0), swap(gro, -1, 0)
-    ze, zo, de, do = exchange(*sides)
-    ze, zo, de, do, re, ro = lax.optimization_barrier((ze, zo, de, do, re, ro))
-    ce = swap(relay(place, ze, zo), 1, 0)
-    return settle(place, gradient, (ze, zo, de, do, re, ro, ce), tile)
+    ze, zo, spectrum = lax.optimization_barrier((ze, zo, spectrum))
+    sides = (ze, zo, *relay(place, ze, zo, corners_body))
+    _, gradient, ze, zo, re, ro = late(
+        offsets, place, padded, gradient, sides, probe, spectrum, measured, tables
+    )
+    ze, zo, re, ro = swap(ze, 0, 1), swap(zo, 0, -1), swap(re, 1, 0), swap(ro, -1, 0)
+    shares = (ze, zo, re, ro, *relay(place, ze, zo, shares_body))
+    return settle(place, gradient, shares, tile)
 
 
 def solution(mesh):

time: 89.9 us -> 89.6 us (level)
  the two profiles are of different devices: /device:TPU:13 before, /device:TPU:11 now
where the time goes in v4:
time: 89.6 us; the launch traced here: 88.9 us
  Pallas kernels  27.9 us (31%)
  waiting for transfers between devices  26.9 us (30%)
  starting transfers between devices  24.6 us (27%)
  local copies, waits for them, and re-layouts  8.52 us (10%)
    ppermute x12, waiting for transfers between devices, swap(): return lax.ppermute(x, ('row', 'col'), pairs)  26.9 us
    ppermute x12, starting transfers between devices, swap(): return lax.ppermute(x, ('row', 'col'), pairs)  24.6 us
    pallas_call x1, Pallas kernels, late(): pl.pallas_call(late_body, out_shape=[jax.ShapeDtypeStruct(x, jnp.float32)...  12.3 us
    pallas_call x1, Pallas kernels, early(): pl.pallas_call(early_body, out_shape=[jax.ShapeDtypeStruct(extended, jnp....  7.76 us
    unnamed x18, local copies, waits for them, and re-layouts  7.75 us
    pallas_call x1, Pallas kernels, pack(): pl.pallas_call(pack_body, out_shape=(strip, strip, rows, rows), in_specs=...  3.93 us
    pallas_call x1, Pallas kernels, settle(): pl.pallas_call(settle_body, out_shape=[jax.ShapeDtypeStruct(gradient.shap...  2.63 us
  transfers between devices with their start and end apart: 12, of which 5 were waited for; matrix products, arithmetic and copies ran while one was open for 1% of the time, Pallas kernels for 9%

profile of v4, /device:TPU:11, one launch (start us, length us, event | category | flops | bytes accessed | tf_op | source)
XLA Modules:
  0.0 88.9 jit_solution(3513465913540322149)
XLA Ops:
  0.7 3.9 %pack.1 = (f32[4,256,128]{2,1,0:T(8,128)}, f32[4,256,128]{2,1,0:T(8,128)}, f32[4,64,512]{2,1,0:T(8,128)}, f32[4,64,512]{2,1,0:T(8,128)}) custom-call(s32[2]{0:T(128)} %pad_add_fusion.place, f32[4,512,512]{2,1,0:T(8,128)} %objects.3), custom_call_target="tpu_custom_call" | custom-call | tf_op jit(solution)/shard_map/pack/pallas_call | solution.py:186
  4.6 0.7 collective-permute-start
  5.3 3.0 %collective-permute-start.1 = (f32[4,64,512]{2,1,0:T(8,128)}, f32[4,64,512]{2,1,0:T(8,128)S(1)}, u32[]{:S(2)}, u32[]{:S(2)}) collective-permute-start(f32[4,64,512]{2,1,0:T(8,128)} %get-tuple-element.26), channel_id=1, source_target_pairs={{4,8},{5,9},{6,10},{7,11},{8,4},{9,5},{10,6},{11,7},{12,16},{13,17... | collective-permute-start | bytes 1572872 | tf_op jit(solution)/shard_map/ppermute | solution.py:525
  8.6 4.3 %collective-permute-start.3 = (f32[4,256,128]{2,1,0:T(8,128)}, f32[4,256,128]{2,1,0:T(8,128)S(1)}, u32[]{:S(2)}, u32[]{:S(2)}) collective-permute-start(f32[4,256,128]{2,1,0:T(8,128)} %get-tuple-element.30), channel_id=1, source_target_pairs={{1,2},{2,1},{5,6},{6,5},{9,10},{10,9},{13,14},{14,13},{17,18},{18,... | collective-permute-start | bytes 1572872 | tf_op jit(solution)/shard_map/ppermute | solution.py:525
  12.9 0.8 copy.11.offsets
  13.7 8.2 %collective-permute-done.1.ro = f32[4,64,512]{2,1,0:T(8,128)S(1)} collective-permute-done((f32[4,64,512]{2,1,0:T(8,128)}, f32[4,64,512]{2,1,0:T(8,128)S(1)}, u32[]{:S(2)}, u32[]{:S(2)}) %collective-permute-start.1) | collective-permute-done | bytes 524320 | tf_op jit(solution)/shard_map/ppermute | solution.py:525
  21.9 2.2 %copy-done = f32[4,512,512]{2,1,0:T(8,128)S(1)} copy-done((f32[4,512,512]{2,1,0:T(8,128)S(1)}, f32[4,512,512]{2,1,0:T(8,128)}, u32[]{:S(2)}) %copy-start) | copy-done | bytes 4194328
  24.8 1.7 %copy-done.2 = f32[1,1,9,256,256]{4,3,2,1,0:T(8,128)S(1)} copy-done((f32[1,1,9,256,256]{4,3,2,1,0:T(8,128)S(1)}, f32[1,1,9,256,256]{4,3,2,1,0:T(8,128)}, u32[]{:S(2)}) %copy-start.2) | copy-done | bytes 2359320
  26.5 1.0 %copy-done.4 = f32[2,256,256]{2,1,0:T(8,128)S(1)} copy-done((f32[2,256,256]{2,1,0:T(8,128)S(1)}, f32[2,256,256]{2,1,0:T(8,128)}, u32[]{:S(2)}) %copy-start.4) | copy-done | bytes 524312
  27.5 1.0 %copy-done.5 = f32[2,256,256]{2,1,0:T(8,128)S(1)} copy-done((f32[2,256,256]{2,1,0:T(8,128)S(1)}, f32[2,256,256]{2,1,0:T(8,128)}, u32[]{:S(2)}) %copy-start.5) | copy-done | bytes 524312
  28.6 1.1 %copy-done.7 = bf16[6,256,256]{2,1,0:T(8,128)(2,1)S(1)} copy-done((bf16[6,256,256]{2,1,0:T(8,128)(2,1)S(1)}, bf16[6,256,256]{2,1,0:T(8,128)(2,1)}, u32[]{:S(2)}) %copy-start.7) | copy-done | bytes 786456
  29.7 7.8 %early.1 = (f32[4,6,648,128]{3,2,1,0:T(8,128)S(1)}, f32[4,6,648,128]{3,2,1,0:T(8,128)S(1)}, f32[2,256,256]{2,1,0:T(8,128)S(1)}) custom-call(s32[9,2]{1,0:T(8,128)S(1)} %copy.11.offsets, s32[2]{0:T(128)S(1)} %copy-done.1, f32[4,512,512]{2,1,0:T(8,128)S(1)} %copy-done, f32[4,64,512]{2,1,0:T(8,128)S(1)} %collective-permute-done.re, ...), custom_call_target="tpu_custom_call" | custom-call | flops 7247757312 | bytes 2359296 | tf_op jit(solution)/shard_map/early/pallas_call | solution.py:422
  37.5 0.7 corners.1
  38.2 3.4 %collective-permute-start.5 = (f32[4,64,128]{2,1,0:T(8,128)S(1)}, f32[4,64,128]{2,1,0:T(8,128)S(1)}, u32[]{:S(2)}, u32[]{:S(2)}) collective-permute-start(f32[4,64,128]{2,1,0:T(8,128)S(1)} %get-tuple-element.35), channel_id=1, source_target_pairs={{4,8},{5,9},{6,10},{7,11},{8,4},{9,5},{10,6},{11,7},{12,16},{13,17... | collective-permute-start | bytes 393224 | tf_op jit(solution)/shard_map/ppermute | solution.py:525
  41.7 3.8 %collective-permute-done.5.co = f32[4,64,128]{2,1,0:T(8,128)S(1)} collective-permute-done((f32[4,64,128]{2,1,0:T(8,128)S(1)}, f32[4,64,128]{2,1,0:T(8,128)S(1)}, u32[]{:S(2)}, u32[]{:S(2)}) %collective-permute-start.5) | collective-permute-done | bytes 131104 | tf_op jit(solution)/shard_map/ppermute | solution.py:525
  45.5 12.3 %late.1 = (f32[4,6,648,128]{3,2,1,0:T(8,128)S(1)}, f32[4,6,648,128]{3,2,1,0:T(8,128)S(1)}, f32[4,320,128]{2,1,0:T(8,128)S(1)}, f32[4,320,128]{2,1,0:T(8,128)S(1)...) custom-call(s32[9,2]{1,0:T(8,128)S(1)} %copy.11.offsets, ...), custom_call_target="tpu_custom_call", output_to_operand_aliasing={{0}: (2, {}), {1}: (3, {})} | custom-call | flops 7247757312 | bytes 2359296 | tf_op jit(solution)/shard_map/late/pallas_call | solution.py:443
  58.3 4.3 %collective-permute-start.7 = (f32[4,320,128]{2,1,0:T(8,128)S(1)}, f32[4,320,128]{2,1,0:T(8,128)S(1)}, u32[]{:S(2)}, u32[]{:S(2)}) collective-permute-start(f32[4,320,128]{2,1,0:T(8,128)S(1)} %get-tuple-element.39), channel_id=1, source_target_pairs={{1,2},{2,1},{5,6},{6,5},{9,10},{10,9},{13,14},{14,13},{17,18},{18,... | collective-permute-start | bytes 1966088 | tf_op jit(solution)/shard_map/ppermute | solution.py:525
  62.8 4.4 %collective-permute-start.9 = (f32[4,64,512]{2,1,0:T(8,128)S(1)}, f32[4,64,512]{2,1,0:T(8,128)S(1)}, u32[]{:S(2)}, u32[]{:S(2)}) collective-permute-start(f32[4,64,512]{2,1,0:T(8,128)S(1)} %get-tuple-element.41), channel_id=1, source_target_pairs={{4,8},{5,9},{6,10},{7,11},{8,4},{9,5},{10,6},{11,7},{12,16},{13,17... | collective-permute-start | bytes 1572872 | tf_op jit(solution)/shard_map/ppermute | solution.py:525
  67.3 7.3 %collective-permute-done.6.ze = f32[4,320,128]{2,1,0:T(8,128)S(1)} collective-permute-done((f32[4,320,128]{2,1,0:T(8,128)S(1)}, f32[4,320,128]{2,1,0:T(8,128)S(1)}, u32[]{:S(2)}, u32[]{:S(2)}) %collective-permute-start.6) | collective-permute-done | bytes 655392 | tf_op jit(solution)/shard_map/ppermute | solution.py:525
  74.6 3.1 %collective-permute-done.7.zo = f32[4,320,128]{2,1,0:T(8,128)S(1)} collective-permute-done((f32[4,320,128]{2,1,0:T(8,128)S(1)}, f32[4,320,128]{2,1,0:T(8,128)S(1)}, u32[]{:S(2)}, u32[]{:S(2)}) %collective-permute-start.7) | collective-permute-done | bytes 655392 | tf_op jit(solution)/shard_map/ppermute | solution.py:525
  77.7 0.7 shares.1
  79.0 2.8 %collective-permute-start.11 = (f32[4,64,128]{2,1,0:T(8,128)S(1)}, f32[4,64,128]{2,1,0:T(8,128)S(1)}, u32[]{:S(2)}, u32[]{:S(2)}) collective-permute-start(f32[4,64,128]{2,1,0:T(8,128)S(1)} %get-tuple-element.43), channel_id=1, source_target_pairs={{4,8},{5,9},{6,10},{7,11},{8,4},{9,5},{10,6},{11,7},{12,16},{13,17... | collective-permute-start | bytes 393224 | tf_op jit(solution)/shard_map/ppermute | solution.py:525
  81.8 4.4 %collective-permute-done.11.co = f32[4,64,128]{2,1,0:T(8,128)S(1)} collective-permute-done((f32[4,64,128]{2,1,0:T(8,128)S(1)}, f32[4,64,128]{2,1,0:T(8,128)S(1)}, u32[]{:S(2)}, u32[]{:S(2)}) %collective-permute-start.11) | collective-permute-done | bytes 131104 | tf_op jit(solution)/shard_map/ppermute | solution.py:525
  86.1 2.6 %settle.1 = (f32[4,6,648,128]{3,2,1,0:T(8,128)S(1)}, f32[4,512,512]{2,1,0:T(8,128)}) custom-call(s32[2]{0:T(128)S(1)} %copy-done.1, f32[4,6,648,128]{3,2,1,0:T(8,128)S(1)} %get-tuple-element.37.gradient_in, f32[4,320,128]{2,1,0:T(8,128)S(1)} %collective-permute-done.6.ze, ...), custom_call_target="tpu_custom_call", output_to_operand_aliasing={{0}: (1, {})} | custom-call | tf_op jit(solution)/shard_map/settle/pallas_call | solution.py:498
  (26 shorter events, 3.0 us)
Async XLA Ops:
  4.6 9.1 %collective-permute-start = (f32[4,64,512]{2,1,0:T(8,128)}, f32[4,64,512]{2,1,0:T(8,128)S(1)}, u32[]{:S(2)}, u32[]{:S(2)}) collective-permute-start(f32[4,64,512]{2,1,0:T(8,128)} %get-tuple-element.25), channel_id=1, source_target_pairs={{0,4},{1,5},{2,6},{3,7},{4,0},{5,1},{6,2},{7,3},{8,12},{9,13},{10,... | collective-permute-start | bytes 1572872 | tf_op jit(solution)/shard_map/ppermute | solution.py:525
  5.3 16.6 %collective-permute-start.1 = (f32[4,64,512]{2,1,0:T(8,128)}, f32[4,64,512]{2,1,0:T(8,128)S(1)}, u32[]{:S(2)}, u32[]{:S(2)}) collective-permute-start(f32[4,64,512]{2,1,0:T(8,128)} %get-tuple-element.26), channel_id=1, source_target_pairs={{4,8},{5,9},{6,10},{7,11},{8,4},{9,5},{10,6},{11,7},{12,16},{13,17... | collective-permute-start | bytes 1572872 | tf_op jit(solution)/shard_map/ppermute | solution.py:525
  8.4 29.1 %collective-permute-start.2 = (f32[4,256,128]{2,1,0:T(8,128)}, f32[4,256,128]{2,1,0:T(8,128)S(1)}, u32[]{:S(2)}, u32[]{:S(2)}) collective-permute-start(f32[4,256,128]{2,1,0:T(8,128)} %get-tuple-element.29), channel_id=1, source_target_pairs={{0,1},{1,0},{2,3},{3,2},{4,5},{5,4},{6,7},{7,6},{8,9},{9,8},{10,11... | collective-permute-start | bytes 1572872 | tf_op jit(solution)/shard_map/ppermute | solution.py:525
  8.6 28.9 %collective-permute-start.3 = (f32[4,256,128]{2,1,0:T(8,128)}, f32[4,256,128]{2,1,0:T(8,128)S(1)}, u32[]{:S(2)}, u32[]{:S(2)}) collective-permute-start(f32[4,256,128]{2,1,0:T(8,128)} %get-tuple-element.30), channel_id=1, source_target_pairs={{1,2},{2,1},{5,6},{6,5},{9,10},{10,9},{13,14},{14,13},{17,18},{18,... | collective-permute-start | bytes 1572872 | tf_op jit(solution)/shard_map/ppermute | solution.py:525
  21.9 2.2 %copy-start = (f32[4,512,512]{2,1,0:T(8,128)S(1)}, f32[4,512,512]{2,1,0:T(8,128)}, u32[]{:S(2)}) copy-start(f32[4,512,512]{2,1,0:T(8,128)} %objects.3) | copy-start | bytes 12582916
  24.1 0.7 copy-start.1
  24.8 1.7 %copy-start.2 = (f32[1,1,9,256,256]{4,3,2,1,0:T(8,128)S(1)}, f32[1,1,9,256,256]{4,3,2,1,0:T(8,128)}, u32[]{:S(2)}) copy-start(f32[1,1,9,256,256]{4,3,2,1,0:T(8,128)} %param.9) | copy-start | bytes 7077892
  26.5 1.0 %copy-start.4 = (f32[2,256,256]{2,1,0:T(8,128)S(1)}, f32[2,256,256]{2,1,0:T(8,128)}, u32[]{:S(2)}) copy-start(f32[2,256,256]{2,1,0:T(8,128)} %kernel.1) | copy-start | bytes 1572868
  27.5 1.0 %copy-start.5 = (f32[2,256,256]{2,1,0:T(8,128)S(1)}, f32[2,256,256]{2,1,0:T(8,128)}, u32[]{:S(2)}) copy-start(f32[2,256,256]{2,1,0:T(8,128)} %probe.3) | copy-start | bytes 1572868
  28.5 1.1 %copy-start.7 = (bf16[6,256,256]{2,1,0:T(8,128)(2,1)S(1)}, bf16[6,256,256]{2,1,0:T(8,128)(2,1)}, u32[]{:S(2)}) copy-start(bf16[6,256,256]{2,1,0:T(8,128)(2,1)} %constant.28.clone.tables) | copy-start | bytes 2359300
  29.7 15.9 %copy-start.3 = (f32[1,1,9,256,256]{4,3,2,1,0:T(8,128)S(1)}, f32[1,1,9,256,256]{4,3,2,1,0:T(8,128)}, u32[]{:S(2)}) copy-start(f32[1,1,9,256,256]{4,3,2,1,0:T(8,128)} %param.9) | copy-start | bytes 7077892
  29.7 15.9 %copy-start.6 = (f32[2,256,256]{2,1,0:T(8,128)S(1)}, f32[2,256,256]{2,1,0:T(8,128)}, u32[]{:S(2)}) copy-start(f32[2,256,256]{2,1,0:T(8,128)} %probe.3) | copy-start | bytes 1572868
  29.7 15.9 %copy-start.8 = (bf16[6,256,256]{2,1,0:T(8,128)(2,1)S(1)}, bf16[6,256,256]{2,1,0:T(8,128)(2,1)}, u32[]{:S(2)}) copy-start(bf16[6,256,256]{2,1,0:T(8,128)(2,1)} %constant.28.clone.tables) | copy-start | bytes 2359300
  38.2 3.5 %collective-permute-start.4 = (f32[4,64,128]{2,1,0:T(8,128)S(1)}, f32[4,64,128]{2,1,0:T(8,128)S(1)}, u32[]{:S(2)}, u32[]{:S(2)}) collective-permute-start(f32[4,64,128]{2,1,0:T(8,128)S(1)} %get-tuple-element.34), channel_id=1, source_target_pairs={{0,4},{1,5},{2,6},{3,7},{4,0},{5,1},{6,2},{7,3},{8,12},{9,13},{10,... | collective-permute-start | bytes 393224 | tf_op jit(solution)/shard_map/ppermute | solution.py:525
  38.2 7.3 %collective-permute-start.5 = (f32[4,64,128]{2,1,0:T(8,128)S(1)}, f32[4,64,128]{2,1,0:T(8,128)S(1)}, u32[]{:S(2)}, u32[]{:S(2)}) collective-permute-start(f32[4,64,128]{2,1,0:T(8,128)S(1)} %get-tuple-element.35), channel_id=1, source_target_pairs={{4,8},{5,9},{6,10},{7,11},{8,4},{9,5},{10,6},{11,7},{12,16},{13,17... | collective-permute-start | bytes 393224 | tf_op jit(solution)/shard_map/ppermute | solution.py:525
  57.8 16.8 %collective-permute-start.6 = (f32[4,320,128]{2,1,0:T(8,128)S(1)}, f32[4,320,128]{2,1,0:T(8,128)S(1)}, u32[]{:S(2)}, u32[]{:S(2)}) collective-permute-start(f32[4,320,128]{2,1,0:T(8,128)S(1)} %get-tuple-element.38), channel_id=1, source_target_pairs={{0,1},{1,0},{2,3},{3,2},{4,5},{5,4},{6,7},{7,6},{8,9},{9,8},{10,11... | collective-permute-start | bytes 1966088 | tf_op jit(solution)/shard_map/ppermute | solution.py:525
  58.3 19.4 %collective-permute-start.7 = (f32[4,320,128]{2,1,0:T(8,128)S(1)}, f32[4,320,128]{2,1,0:T(8,128)S(1)}, u32[]{:S(2)}, u32[]{:S(2)}) collective-permute-start(f32[4,320,128]{2,1,0:T(8,128)S(1)} %get-tuple-element.39), channel_id=1, source_target_pairs={{1,2},{2,1},{5,6},{6,5},{9,10},{10,9},{13,14},{14,13},{17,18},{18,... | collective-permute-start | bytes 1966088 | tf_op jit(solution)/shard_map/ppermute | solution.py:525
  62.6 19.2 %collective-permute-start.8 = (f32[4,64,512]{2,1,0:T(8,128)S(1)}, f32[4,64,512]{2,1,0:T(8,128)S(1)}, u32[]{:S(2)}, u32[]{:S(2)}) collective-permute-start(f32[4,64,512]{2,1,0:T(8,128)S(1)} %get-tuple-element.40), channel_id=1, source_target_pairs={{0,4},{1,5},{2,6},{3,7},{4,0},{5,1},{6,2},{7,3},{8,12},{9,13},{10,... | collective-permute-start | bytes 1572872 | tf_op jit(solution)/shard_map/ppermute | solution.py:525
  62.8 18.9 %collective-permute-start.9 = (f32[4,64,512]{2,1,0:T(8,128)S(1)}, f32[4,64,512]{2,1,0:T(8,128)S(1)}, u32[]{:S(2)}, u32[]{:S(2)}) collective-permute-start(f32[4,64,512]{2,1,0:T(8,128)S(1)} %get-tuple-element.41), channel_id=1, source_target_pairs={{4,8},{5,9},{6,10},{7,11},{8,4},{9,5},{10,6},{11,7},{12,16},{13,17... | collective-permute-start | bytes 1572872 | tf_op jit(solution)/shard_map/ppermute | solution.py:525
  78.4 3.4 %collective-permute-start.10 = (f32[4,64,128]{2,1,0:T(8,128)S(1)}, f32[4,64,128]{2,1,0:T(8,128)S(1)}, u32[]{:S(2)}, u32[]{:S(2)}) collective-permute-start(f32[4,64,128]{2,1,0:T(8,128)S(1)} %get-tuple-element.42), channel_id=1, source_target_pairs={{0,4},{1,5},{2,6},{3,7},{4,0},{5,1},{6,2},{7,3},{8,12},{9,13},{10,... | collective-permute-start | bytes 393224 | tf_op jit(solution)/shard_map/ppermute | solution.py:525
  79.0 7.2 %collective-permute-start.11 = (f32[4,64,128]{2,1,0:T(8,128)S(1)}, f32[4,64,128]{2,1,0:T(8,128)S(1)}, u32[]{:S(2)}, u32[]{:S(2)}) collective-permute-start(f32[4,64,128]{2,1,0:T(8,128)S(1)} %get-tuple-element.43), channel_id=1, source_target_pairs={{4,8},{5,9},{6,10},{7,11},{8,4},{9,5},{10,6},{11,7},{12,16},{13,17... | collective-permute-start | bytes 393224 | tf_op jit(solution)/shard_map/ppermute | solution.py:525

commit v5 on v4

v5 whole, which is shorter than its diff:
```python
import itertools
import jax
import jax.numpy as jnp
import numpy as np
from jax import lax
from jax.experimental import pallas as pl
from jax.experimental.pallas import tpu as pltpu
from jax.sharding import PartitionSpec as P

HALO = 64
RATE = 0.5
LANES = 128
ROWS = 8
GROUPS = (3, 2, 1)
VMEM = 24 * 1024 * 1024
SMALL = 12 * 1024 * 1024
LARGE = 24 * 1024 * 1024
WHOLE = pl.BlockSpec(memory_space=pltpu.VMEM)
SCALARS = pl.BlockSpec(memory_space=pltpu.SMEM)


def make_tables(width):
    half = width // 2
    index = np.arange(width)
    angle = 2.0 * np.pi / width * (index[:, None] * index[None, :] % width)
    cosine = np.cos(angle) / np.sqrt(width)
    sine = np.sin(angle) / np.sqrt(width)

    def block(parity):
        c, s = cosine[parity::2, :half], sine[parity::2, :half]
        return np.block([[c, s], [-s, c]])

    even, odd = block(0), block(1)
    order = np.zeros((width, width))
    order[index[0::2], np.arange(half)] = 1.0
    order[index[1::2], half + np.arange(half)] = 1.0
    return np.stack([even, odd, even.T, odd.T, order, RATE * order]).astype(jnp.bfloat16)


def dot(a, b):
    return jnp.dot(a, b, preferred_element_type=jnp.float32)


def forward(xr, xi, tables):
    half = xr.shape[0] // 2
    le, lo, re, ro = tables[0], tables[1], tables[2], tables[3]
    u = jnp.concatenate([xr[:half] + xr[half:], xi[:half] + xi[half:]], 0)
    v = jnp.concatenate([xr[:half] - xr[half:], xi[:half] - xi[half:]], 0)
    e = dot(le, u.astype(jnp.bfloat16))
    o = dot(lo, v.astype(jnp.bfloat16))
    yield

    def fold(parts):
        fr, fi = parts[:half], parts[half:]
        p = jnp.concatenate([fr[:, :half] + fr[:, half:], fi[:, :half] + fi[:, half:]], 1)
        m = jnp.concatenate([fr[:, :half] - fr[:, half:], fi[:, :half] - fi[:, half:]], 1)
        return p.astype(jnp.bfloat16), m.astype(jnp.bfloat16)

    pe, me = fold(e)
    po, mo = fold(o)
    y = dot(jnp.concatenate([pe, po], 0), re)
    z = dot(jnp.concatenate([me, mo], 0), ro)
    yield
    return (
        jnp.concatenate([y[:, :half], z[:, :half]], 1),
        jnp.concatenate([y[:, half:], z[:, half:]], 1),
    )


def inverse(xr, xi, tables):
    half = xr.shape[0] // 2
    le, lo, re, ro = tables[2], tables[3], tables[0], tables[1]
    e = dot(le, jnp.concatenate([xr[:half], xi[:half]], 0).astype(jnp.bfloat16))
    o = dot(lo, jnp.concatenate([xr[half:], xi[half:]], 0).astype(jnp.bfloat16))
    yield
    p = (e + o).astype(jnp.bfloat16)
    m = (e - o).astype(jnp.bfloat16)

    def pick(cols):
        return jnp.concatenate(
            [
                jnp.concatenate([p[:half, cols], p[half:, cols]], 1),
                jnp.concatenate([m[:half, cols], m[half:, cols]], 1),
            ],
            0,
        )

    y = dot(pick(slice(0, half)), re)
    z = dot(pick(slice(half, 2 * half)), ro)
    yield
    s, d = y + z, y - z
    return (
        jnp.concatenate([s[:, :half], d[:, :half]], 1),
        jnp.concatenate([s[:, half:], d[:, half:]], 1),
    )


def reorder(x, order, stage):
    half = x.shape[0] // 2
    high = x.astype(jnp.bfloat16)
    low = (x - high.astype(jnp.float32)).astype(jnp.bfloat16)
    columns = dot(high, order) + dot(low, order)
    parts = []
    for k in range(2):
        stage[k] = columns[:, k * LANES : (k + 1) * LANES]
        parts.append(
            jnp.concatenate([stage[k, pl.ds(0, half, 2), :], stage[k, pl.ds(1, half, 2), :]], 0)
        )
    return jnp.concatenate(parts, 1)


def rolled(x, down, right):
    return pltpu.roll(pltpu.roll(x, down, 0), right, 1)


def masks(down, right):
    sub = lax.broadcasted_iota(jnp.int32, (ROWS, LANES), 0) >= down
    lane = lax.broadcasted_iota(jnp.int32, (1, LANES), 1) >= right
    return sub, lane


def window(ref, channel, row, tile, down, right, width):
    sub, lane = masks(down, right)
    parts = []
    for k in range(3):
        at = ref[channel, tile + k, pl.ds(row, width), :]
        after = ref[channel, tile + k, pl.ds(row + width, ROWS), :]
        parts.append(jnp.concatenate([jnp.where(sub, at[:ROWS], after), at[ROWS:]], 0))
    return jnp.concatenate([jnp.where(lane, parts[0], parts[2]), parts[1]], 1)


def accumulate(ref, channel, row, tile, down, right, value):
    width = value.shape[0]
    sub, lane = masks(down, right)
    first = value[:, :LANES]
    for k, part in enumerate(
        (jnp.where(lane, first, 0.0), value[:, LANES:], jnp.where(lane, 0.0, first))
    ):
        head = part[:ROWS]
        ref[channel, tile + k, pl.ds(row, ROWS), :] += jnp.where(sub, head, 0.0)
        ref[channel, tile + k, pl.ds(row + ROWS, width - ROWS), :] += part[ROWS:]
        ref[channel, tile + k, pl.ds(row + width, ROWS), :] += jnp.where(sub, 0.0, head)


def fold_pair(a, b, low_first):
    lane = lax.broadcasted_iota(jnp.int32, (1, LANES), 1) < HALO
    if low_first:
        return jnp.where(lane, a, pltpu.roll(b, HALO, 1))
    return jnp.where(lane, pltpu.roll(a, HALO, 1), b)


def here():
    return lax.axis_index("row") % 2, lax.axis_index("col") % 2


def low_lanes():
    return lax.broadcasted_iota(jnp.int32, (1, LANES), 1) < HALO


def pack_body(objects, padded, ze, zo, re, ro, co, sems):
    tile = objects.shape[2]
    tiles = tile // LANES
    half = ze.shape[1]
    row, col = here()
    even = col == 0
    outer = pl.multiple_of(HALO + row * (tile - HALO), HALO)
    inner = pl.multiple_of(HALO + (1 - row) * (tile - HALO), HALO)
    lane = low_lanes()
    copies = [
        pltpu.make_async_copy(
            objects.at[:, :, pl.ds(k * LANES, LANES)],
            padded.at[:, k + 1, pl.ds(HALO, tile), :],
            sems.at[k],
        )
        for k in range(tiles)
    ]
    edges = (0, tiles - 1)
    between = range(1, tiles - 1)
    for k in (*edges, *between):
        copies[k].start()
    for k in edges:
        copies[k].wait()
    for ch in range(ze.shape[0]):
        low, high = (
            fold_pair(
                padded[ch, k + 1, HALO : HALO + half],
                padded[ch, k + 1, HALO + half : HALO + tile],
                k == 0,
            )
            for k in edges
        )
        zo[ch], ze[ch] = jnp.where(even, low, high), jnp.where(even, high, low)
        first, last = (padded[ch, k + 1, pl.ds(outer, HALO)] for k in edges)
        co[ch] = jnp.where(lane, first, last)
    for k in between:
        copies[k].wait()
    for ch in range(ze.shape[0]):
        for k in range(tiles):
            lanes = slice(k * LANES, (k + 1) * LANES)
            re[ch, :, lanes] = padded[ch, k + 1, pl.ds(inner, HALO)]
            ro[ch, :, lanes] = padded[ch, k + 1, pl.ds(outer, HALO)]


def floats(*shape):
    return jax.ShapeDtypeStruct(shape, jnp.float32)


def pack(objects):
    channels, tile = objects.shape[:2]
    strip, rows = floats(channels, tile // 2, LANES), floats(channels, HALO, tile)
    extended = pltpu.VMEM(
        (channels, tile // LANES + 2, tile + 2 * HALO + ROWS, LANES), jnp.float32
    )
    return pl.pallas_call(
        pack_body,
        out_shape=(extended, strip, strip, rows, rows, floats(channels, HALO, LANES)),
        in_specs=[pl.BlockSpec(memory_space=pltpu.HBM)],
        out_specs=[WHOLE] * 6,
        scratch_shapes=[pltpu.SemaphoreType.DMA((tile // LANES,))],
        compiler_params=pltpu.CompilerParams(vmem_limit_bytes=LARGE),
        name="pack",
    )(objects)


def extend_body(ze_in, zo_in, re, co, ze, zo):
    even = here()[1] == 0
    half, last = ze_in.shape[1], re.shape[2] - LANES
    lane = low_lanes()
    for ch in range(ze.shape[0]):
        ze[ch, :half] = ze_in[ch]
        zo[ch, :half] = zo_in[ch]
        rows = jnp.where(lane, re[ch, :, :LANES], re[ch, :, last:])
        low = jnp.where(lane, rows, pltpu.roll(co[ch], HALO, 1))
        high = jnp.where(lane, pltpu.roll(rows, HALO, 1), co[ch])
        zo[ch, half:] = jnp.where(even, low, high)
        ze[ch, half:] = jnp.where(even, high, low)


def extend(ze, zo, re, co):
    strip = floats(ze.shape[0], ze.shape[1] + HALO, LANES)
    return pl.pallas_call(
        extend_body,
        out_shape=(strip, strip),
        in_specs=[WHOLE] * 4,
        out_specs=[WHOLE] * 2,
        compiler_params=pltpu.CompilerParams(vmem_limit_bytes=SMALL),
        name="extend",
    )(ze, zo, re, co)


def gather_body(ze_in, zo_in, ce, co, ze, zo):
    row, col = here()
    below, even = row == 0, col == 0
    lane = low_lanes()
    half = ze.shape[1]
    first, last = slice(0, HALO), slice(half - HALO, half)
    for ch in range(ze.shape[0]):
        top = jnp.where(below, co[ch], ce[ch])
        bottom = jnp.where(below, ce[ch], co[ch])
        left = (jnp.where(lane, pltpu.roll(top, HALO, 1), 0.0), jnp.where(lane, 0.0, bottom))
        right = (jnp.where(lane, top, 0.0), jnp.where(lane, 0.0, pltpu.roll(bottom, HALO, 1)))
        for rows, low, high in zip((first, last), left, right):
            zo[ch, rows] += jnp.where(even, low, high)
            ze[ch, rows] += jnp.where(even, high, low)


def gather(ze, zo, ce, co):
    strip = floats(*ze.shape)
    return pl.pallas_call(
        gather_body,
        out_shape=(strip, strip),
        in_specs=[WHOLE] * 4,
        out_specs=[WHOLE] * 2,
        input_output_aliases={0: 0, 1: 1},
        compiler_params=pltpu.CompilerParams(vmem_limit_bytes=SMALL),
        name="gather",
    )(ze, zo, ce, co)


def chain(top, left, padded, probe, spectrum, measured, tables, gradient):
    width = probe.shape[1]
    down, right = top % ROWS, left % LANES
    row, column = pl.multiple_of(top - down, ROWS), left // LANES
    spot = (row, column, down, right)
    pr, pim = rolled(probe[0], down, right), rolled(probe[1], down, right)
    kr, kim = spectrum[0], spectrum[1]
    o1r = window(padded, 0, *spot, width)
    o1i = window(padded, 1, *spot, width)
    fr, fi = yield from forward(pr * o1r - pim * o1i, pr * o1i + pim * o1r, tables)
    sr, si = yield from inverse(kr * fr - kim * fi, kr * fi + kim * fr, tables)
    o2r = window(padded, 2, *spot, width)
    o2i = window(padded, 3, *spot, width)
    zr, zi = yield from forward(sr * o2r - si * o2i, sr * o2i + si * o2r, tables)
    factor = measured[...] * lax.rsqrt(zr * zr + zi * zi + 1.0) - RATE
    gr, gi = yield from inverse(zr * factor, zi * factor, tables)
    accumulate(gradient, 2, *spot, sr * gr + si * gi)
    accumulate(gradient, 3, *spot, sr * gi - si * gr)
    ur, ui = yield from forward(o2r * gr + o2i * gi, o2r * gi - o2i * gr, tables)
    wr, wi = yield from inverse(kr * ur + kim * ui, kr * ui - kim * ur, tables)
    accumulate(gradient, 0, *spot, pr * wr + pim * wi)
    accumulate(gradient, 1, *spot, pr * wi - pim * wr)


def rows_of(row, tile):
    outer = pl.multiple_of(row * (tile + HALO), HALO)
    inner = pl.multiple_of((1 - row) * (tile + HALO), HALO)
    return outer, inner


def assemble(padded, ze, zo, tile):
    row, col = here()
    even = col == 0
    half = tile // 2
    outer, inner = rows_of(row, tile)
    for ch in range(ze.shape[0]):
        for side, at in ((0, 0), (1, padded.shape[1] - 1)):
            strip = jnp.where(even, (zo, ze)[side][ch], (ze, zo)[side][ch])
            turned = pltpu.roll(strip, HALO, 1)
            first, second = (turned, strip) if side == 0 else (strip, turned)
            padded[ch, at, HALO : HALO + half] = first[:half]
            padded[ch, at, HALO + half : HALO + tile] = second[:half]
            padded[ch, at, pl.ds(inner, HALO)] = first[half:]
            padded[ch, at, pl.ds(outer, HALO)] = second[half:]


def harvest(gradient, ze, zo, re, ro, ce, co):
    tile = re.shape[2]
    tiles = tile // LANES
    half = ze.shape[1]
    row, col = here()
    even = col == 0
    lane = low_lanes()
    outer, inner = rows_of(row, tile)
    for ch in range(re.shape[0]):
        for out, rows in ((ce, inner), (co, outer)):
            out[ch] = jnp.where(
                lane, gradient[ch, tiles + 1, pl.ds(rows, HALO)], gradient[ch, 0, pl.ds(rows, HALO)]
            )
        left, right = (
            fold_pair(
                gradient[ch, at, HALO : HALO + half],
                gradient[ch, at, HALO + half : HALO + tile],
                at > 0,
            )
            for at in (0, tiles + 1)
        )
        ze[ch] = jnp.where(even, right, left)
        zo[ch] = jnp.where(even, left, right)
        for k in range(tiles):
            lanes = slice(k * LANES, (k + 1) * LANES)
            re[ch, :, lanes] = gradient[ch, k + 1, pl.ds(inner, HALO)]
            ro[ch, :, lanes] = gradient[ch, k + 1, pl.ds(outer, HALO)]


def sort_positions(offsets, order, inside):
    count = offsets.shape[1]
    needs = [(offsets[1, i] >= 0) & (offsets[1, i] <= inside) for i in range(count)]
    at = jnp.int32(0)
    for i in range(count):
        order[at] = i
        at += needs[i].astype(jnp.int32)
    first = at
    for i in range(count):
        order[at] = i
        at += 1 - needs[i].astype(jnp.int32)
    return first


def run_groups(begin, end, offsets, order, padded, probe, spectrum, measured, tables, gradient):
    group = group_of(offsets.shape[1])

    def one(g, carry):
        chains = []
        for k in range(group):
            which = order[g * group + k]
            chains.append(
                chain(
                    offsets[0, which] + HALO,
                    offsets[1, which] + LANES,
                    padded,
                    probe,
                    spectrum,
                    measured.at[which],
                    tables,
                    gradient,
                )
            )
        for _ in itertools.zip_longest(*chains):
            pass
        return carry

    lax.fori_loop(begin, end, one, 0)


def prepare_body(
    padded, probe_in, kernel, measured, tables_in,
    gradient, probe, tables, spectrum, amplitudes, held, patterns, stage, sems,
):
    tile = gradient.shape[2] - 2 * HALO - ROWS
    tiles = gradient.shape[1] - 2
    loads = [
        pltpu.make_async_copy(source, target, sems.at[n])
        for n, (source, target) in enumerate(
            ((tables_in, tables), (kernel, held), (probe_in, probe), (measured, patterns))
        )
    ]
    rows = pl.ds(HALO, tile)
    copies = [
        pltpu.make_async_copy(
            padded.at[:, k + 1, rows, :], gradient.at[:, k + 1, rows, :], sems.at[len(loads) + k]
        )
        for k in range(tiles)
    ]
    for copy in loads + copies:
        copy.start()
    bottom = gradient.shape[2] - HALO - tile
    for ch in range(gradient.shape[0]):
        for at in (0, tiles + 1):
            gradient[ch, at] = jnp.zeros(gradient.shape[2:], jnp.float32)
        for k in range(tiles):
            gradient[ch, k + 1, :HALO] = jnp.zeros((HALO, LANES), jnp.float32)
            gradient[ch, k + 1, HALO + tile :] = jnp.zeros((bottom, LANES), jnp.float32)
    for copy in loads:
        copy.wait()
    for part in range(2):
        spectrum[part] = reorder(held[part], tables[4], stage.at[part])
    for which in range(patterns.shape[0]):
        amplitudes[which] = reorder(patterns[which], tables[5], stage.at[which % 2])
    for copy in copies:
        copy.wait()


def early_body(
    offsets, padded_in, gradient_in, re, ro, probe, spectrum, amplitudes, tables,
    padded, gradient, order,
):
    tile, width = re.shape[2], probe.shape[1]
    outer, inner = rows_of(here()[0], tile)
    first = sort_positions(offsets, order, tile - width)
    for ch in range(gradient.shape[0]):
        for k in range(tile // LANES):
            lanes = slice(k * LANES, (k + 1) * LANES)
            padded[ch, k + 1, pl.ds(inner, HALO)] = re[ch, :, lanes]
            padded[ch, k + 1, pl.ds(outer, HALO)] = ro[ch, :, lanes]
    run_groups(
        0, first // group_of(offsets.shape[1]), offsets, order,
        padded, probe, spectrum, amplitudes, tables, gradient,
    )


def late_body(
    offsets, padded_in, gradient_in, ze, zo, probe, spectrum, amplitudes, tables,
    padded, gradient, gze, gzo, gre, gro, gce, gco, order,
):
    tile, width = gre.shape[2], probe.shape[1]
    first = sort_positions(offsets, order, tile - width)
    assemble(padded, ze, zo, tile)
    group = group_of(offsets.shape[1])
    run_groups(
        first // group, offsets.shape[1] // group, offsets, order,
        padded, probe, spectrum, amplitudes, tables, gradient,
    )
    harvest(gradient, gze, gzo, gre, gro, gce, gco)


def group_of(count):
    return next(k for k in GROUPS if count % k == 0)


def cost(positions, width):
    return pl.CostEstimate(
        flops=positions * 6 * 8 * width**3, bytes_accessed=positions * 4 * width * width, transcendentals=0
    )


def prepare(padded, probe, kernel, measured, tables):
    width = probe.shape[1]
    far = pl.BlockSpec(memory_space=pltpu.HBM)
    anywhere = pl.BlockSpec(memory_space=pl.ANY)
    return pl.pallas_call(
        prepare_body,
        out_shape=[
            floats(*padded.shape),
            floats(*probe.shape),
            jax.ShapeDtypeStruct(tables.shape, tables.dtype),
            floats(*kernel.shape),
            floats(*measured.shape),
        ],
        in_specs=[WHOLE] + [far] * 3 + [anywhere],
        out_specs=[WHOLE] * 5,
        scratch_shapes=[
            pltpu.VMEM(kernel.shape, jnp.float32),
            pltpu.VMEM(measured.shape, jnp.float32),
            pltpu.VMEM((2, 2, width, LANES), jnp.float32),
            pltpu.SemaphoreType.DMA((4 + padded.shape[1] - 2,)),
        ],
        compiler_params=pltpu.CompilerParams(vmem_limit_bytes=VMEM),
        cost_estimate=cost(2, width),
        name="prepare",
    )(padded, probe, kernel, measured, tables)


def early(offsets, padded, gradient, re, ro, fixed):
    count, width = fixed[2].shape[:2]
    return pl.pallas_call(
        early_body,
        out_shape=[floats(*padded.shape), floats(*gradient.shape)],
        in_specs=[SCALARS] + [WHOLE] * 8,
        out_specs=[WHOLE] * 2,
        scratch_shapes=[pltpu.SMEM((count + 1,), jnp.int32)],
        input_output_aliases={1: 0, 2: 1},
        compiler_params=pltpu.CompilerParams(vmem_limit_bytes=VMEM),
        cost_estimate=cost(count, width),
        name="early",
    )(offsets, padded, gradient, re, ro, *fixed)


def late(offsets, padded, gradient, ze, zo, fixed):
    count, width = fixed[2].shape[:2]
    channels, half = ze.shape[0], ze.shape[1] - HALO
    strip, rows = floats(channels, half, LANES), floats(channels, HALO, 2 * half)
    corner = floats(channels, HALO, LANES)
    return pl.pallas_call(
        late_body,
        out_shape=[
            floats(*padded.shape), floats(*gradient.shape), strip, strip, rows, rows, corner, corner
        ],
        in_specs=[SCALARS] + [WHOLE] * 8,
        out_specs=[WHOLE] * 8,
        scratch_shapes=[pltpu.SMEM((count + 1,), jnp.int32)],
        input_output_aliases={1: 0, 2: 1},
        compiler_params=pltpu.CompilerParams(vmem_limit_bytes=VMEM),
        cost_estimate=cost(count, width),
        name="late",
    )(offsets, padded, gradient, ze, zo, *fixed)


def settle_body(gradient_in, ze, zo, re, ro, gradient, out, sems):
    tile = re.shape[2]
    tiles = tile // LANES
    half = ze.shape[1]
    row, col = here()
    even = col == 0
    outer = pl.multiple_of(HALO + row * (tile - HALO), HALO)
    inner = pl.multiple_of(HALO + (1 - row) * (tile - HALO), HALO)
    lane = low_lanes()

    def copy(k):
        return pltpu.make_async_copy(
            gradient.at[:, k + 1, pl.ds(HALO, tile), :],
            out.at[:, :, pl.ds(k * LANES, LANES)],
            sems.at[k],
        )

    for k in list(range(1, tiles - 1)) + [0, tiles - 1]:
        for ch in range(re.shape[0]):
            lanes = slice(k * LANES, (k + 1) * LANES)
            gradient[ch, k + 1, pl.ds(inner, HALO)] += re[ch, :, lanes]
            gradient[ch, k + 1, pl.ds(outer, HALO)] += ro[ch, :, lanes]
        for side in range(2):
            if k != (0, tiles - 1)[side]:
                continue
            mask = lane if side == 0 else jnp.logical_not(lane)
            for ch in range(re.shape[0]):
                strip = jnp.where(even, (zo, ze)[side][ch], (ze, zo)[side][ch])
                turned = pltpu.roll(strip, HALO, 1)
                first, second = (strip, turned) if side == 0 else (turned, strip)
                gradient[ch, k + 1, HALO : HALO + half] += jnp.where(mask, first, 0.0)
                gradient[ch, k + 1, HALO + half : HALO + tile] += jnp.where(
                    mask, second[: tile - half], 0.0
                )
        copy(k).start()
    for k in range(tiles):
        copy(k).wait()


def settle(gradient, shares, tile):
    channels = gradient.shape[0]
    return pl.pallas_call(
        settle_body,
        out_shape=[
            jax.ShapeDtypeStruct(gradient.shape, jnp.float32),
            jax.ShapeDtypeStruct((channels, tile, tile), jnp.float32),
        ],
        in_specs=[WHOLE] * 5,
        out_specs=[WHOLE, pl.BlockSpec(memory_space=pl.ANY)],
        input_output_aliases={0: 0},
        scratch_shapes=[pltpu.SemaphoreType.DMA((tile // LANES,))],
        compiler_params=pltpu.CompilerParams(vmem_limit_bytes=VMEM),
        name="settle",
    )(gradient, *shares)[1]


def swap(x, row, col):
    rows, cols = lax.axis_size("row"), lax.axis_size("col")

    def partner(i, kind):
        return i + kind * (1 - 2 * (i % 2))

    pairs = [
        (r * cols + c, partner(r, row) * cols + partner(c, col))
        for r in range(rows)
        for c in range(cols)
        if 0 <= partner(r, row) < rows and 0 <= partner(c, col) < cols
    ]
    return lax.ppermute(x, ("row", "col"), pairs)


def per_device(objects, probe, kernel, measured, offsets):
    tile = objects.shape[1]
    tables = jnp.asarray(make_tables(probe.shape[1]))
    offsets, measured = offsets[0, 0].T, measured[0, 0]
    objects, probe, kernel, measured = (
        pltpu.with_memory_space_constraint(x, pltpu.HBM) for x in (objects, probe, kernel, measured)
    )
    padded, ze, zo, re, ro, co = pack(objects)
    re, co = swap(re, 1, 0), swap(co, -1, 0)
    re, ro = lax.optimization_barrier((re, ro))
    ro = swap(ro, -1, 0)
    ze, zo = extend(ze, zo, re, co)
    ze, zo, padded = lax.optimization_barrier((ze, zo, padded))
    ze, zo = swap(ze, 0, 1), swap(zo, 0, -1)
    gradient, *fixed = prepare(padded, probe, kernel, measured, tables)
    probe, tables, spectrum, amplitudes = fixed
    fixed = (probe, spectrum, amplitudes, tables)
    padded, gradient = early(offsets, padded, gradient, re, ro, fixed)
    _, gradient, ze, zo, re, ro, ce, co = late(offsets, padded, gradient, ze, zo, fixed)
    ce, co, re, ro = swap(ce, 1, 0), swap(co, -1, 0), swap(re, 1, 0), swap(ro, -1, 0)
    ze, zo = gather(ze, zo, ce, co)
    ze, zo = swap(ze, 0, 1), swap(zo, 0, -1)
    return settle(gradient, (ze, zo, re, ro), tile)


def solution(mesh):
    return jax.shard_map(
        per_device,
        mesh=mesh,
        in_specs=(
            P(None, "row", "col"),
            P(),
            P(),
            P("row", "col", None, None, None),
            P("row", "col", None, None),
        ),
        out_specs=P(None, "row", "col"),
        check_vma=False,
    )
```

time: 89.6 us -> 79.2 us (0.88)
  local copies, waits for them, and re-layouts: 8.52 us -> 1.14 us
  waiting for transfers between devices: 26.9 us -> 30.6 us
  Pallas kernels: 27.9 us -> 24.6 us
  starting transfers between devices: 24.6 us -> 21.8 us
    unnamed x18 -> x4, local copies, waits for them, and re-layouts: 7.75 us -> 1.14 us
    ppermute x12 -> x11, waiting for transfers between devices: 26.9 us -> 30.6 us  [swap(): return lax.ppermute(x, ('row', 'col'), pairs)]
    pallas_call x5 -> x6, Pallas kernels: 25.3 us -> 22.5 us  [the longest x1 11.2 us: late(): pl.pallas_call(late_body, out_shape=[floats(*padded.shape), floats(*gradi...]
    ppermute x12 -> x11, starting transfers between devices: 24.6 us -> 21.8 us  [swap(): return lax.ppermute(x, ('row', 'col'), pairs)]
  transfers between devices with their start and end apart: 12 -> 11, of which waited for: 5 -> 8; matrix products, arithmetic and copies ran while one was open for 1% -> 0% of each run, Pallas kernels for 9% -> 11%
where the time goes in v5:
time: 79.2 us; the launch traced here: 78.5 us
  waiting for transfers between devices  30.6 us (39%)
  Pallas kernels  24.6 us (31%)
  starting transfers between devices  21.8 us (28%)
  local copies, waits for them, and re-layouts  1.14 us (1%)
    ppermute x11, waiting for transfers between devices, swap(): return lax.ppermute(x, ('row', 'col'), pairs)  30.6 us
    ppermute x11, starting transfers between devices, swap(): return lax.ppermute(x, ('row', 'col'), pairs)  21.8 us
    pallas_call x1, Pallas kernels, late(): pl.pallas_call(late_body, out_shape=[floats(*padded.shape), floats(*gradi...  11.2 us
    pallas_call x1, Pallas kernels, early(): pl.pallas_call(early_body, out_shape=[floats(*padded.shape), floats(*grad...  5.43 us
    pallas_call x1, Pallas kernels, prepare(): pl.pallas_call(prepare_body, out_shape=[floats(*padded.shape), floats(*pr...  3.22 us
    pallas_call x1, Pallas kernels, pack(): pl.pallas_call(pack_body, out_shape=(extended, strip, strip, rows, rows,...  2.4 us
    pallas_call x1, Pallas kernels, settle(): pl.pallas_call(settle_body, out_shape=[jax.ShapeDtypeStruct(gradient.shap...  2.09 us
  transfers between devices with their start and end apart: 11, of which 8 were waited for; matrix products, arithmetic and copies ran while one was open for 0% of the time, Pallas kernels for 11%

profile of v5, /device:TPU:11, one launch (start us, length us, event | category | flops | bytes accessed | tf_op | source)
XLA Modules:
  0.0 78.5 jit_solution(5134625153991009178)
XLA Ops:
  0.0 2.4 %pack.1 = (f32[4,6,648,128]{3,2,1,0:T(8,128)S(1)}, f32[4,256,128]{2,1,0:T(8,128)S(1)}, f32[4,256,128]{2,1,0:T(8,128)S(1)}, f32[4,64,512]{2,1,0:T(8,128)S(1)}, f3...) custom-call(f32[4,512,512]{2,1,0:T(8,128)} %objects.1), custom_call_target="tpu_custom_call" | custom-call | tf_op jit(solution)/shard_map/pack/pallas_call | solution.py:214
  2.4 0.7 collective-permute-start
  3.2 1.5 %collective-permute-done.re = f32[4,64,512]{2,1,0:T(8,128)S(1)} collective-permute-done((f32[4,64,512]{2,1,0:T(8,128)S(1)}, f32[4,64,512]{2,1,0:T(8,128)S(1)}, u32[]{:S(2)}, u32[]{:S(2)}) %collective-permute-start) | collective-permute-done | bytes 524320 | tf_op jit(solution)/shard_map/ppermute | solution.py:606
  4.7 3.4 %collective-permute-start.2 = (f32[4,64,512]{2,1,0:T(8,128)S(1)}, f32[4,64,512]{2,1,0:T(8,128)S(1)}, u32[]{:S(2)}, u32[]{:S(2)}) collective-permute-start(f32[4,64,512]{2,1,0:T(8,128)S(1)} %get-tuple-element.46), channel_id=1, source_target_pairs={{4,8},{5,9},{6,10},{7,11},{8,4},{9,5},{10,6},{11,7},{12,16},{13,17... | collective-permute-start | bytes 1572872 | tf_op jit(solution)/shard_map/ppermute | solution.py:606
  8.1 3.1 %collective-permute-start.1 = (f32[4,64,128]{2,1,0:T(8,128)S(1)}, f32[4,64,128]{2,1,0:T(8,128)S(1)}, u32[]{:S(2)}, u32[]{:S(2)}) collective-permute-start(f32[4,64,128]{2,1,0:T(8,128)S(1)} %get-tuple-element.40), channel_id=1, source_target_pairs={{4,8},{5,9},{6,10},{7,11},{8,4},{9,5},{10,6},{11,7},{12,16},{13,17... | collective-permute-start | bytes 393224 | tf_op jit(solution)/shard_map/ppermute | solution.py:606
  11.2 13.1 %collective-permute-done.1.co = f32[4,64,128]{2,1,0:T(8,128)S(1)} collective-permute-done((f32[4,64,128]{2,1,0:T(8,128)S(1)}, f32[4,64,128]{2,1,0:T(8,128)S(1)}, u32[]{:S(2)}, u32[]{:S(2)}) %collective-permute-start.1) | collective-permute-done | bytes 131104 | tf_op jit(solution)/shard_map/ppermute | solution.py:606
  24.3 0.1 extend.1
  24.4 0.2 collective-permute-start.3
  24.6 4.3 %collective-permute-start.4 = (f32[4,320,128]{2,1,0:T(8,128)S(1)}, f32[4,320,128]{2,1,0:T(8,128)S(1)}, u32[]{:S(2)}, u32[]{:S(2)}) collective-permute-start(f32[4,320,128]{2,1,0:T(8,128)S(1)} %get-tuple-element.54), channel_id=1, source_target_pairs={{1,2},{2,1},{5,6},{6,5},{9,10},{10,9},{13,14},{14,13},{17,18},{18,... | collective-permute-start | bytes 1966088 | tf_op jit(solution)/shard_map/ppermute | solution.py:606
  29.0 1.1 %copy-done = bf16[6,256,256]{2,1,0:T(8,128)(2,1)S(1)} copy-done((bf16[6,256,256]{2,1,0:T(8,128)(2,1)S(1)}, bf16[6,256,256]{2,1,0:T(8,128)(2,1)}, u32[]{:S(2)}) %copy-start) | copy-done | bytes 786456
  30.1 3.2 %prepare.1 = (f32[4,6,648,128]{3,2,1,0:T(8,128)S(1)}, f32[2,256,256]{2,1,0:T(8,128)S(1)}, bf16[6,256,256]{2,1,0:T(8,128)(2,1)S(1)}, f32[2,256,256]{2,1,0:T(8,128)S(1)}, f32[9,256,256]{2,1,0:T(8,128)S(1)}) custom-call(f32[4,6,648,128]{3,2,1,0:T(8,128)S(1)} %get-tuple-element.44.padded.padded_in, f32[2,256,256]{2,1,0:T(8,128)} %probe_in.1, ...), custom_call_target="tpu_custom_call" | custom-call | flops 1610612736 | bytes 524288 | tf_op jit(solution)/shard_map/prepare/pallas_call | solution.py:480
  33.3 5.4 %early.1 = (f32[4,6,648,128]{3,2,1,0:T(8,128)S(1)}, f32[4,6,648,128]{3,2,1,0:T(8,128)S(1)}) custom-call(s32[2,9]{1,0:T(2,128)S(1)} %bitcast.4, f32[4,6,648,128]{3,2,1,0:T(8,128)S(1)} %get-tuple-element.44.padded.padded_in, f32[4,6,648,128]{3,2,1,0:T(8,128)S(1)} %get-tuple-element.45.gradient_in, ...), custom_call_target="tpu_custom_call", output_to_operand_aliasing={{0}: (1, {}), {1}: (2, {})} | custom-call | flops 7247757312 | bytes 2359296 | tf_op jit(solution)/shard_map/early/pallas_call | solution.py:505
  38.8 0.4 collective-permute-done.3.ze
  39.2 2.7 %collective-permute-done.4.zo = f32[4,320,128]{2,1,0:T(8,128)S(1)} collective-permute-done((f32[4,320,128]{2,1,0:T(8,128)S(1)}, f32[4,320,128]{2,1,0:T(8,128)S(1)}, u32[]{:S(2)}, u32[]{:S(2)}) %collective-permute-start.4) | collective-permute-done | bytes 655392 | tf_op jit(solution)/shard_map/ppermute | solution.py:606
  41.9 11.2 %late.1 = (f32[4,6,648,128]{3,2,1,0:T(8,128)S(1)}, f32[4,6,648,128]{3,2,1,0:T(8,128)S(1)}, f32[4,256,128]{2,1,0:T(8,128)S(1)}, f32[4,256,128]{2,1,0:T(8,128)S(1)...) custom-call(s32[2,9]{1,0:T(2,128)S(1)} %bitcast.5, ...), custom_call_target="tpu_custom_call", output_to_operand_aliasing={{0}: (1, {}), {1}: (2, {})} | custom-call | flops 7247757312 | bytes 2359296 | tf_op jit(solution)/shard_map/late/pallas_call | solution.py:523
  53.2 3.8 %collective-permute-start.6 = (f32[4,64,128]{2,1,0:T(8,128)S(1)}, f32[4,64,128]{2,1,0:T(8,128)S(1)}, u32[]{:S(2)}, u32[]{:S(2)}) collective-permute-start(f32[4,64,128]{2,1,0:T(8,128)S(1)} %get-tuple-element.59), channel_id=1, source_target_pairs={{4,8},{5,9},{6,10},{7,11},{8,4},{9,5},{10,6},{11,7},{12,16},{13,17... | collective-permute-start | bytes 393224 | tf_op jit(solution)/shard_map/ppermute | solution.py:606
  57.1 2.7 %collective-permute-start.10 = (f32[4,64,512]{2,1,0:T(8,128)S(1)}, f32[4,64,512]{2,1,0:T(8,128)S(1)}, u32[]{:S(2)}, u32[]{:S(2)}) collective-permute-start(f32[4,64,512]{2,1,0:T(8,128)S(1)} %get-tuple-element.63), channel_id=1, source_target_pairs={{4,8},{5,9},{6,10},{7,11},{8,4},{9,5},{10,6},{11,7},{12,16},{13,17... | collective-permute-start | bytes 1572872 | tf_op jit(solution)/shard_map/ppermute | solution.py:606
  59.7 1.1 %collective-permute-done.6.co = f32[4,64,128]{2,1,0:T(8,128)S(1)} collective-permute-done((f32[4,64,128]{2,1,0:T(8,128)S(1)}, f32[4,64,128]{2,1,0:T(8,128)S(1)}, u32[]{:S(2)}, u32[]{:S(2)}) %collective-permute-start.6) | collective-permute-done | bytes 131104 | tf_op jit(solution)/shard_map/ppermute | solution.py:606
  60.8 0.1 gather.1
  61.0 3.4 %collective-permute-start.8 = (f32[4,256,128]{2,1,0:T(8,128)S(1)}, f32[4,256,128]{2,1,0:T(8,128)S(1)}, u32[]{:S(2)}, u32[]{:S(2)}) collective-permute-start(f32[4,256,128]{2,1,0:T(8,128)S(1)} %get-tuple-element.61), channel_id=1, source_target_pairs={{1,2},{2,1},{5,6},{6,5},{9,10},{10,9},{13,14},{14,13},{17,18},{18,... | collective-permute-start | bytes 1572872 | tf_op jit(solution)/shard_map/ppermute | solution.py:606
  64.4 8.5 %collective-permute-done.10.ro = f32[4,64,512]{2,1,0:T(8,128)S(1)} collective-permute-done((f32[4,64,512]{2,1,0:T(8,128)S(1)}, f32[4,64,512]{2,1,0:T(8,128)S(1)}, u32[]{:S(2)}, u32[]{:S(2)}) %collective-permute-start.10) | collective-permute-done | bytes 524320 | tf_op jit(solution)/shard_map/ppermute | solution.py:606
  73.0 1.6 %collective-permute-done.7.ze = f32[4,256,128]{2,1,0:T(8,128)S(1)} collective-permute-done((f32[4,256,128]{2,1,0:T(8,128)S(1)}, f32[4,256,128]{2,1,0:T(8,128)S(1)}, u32[]{:S(2)}, u32[]{:S(2)}) %collective-permute-start.7) | collective-permute-done | bytes 524320 | tf_op jit(solution)/shard_map/ppermute | solution.py:606
  74.6 1.7 %collective-permute-done.8.zo = f32[4,256,128]{2,1,0:T(8,128)S(1)} collective-permute-done((f32[4,256,128]{2,1,0:T(8,128)S(1)}, f32[4,256,128]{2,1,0:T(8,128)S(1)}, u32[]{:S(2)}, u32[]{:S(2)}) %collective-permute-start.8) | collective-permute-done | bytes 524320 | tf_op jit(solution)/shard_map/ppermute | solution.py:606
  76.2 2.1 %settle.1 = (f32[4,6,648,128]{3,2,1,0:T(8,128)S(1)}, f32[4,512,512]{2,1,0:T(8,128)}) custom-call(f32[4,6,648,128]{3,2,1,0:T(8,128)S(1)} %get-tuple-element.55.gradient_in, f32[4,256,128]{2,1,0:T(8,128)S(1)} %collective-permute-done.7.ze, f32[4,256,128]{2,1,0:T(8,128)S(1)} %collective-permute-done.8.zo, ...), custom_call_target="tpu_custom_call", output_to_operand_aliasing={{0}: (0, {})} | custom-call | tf_op jit(solution)/shard_map/settle/pallas_call | solution.py:579
  (9 shorter events, 0.2 us)
Async XLA Ops:
  2.4 30.9 %copy-start.1 = (s32[1,1,9,2]{2,3,1,0:T(2,128)S(1)}, s32[1,1,9,2]{2,3,1,0:T(2,128)}, u32[]{:S(2)}) copy-start(s32[1,1,9,2]{2,3,1,0:T(2,128)} %param.10) | copy-start | bytes 220
  2.4 2.3 %collective-permute-start = (f32[4,64,512]{2,1,0:T(8,128)S(1)}, f32[4,64,512]{2,1,0:T(8,128)S(1)}, u32[]{:S(2)}, u32[]{:S(2)}) collective-permute-start(f32[4,64,512]{2,1,0:T(8,128)S(1)} %get-tuple-element.37), channel_id=1, source_target_pairs={{0,4},{1,5},{2,6},{3,7},{4,0},{5,1},{6,2},{7,3},{8,12},{9,13},{10,... | collective-permute-start | bytes 1572872 | tf_op jit(solution)/shard_map/ppermute | solution.py:606
  4.7 28.6 %collective-permute-start.2 = (f32[4,64,512]{2,1,0:T(8,128)S(1)}, f32[4,64,512]{2,1,0:T(8,128)S(1)}, u32[]{:S(2)}, u32[]{:S(2)}) collective-permute-start(f32[4,64,512]{2,1,0:T(8,128)S(1)} %get-tuple-element.46), channel_id=1, source_target_pairs={{4,8},{5,9},{6,10},{7,11},{8,4},{9,5},{10,6},{11,7},{12,16},{13,17... | collective-permute-start | bytes 1572872 | tf_op jit(solution)/shard_map/ppermute | solution.py:606
  8.1 16.2 %collective-permute-start.1 = (f32[4,64,128]{2,1,0:T(8,128)S(1)}, f32[4,64,128]{2,1,0:T(8,128)S(1)}, u32[]{:S(2)}, u32[]{:S(2)}) collective-permute-start(f32[4,64,128]{2,1,0:T(8,128)S(1)} %get-tuple-element.40), channel_id=1, source_target_pairs={{4,8},{5,9},{6,10},{7,11},{8,4},{9,5},{10,6},{11,7},{12,16},{13,17... | collective-permute-start | bytes 393224 | tf_op jit(solution)/shard_map/ppermute | solution.py:606
  24.4 14.8 %collective-permute-start.3 = (f32[4,320,128]{2,1,0:T(8,128)S(1)}, f32[4,320,128]{2,1,0:T(8,128)S(1)}, u32[]{:S(2)}, u32[]{:S(2)}) collective-permute-start(f32[4,320,128]{2,1,0:T(8,128)S(1)} %get-tuple-element.53), channel_id=1, source_target_pairs={{0,1},{1,0},{2,3},{3,2},{4,5},{5,4},{6,7},{7,6},{8,9},{9,8},{10,11... | collective-permute-start | bytes 1966088 | tf_op jit(solution)/shard_map/ppermute | solution.py:606
  24.6 17.3 %collective-permute-start.4 = (f32[4,320,128]{2,1,0:T(8,128)S(1)}, f32[4,320,128]{2,1,0:T(8,128)S(1)}, u32[]{:S(2)}, u32[]{:S(2)}) collective-permute-start(f32[4,320,128]{2,1,0:T(8,128)S(1)} %get-tuple-element.54), channel_id=1, source_target_pairs={{1,2},{2,1},{5,6},{6,5},{9,10},{10,9},{13,14},{14,13},{17,18},{18,... | collective-permute-start | bytes 1966088 | tf_op jit(solution)/shard_map/ppermute | solution.py:606
  29.0 1.1 %copy-start = (bf16[6,256,256]{2,1,0:T(8,128)(2,1)S(1)}, bf16[6,256,256]{2,1,0:T(8,128)(2,1)}, u32[]{:S(2)}) copy-start(bf16[6,256,256]{2,1,0:T(8,128)(2,1)} %constant.2.clone.tables_in) | copy-start | bytes 2359300
  53.1 6.6 %collective-permute-start.5 = (f32[4,64,128]{2,1,0:T(8,128)S(1)}, f32[4,64,128]{2,1,0:T(8,128)S(1)}, u32[]{:S(2)}, u32[]{:S(2)}) collective-permute-start(f32[4,64,128]{2,1,0:T(8,128)S(1)} %get-tuple-element.58), channel_id=1, source_target_pairs={{0,4},{1,5},{2,6},{3,7},{4,0},{5,1},{6,2},{7,3},{8,12},{9,13},{10,... | collective-permute-start | bytes 393224 | tf_op jit(solution)/shard_map/ppermute | solution.py:606
  53.2 7.6 %collective-permute-start.6 = (f32[4,64,128]{2,1,0:T(8,128)S(1)}, f32[4,64,128]{2,1,0:T(8,128)S(1)}, u32[]{:S(2)}, u32[]{:S(2)}) collective-permute-start(f32[4,64,128]{2,1,0:T(8,128)S(1)} %get-tuple-element.59), channel_id=1, source_target_pairs={{4,8},{5,9},{6,10},{7,11},{8,4},{9,5},{10,6},{11,7},{12,16},{13,17... | collective-permute-start | bytes 393224 | tf_op jit(solution)/shard_map/ppermute | solution.py:606
  57.0 7.5 %collective-permute-start.9 = (f32[4,64,512]{2,1,0:T(8,128)S(1)}, f32[4,64,512]{2,1,0:T(8,128)S(1)}, u32[]{:S(2)}, u32[]{:S(2)}) collective-permute-start(f32[4,64,512]{2,1,0:T(8,128)S(1)} %get-tuple-element.62), channel_id=1, source_target_pairs={{0,4},{1,5},{2,6},{3,7},{4,0},{5,1},{6,2},{7,3},{8,12},{9,13},{10,... | collective-permute-start | bytes 1572872 | tf_op jit(solution)/shard_map/ppermute | solution.py:606
  57.1 15.9 %collective-permute-start.10 = (f32[4,64,512]{2,1,0:T(8,128)S(1)}, f32[4,64,512]{2,1,0:T(8,128)S(1)}, u32[]{:S(2)}, u32[]{:S(2)}) collective-permute-start(f32[4,64,512]{2,1,0:T(8,128)S(1)} %get-tuple-element.63), channel_id=1, source_target_pairs={{4,8},{5,9},{6,10},{7,11},{8,4},{9,5},{10,6},{11,7},{12,16},{13,17... | collective-permute-start | bytes 1572872 | tf_op jit(solution)/shard_map/ppermute | solution.py:606
  61.0 13.6 %collective-permute-start.7 = (f32[4,256,128]{2,1,0:T(8,128)S(1)}, f32[4,256,128]{2,1,0:T(8,128)S(1)}, u32[]{:S(2)}, u32[]{:S(2)}) collective-permute-start(f32[4,256,128]{2,1,0:T(8,128)S(1)} %get-tuple-element.60), channel_id=1, source_target_pairs={{0,1},{1,0},{2,3},{3,2},{4,5},{5,4},{6,7},{7,6},{8,9},{9,8},{10,11... | collective-permute-start | bytes 1572872 | tf_op jit(solution)/shard_map/ppermute | solution.py:606
  61.0 15.2 %collective-permute-start.8 = (f32[4,256,128]{2,1,0:T(8,128)S(1)}, f32[4,256,128]{2,1,0:T(8,128)S(1)}, u32[]{:S(2)}, u32[]{:S(2)}) collective-permute-start(f32[4,256,128]{2,1,0:T(8,128)S(1)} %get-tuple-element.61), channel_id=1, source_target_pairs={{1,2},{2,1},{5,6},{6,5},{9,10},{10,9},{13,14},{14,13},{17,18},{18,... | collective-permute-start | bytes 1572872 | tf_op jit(solution)/shard_map/ppermute | solution.py:606

commit v6 on v5

--- a/solution.py
+++ b/solution.py
@@ -244,19 +244,21 @@
         in_specs=[WHOLE] * 4,
         out_specs=[WHOLE] * 2,
         compiler_params=pltpu.CompilerParams(vmem_limit_bytes=SMALL),
+        cost_estimate=cost(6, 2 * LANES),
         name="extend",
     )(ze, zo, re, co)
 
 
-def gather_body(ze_in, zo_in, ce, co, ze, zo):
+def gather_body(ze_in, zo_in, re, co, ze, zo):
     row, col = here()
     below, even = row == 0, col == 0
     lane = low_lanes()
     half = ze.shape[1]
     first, last = slice(0, HALO), slice(half - HALO, half)
     for ch in range(ze.shape[0]):
-        top = jnp.where(below, co[ch], ce[ch])
-        bottom = jnp.where(below, ce[ch], co[ch])
+        ce = re[ch, :, re.shape[2] - LANES :]
+        top = jnp.where(below, co[ch], ce)
+        bottom = jnp.where(below, ce, co[ch])
         left = (jnp.where(lane, pltpu.roll(top, HALO, 1), 0.0), jnp.where(lane, 0.0, bottom))
         right = (jnp.where(lane, top, 0.0), jnp.where(lane, 0.0, pltpu.roll(bottom, HALO, 1)))
         for rows, low, high in zip((first, last), left, right):
@@ -264,7 +266,7 @@
             ze[ch, rows] += jnp.where(even, high, low)
 
 
-def gather(ze, zo, ce, co):
+def gather(ze, zo, re, co):
     strip = floats(*ze.shape)
     return pl.pallas_call(
         gather_body,
@@ -273,8 +275,9 @@
         out_specs=[WHOLE] * 2,
         input_output_aliases={0: 0, 1: 1},
         compiler_params=pltpu.CompilerParams(vmem_limit_bytes=SMALL),
+        cost_estimate=cost(6, 2 * LANES),
         name="gather",
-    )(ze, zo, ce, co)
+    )(ze, zo, re, co)
 
 
 def chain(top, left, padded, probe, spectrum, measured, tables, gradient):
@@ -323,8 +326,8 @@
             padded[ch, at, pl.ds(outer, HALO)] = second[half:]
 
 
-def harvest(gradient, ze, zo, re, ro, ce, co):
-    tile = re.shape[2]
+def harvest(gradient, ze, zo, re, ro, co):
+    tile = ro.shape[2]
     tiles = tile // LANES
     half = ze.shape[1]
     row, col = here()
@@ -332,10 +335,12 @@
     lane = low_lanes()
     outer, inner = rows_of(row, tile)
     for ch in range(re.shape[0]):
-        for out, rows in ((ce, inner), (co, outer)):
-            out[ch] = jnp.where(
+        re[ch, :, tile:], co[ch] = (
+            jnp.where(
                 lane, gradient[ch, tiles + 1, pl.ds(rows, HALO)], gradient[ch, 0, pl.ds(rows, HALO)]
             )
+            for rows in (inner, outer)
+        )
         left, right = (
             fold_pair(
                 gradient[ch, at, HALO : HALO + half],
@@ -450,9 +455,9 @@
 
 def late_body(
     offsets, padded_in, gradient_in, ze, zo, probe, spectrum, amplitudes, tables,
-    padded, gradient, gze, gzo, gre, gro, gce, gco, order,
+    padded, gradient, gze, gzo, gre, gro, gco, order,
 ):
-    tile, width = gre.shape[2], probe.shape[1]
+    tile, width = gro.shape[2], probe.shape[1]
     first = sort_positions(offsets, order, tile - width)
     assemble(padded, ze, zo, tile)
     group = group_of(offsets.shape[1])
@@ -460,7 +465,7 @@
         first // group, offsets.shape[1] // group, offsets, order,
         padded, probe, spectrum, amplitudes, tables, gradient,
     )
-    harvest(gradient, gze, gzo, gre, gro, gce, gco)
+    harvest(gradient, gze, gzo, gre, gro, gco)
 
 
 def group_of(count):
@@ -476,7 +481,6 @@
 def prepare(padded, probe, kernel, measured, tables):
     width = probe.shape[1]
     far = pl.BlockSpec(memory_space=pltpu.HBM)
-    anywhere = pl.BlockSpec(memory_space=pl.ANY)
     return pl.pallas_call(
         prepare_body,
         out_shape=[
@@ -486,7 +490,7 @@
             floats(*kernel.shape),
             floats(*measured.shape),
         ],
-        in_specs=[WHOLE] + [far] * 3 + [anywhere],
+        in_specs=[WHOLE] + [far] * 4,
         out_specs=[WHOLE] * 5,
         scratch_shapes=[
             pltpu.VMEM(kernel.shape, jnp.float32),
@@ -510,7 +514,7 @@
         scratch_shapes=[pltpu.SMEM((count + 1,), jnp.int32)],
         input_output_aliases={1: 0, 2: 1},
         compiler_params=pltpu.CompilerParams(vmem_limit_bytes=VMEM),
-        cost_estimate=cost(count, width),
+        cost_estimate=cost(3, width),
         name="early",
     )(offsets, padded, gradient, re, ro, *fixed)
 
@@ -519,14 +523,14 @@
     count, width = fixed[2].shape[:2]
     channels, half = ze.shape[0], ze.shape[1] - HALO
     strip, rows = floats(channels, half, LANES), floats(channels, HALO, 2 * half)
-    corner = floats(channels, HALO, LANES)
+    wide, corner = floats(channels, HALO, 2 * half + LANES), floats(channels, HALO, LANES)
     return pl.pallas_call(
         late_body,
         out_shape=[
-            floats(*padded.shape), floats(*gradient.shape), strip, strip, rows, rows, corner, corner
+            floats(*padded.shape), floats(*gradient.shape), strip, strip, wide, rows, corner
         ],
         in_specs=[SCALARS] + [WHOLE] * 8,
-        out_specs=[WHOLE] * 8,
+        out_specs=[WHOLE] * 7,
         scratch_shapes=[pltpu.SMEM((count + 1,), jnp.int32)],
         input_output_aliases={1: 0, 2: 1},
         compiler_params=pltpu.CompilerParams(vmem_limit_bytes=VMEM),
@@ -536,7 +540,7 @@
 
 
 def settle_body(gradient_in, ze, zo, re, ro, gradient, out, sems):
-    tile = re.shape[2]
+    tile = ro.shape[2]
     tiles = tile // LANES
     half = ze.shape[1]
     row, col = here()
@@ -613,9 +617,9 @@
     objects, probe, kernel, measured = (
         pltpu.with_memory_space_constraint(x, pltpu.HBM) for x in (objects, probe, kernel, measured)
     )
+    tables = pltpu.with_memory_space_constraint(tables, pltpu.HBM)
     padded, ze, zo, re, ro, co = pack(objects)
     re, co = swap(re, 1, 0), swap(co, -1, 0)
-    re, ro = lax.optimization_barrier((re, ro))
     ro = swap(ro, -1, 0)
     ze, zo = extend(ze, zo, re, co)
     ze, zo, padded = lax.optimization_barrier((ze, zo, padded))
@@ -624,9 +628,9 @@
     probe, tables, spectrum, amplitudes = fixed
     fixed = (probe, spectrum, amplitudes, tables)
     padded, gradient = early(offsets, padded, gradient, re, ro, fixed)
-    _, gradient, ze, zo, re, ro, ce, co = late(offsets, padded, gradient, ze, zo, fixed)
-    ce, co, re, ro = swap(ce, 1, 0), swap(co, -1, 0), swap(re, 1, 0), swap(ro, -1, 0)
-    ze, zo = gather(ze, zo, ce, co)
+    _, gradient, ze, zo, re, ro, co = late(offsets, padded, gradient, ze, zo, fixed)
+    re, co, ro = swap(re, 1, 0), swap(co, -1, 0), swap(ro, -1, 0)
+    ze, zo = gather(ze, zo, re, co)
     ze, zo = swap(ze, 0, 1), swap(zo, 0, -1)
     return settle(gradient, (ze, zo, re, ro), tile)
 

time: 79.2 us -> 66.9 us (0.84)
  waiting for transfers between devices: 30.6 us -> 19.1 us
  local copies, waits for them, and re-layouts: 1.14 us -> 0.01 us
    ppermute x11 -> x10, waiting for transfers between devices: 30.6 us -> 19.1 us  [swap(): return lax.ppermute(x, ('row', 'col'), pairs)]
    unnamed x4 -> x2, local copies, waits for them, and re-layouts: 1.14 us -> 0.01 us
    ppermute x11 -> x10, starting transfers between devices: 21.8 us -> 22 us  [swap(): return lax.ppermute(x, ('row', 'col'), pairs)]
  transfers between devices with their start and end apart: 11 -> 10, of which waited for: 8 -> 7; matrix products, arithmetic and copies ran while one was open for 0% -> 0% of each run, Pallas kernels for 11% -> 14%
where the time goes in v6:
time: 66.9 us; the launch traced here: 66.1 us
  Pallas kernels  24.7 us (37%)
  starting transfers between devices  22 us (33%)
  waiting for transfers between devices  19.1 us (29%)
    ppermute x10, starting transfers between devices, swap(): return lax.ppermute(x, ('row', 'col'), pairs)  22 us
    ppermute x10, waiting for transfers between devices, swap(): return lax.ppermute(x, ('row', 'col'), pairs)  19.1 us
    pallas_call x1, Pallas kernels, late(): pl.pallas_call(late_body, out_shape=[floats(*padded.shape), floats(*gradi...  11 us
    pallas_call x1, Pallas kernels, early(): pl.pallas_call(early_body, out_shape=[floats(*padded.shape), floats(*grad...  5.5 us
    pallas_call x1, Pallas kernels, prepare(): pl.pallas_call(prepare_body, out_shape=[floats(*padded.shape), floats(*pr...  3.41 us
    pallas_call x1, Pallas kernels, pack(): pl.pallas_call(pack_body, out_shape=(extended, strip, strip, rows, rows,...  2.38 us
    pallas_call x1, Pallas kernels, settle(): pl.pallas_call(settle_body, out_shape=[jax.ShapeDtypeStruct(gradient.shap...  2.08 us
  transfers between devices with their start and end apart: 10, of which 7 were waited for; matrix products, arithmetic and copies ran while one was open for 0% of the time, Pallas kernels for 14%

profile of v6, /device:TPU:11, one launch (start us, length us, event | category | flops | bytes accessed | tf_op | source)
XLA Modules:
  0.0 66.1 jit_solution(14207575585725041175)
XLA Ops:
  0.0 2.4 %pack.1 = (f32[4,6,648,128]{3,2,1,0:T(8,128)S(1)}, f32[4,256,128]{2,1,0:T(8,128)S(1)}, f32[4,256,128]{2,1,0:T(8,128)S(1)}, f32[4,64,512]{2,1,0:T(8,128)S(1)}, f3...) custom-call(f32[4,512,512]{2,1,0:T(8,128)} %objects.1), custom_call_target="tpu_custom_call" | custom-call | tf_op jit(solution)/shard_map/pack/pallas_call | solution.py:214
  2.4 0.7 %collective-permute-start = (f32[4,64,512]{2,1,0:T(8,128)S(1)}, f32[4,64,512]{2,1,0:T(8,128)S(1)}, u32[]{:S(2)}, u32[]{:S(2)}) collective-permute-start(f32[4,64,512]{2,1,0:T(8,128)S(1)} %get-tuple-element.34), channel_id=1, source_target_pairs={{0,4},{1,5},{2,6},{3,7},{4,0},{5,1},{6,2},{7,3},{8,12},{9,13},{10,... | collective-permute-start | bytes 1572872 | tf_op jit(solution)/shard_map/ppermute | solution.py:610
  3.1 3.0 %collective-permute-start.1 = (f32[4,64,128]{2,1,0:T(8,128)S(1)}, f32[4,64,128]{2,1,0:T(8,128)S(1)}, u32[]{:S(2)}, u32[]{:S(2)}) collective-permute-start(f32[4,64,128]{2,1,0:T(8,128)S(1)} %get-tuple-element.35), channel_id=1, source_target_pairs={{4,8},{5,9},{6,10},{7,11},{8,4},{9,5},{10,6},{11,7},{12,16},{13,17... | collective-permute-start | bytes 393224 | tf_op jit(solution)/shard_map/ppermute | solution.py:610
  6.2 3.4 %collective-permute-start.2 = (f32[4,64,512]{2,1,0:T(8,128)S(1)}, f32[4,64,512]{2,1,0:T(8,128)S(1)}, u32[]{:S(2)}, u32[]{:S(2)}) collective-permute-start(f32[4,64,512]{2,1,0:T(8,128)S(1)} %get-tuple-element.41), channel_id=1, source_target_pairs={{4,8},{5,9},{6,10},{7,11},{8,4},{9,5},{10,6},{11,7},{12,16},{13,17... | collective-permute-start | bytes 1572872 | tf_op jit(solution)/shard_map/ppermute | solution.py:610
  9.6 1.7 %collective-permute-done.1.co = f32[4,64,128]{2,1,0:T(8,128)S(1)} collective-permute-done((f32[4,64,128]{2,1,0:T(8,128)S(1)}, f32[4,64,128]{2,1,0:T(8,128)S(1)}, u32[]{:S(2)}, u32[]{:S(2)}) %collective-permute-start.1) | collective-permute-done | bytes 131104 | tf_op jit(solution)/shard_map/ppermute | solution.py:610
  11.3 0.1 extend.1
  11.5 0.2 collective-permute-start.3
  11.7 4.3 %collective-permute-start.4 = (f32[4,320,128]{2,1,0:T(8,128)S(1)}, f32[4,320,128]{2,1,0:T(8,128)S(1)}, u32[]{:S(2)}, u32[]{:S(2)}) collective-permute-start(f32[4,320,128]{2,1,0:T(8,128)S(1)} %get-tuple-element.49), channel_id=1, source_target_pairs={{1,2},{2,1},{5,6},{6,5},{9,10},{10,9},{13,14},{14,13},{17,18},{18,... | collective-permute-start | bytes 1966088 | tf_op jit(solution)/shard_map/ppermute | solution.py:610
  16.0 3.4 %prepare.1 = (f32[4,6,648,128]{3,2,1,0:T(8,128)S(1)}, f32[2,256,256]{2,1,0:T(8,128)S(1)}, bf16[6,256,256]{2,1,0:T(8,128)(2,1)S(1)}, f32[2,256,256]{2,1,0:T(8,128)S(1)}, f32[9,256,256]{2,1,0:T(8,128)S(1)}) custom-call(f32[4,6,648,128]{3,2,1,0:T(8,128)S(1)} %get-tuple-element.39.padded.padded_in, f32[2,256,256]{2,1,0:T(8,128)} %probe_in.1, ...), custom_call_target="tpu_custom_call" | custom-call | flops 1610612736 | bytes 524288 | tf_op jit(solution)/shard_map/prepare/pallas_call | solution.py:484
  19.4 2.9 %collective-permute-done.2.ro = f32[4,64,512]{2,1,0:T(8,128)S(1)} collective-permute-done((f32[4,64,512]{2,1,0:T(8,128)S(1)}, f32[4,64,512]{2,1,0:T(8,128)S(1)}, u32[]{:S(2)}, u32[]{:S(2)}) %collective-permute-start.2) | collective-permute-done | bytes 524320 | tf_op jit(solution)/shard_map/ppermute | solution.py:610
  22.3 5.5 %early.1 = (f32[4,6,648,128]{3,2,1,0:T(8,128)S(1)}, f32[4,6,648,128]{3,2,1,0:T(8,128)S(1)}) custom-call(s32[2,9]{1,0:T(2,128)S(1)} %bitcast.4, f32[4,6,648,128]{3,2,1,0:T(8,128)S(1)} %get-tuple-element.39.padded.padded_in, f32[4,6,648,128]{3,2,1,0:T(8,128)S(1)} %get-tuple-element.40.gradient_in, ...), custom_call_target="tpu_custom_call", output_to_operand_aliasing={{0}: (1, {}), {1}: (2, {})} | custom-call | flops 2415919104 | bytes 786432 | tf_op jit(solution)/shard_map/early/pallas_call | solution.py:509
  27.9 1.7 %collective-permute-done.4.zo = f32[4,320,128]{2,1,0:T(8,128)S(1)} collective-permute-done((f32[4,320,128]{2,1,0:T(8,128)S(1)}, f32[4,320,128]{2,1,0:T(8,128)S(1)}, u32[]{:S(2)}, u32[]{:S(2)}) %collective-permute-start.4) | collective-permute-done | bytes 655392 | tf_op jit(solution)/shard_map/ppermute | solution.py:610
  29.6 11.0 %late.1 = (f32[4,6,648,128]{3,2,1,0:T(8,128)S(1)}, f32[4,6,648,128]{3,2,1,0:T(8,128)S(1)}, f32[4,256,128]{2,1,0:T(8,128)S(1)}, f32[4,256,128]{2,1,0:T(8,128)S(1)...) custom-call(s32[2,9]{1,0:T(2,128)S(1)} %bitcast.5, ...), custom_call_target="tpu_custom_call", output_to_operand_aliasing={{0}: (1, {}), {1}: (2, {})} | custom-call | flops 7247757312 | bytes 2359296 | tf_op jit(solution)/shard_map/late/pallas_call | solution.py:527
  40.6 0.1 collective-permute-start.5
  40.7 3.4 %collective-permute-start.6 = (f32[4,64,128]{2,1,0:T(8,128)S(1)}, f32[4,64,128]{2,1,0:T(8,128)S(1)}, u32[]{:S(2)}, u32[]{:S(2)}) collective-permute-start(f32[4,64,128]{2,1,0:T(8,128)S(1)} %get-tuple-element.54), channel_id=1, source_target_pairs={{4,8},{5,9},{6,10},{7,11},{8,4},{9,5},{10,6},{11,7},{12,16},{13,17... | collective-permute-start | bytes 393224 | tf_op jit(solution)/shard_map/ppermute | solution.py:610
  44.2 3.0 %collective-permute-start.9 = (f32[4,64,512]{2,1,0:T(8,128)S(1)}, f32[4,64,512]{2,1,0:T(8,128)S(1)}, u32[]{:S(2)}, u32[]{:S(2)}) collective-permute-start(f32[4,64,512]{2,1,0:T(8,128)S(1)} %get-tuple-element.57), channel_id=1, source_target_pairs={{4,8},{5,9},{6,10},{7,11},{8,4},{9,5},{10,6},{11,7},{12,16},{13,17... | collective-permute-start | bytes 1572872 | tf_op jit(solution)/shard_map/ppermute | solution.py:610
  47.2 0.8 %collective-permute-done.6.co = f32[4,64,128]{2,1,0:T(8,128)S(1)} collective-permute-done((f32[4,64,128]{2,1,0:T(8,128)S(1)}, f32[4,64,128]{2,1,0:T(8,128)S(1)}, u32[]{:S(2)}, u32[]{:S(2)}) %collective-permute-start.6) | collective-permute-done | bytes 131104 | tf_op jit(solution)/shard_map/ppermute | solution.py:610
  48.0 0.1 gather.1
  48.2 0.1 collective-permute-start.7
  48.2 3.6 %collective-permute-start.8 = (f32[4,256,128]{2,1,0:T(8,128)S(1)}, f32[4,256,128]{2,1,0:T(8,128)S(1)}, u32[]{:S(2)}, u32[]{:S(2)}) collective-permute-start(f32[4,256,128]{2,1,0:T(8,128)S(1)} %get-tuple-element.56), channel_id=1, source_target_pairs={{1,2},{2,1},{5,6},{6,5},{9,10},{10,9},{13,14},{14,13},{17,18},{18,... | collective-permute-start | bytes 1572872 | tf_op jit(solution)/shard_map/ppermute | solution.py:610
  51.9 8.2 %collective-permute-done.9.ro = f32[4,64,512]{2,1,0:T(8,128)S(1)} collective-permute-done((f32[4,64,512]{2,1,0:T(8,128)S(1)}, f32[4,64,512]{2,1,0:T(8,128)S(1)}, u32[]{:S(2)}, u32[]{:S(2)}) %collective-permute-start.9) | collective-permute-done | bytes 524320 | tf_op jit(solution)/shard_map/ppermute | solution.py:610
  60.1 2.1 %collective-permute-done.7.ze = f32[4,256,128]{2,1,0:T(8,128)S(1)} collective-permute-done((f32[4,256,128]{2,1,0:T(8,128)S(1)}, f32[4,256,128]{2,1,0:T(8,128)S(1)}, u32[]{:S(2)}, u32[]{:S(2)}) %collective-permute-start.7) | collective-permute-done | bytes 524320 | tf_op jit(solution)/shard_map/ppermute | solution.py:610
  62.1 1.8 %collective-permute-done.8.zo = f32[4,256,128]{2,1,0:T(8,128)S(1)} collective-permute-done((f32[4,256,128]{2,1,0:T(8,128)S(1)}, f32[4,256,128]{2,1,0:T(8,128)S(1)}, u32[]{:S(2)}, u32[]{:S(2)}) %collective-permute-start.8) | collective-permute-done | bytes 524320 | tf_op jit(solution)/shard_map/ppermute | solution.py:610
  63.9 2.1 %settle.1 = (f32[4,6,648,128]{3,2,1,0:T(8,128)S(1)}, f32[4,512,512]{2,1,0:T(8,128)}) custom-call(f32[4,6,648,128]{3,2,1,0:T(8,128)S(1)} %get-tuple-element.50.gradient_in, f32[4,256,128]{2,1,0:T(8,128)S(1)} %collective-permute-done.7.ze, f32[4,256,128]{2,1,0:T(8,128)S(1)} %collective-permute-done.8.zo, ...), custom_call_target="tpu_custom_call", output_to_operand_aliasing={{0}: (0, {})} | custom-call | tf_op jit(solution)/shard_map/settle/pallas_call | solution.py:583
  (5 shorter events, 0.0 us)
Async XLA Ops:
  2.4 8.9 %collective-permute-start = (f32[4,64,512]{2,1,0:T(8,128)S(1)}, f32[4,64,512]{2,1,0:T(8,128)S(1)}, u32[]{:S(2)}, u32[]{:S(2)}) collective-permute-start(f32[4,64,512]{2,1,0:T(8,128)S(1)} %get-tuple-element.34), channel_id=1, source_target_pairs={{0,4},{1,5},{2,6},{3,7},{4,0},{5,1},{6,2},{7,3},{8,12},{9,13},{10,... | collective-permute-start | bytes 1572872 | tf_op jit(solution)/shard_map/ppermute | solution.py:610
  3.1 8.2 %collective-permute-start.1 = (f32[4,64,128]{2,1,0:T(8,128)S(1)}, f32[4,64,128]{2,1,0:T(8,128)S(1)}, u32[]{:S(2)}, u32[]{:S(2)}) collective-permute-start(f32[4,64,128]{2,1,0:T(8,128)S(1)} %get-tuple-element.35), channel_id=1, source_target_pairs={{4,8},{5,9},{6,10},{7,11},{8,4},{9,5},{10,6},{11,7},{12,16},{13,17... | collective-permute-start | bytes 393224 | tf_op jit(solution)/shard_map/ppermute | solution.py:610
  6.2 16.2 %collective-permute-start.2 = (f32[4,64,512]{2,1,0:T(8,128)S(1)}, f32[4,64,512]{2,1,0:T(8,128)S(1)}, u32[]{:S(2)}, u32[]{:S(2)}) collective-permute-start(f32[4,64,512]{2,1,0:T(8,128)S(1)} %get-tuple-element.41), channel_id=1, source_target_pairs={{4,8},{5,9},{6,10},{7,11},{8,4},{9,5},{10,6},{11,7},{12,16},{13,17... | collective-permute-start | bytes 1572872 | tf_op jit(solution)/shard_map/ppermute | solution.py:610
  11.4 10.9 %copy-start = (s32[1,1,9,2]{2,3,1,0:T(2,128)S(1)}, s32[1,1,9,2]{2,3,1,0:T(2,128)}, u32[]{:S(2)}) copy-start(s32[1,1,9,2]{2,3,1,0:T(2,128)} %param.10) | copy-start | bytes 220
  11.5 16.4 %collective-permute-start.3 = (f32[4,320,128]{2,1,0:T(8,128)S(1)}, f32[4,320,128]{2,1,0:T(8,128)S(1)}, u32[]{:S(2)}, u32[]{:S(2)}) collective-permute-start(f32[4,320,128]{2,1,0:T(8,128)S(1)} %get-tuple-element.48), channel_id=1, source_target_pairs={{0,1},{1,0},{2,3},{3,2},{4,5},{5,4},{6,7},{7,6},{8,9},{9,8},{10,11... | collective-permute-start | bytes 1966088 | tf_op jit(solution)/shard_map/ppermute | solution.py:610
  11.7 17.9 %collective-permute-start.4 = (f32[4,320,128]{2,1,0:T(8,128)S(1)}, f32[4,320,128]{2,1,0:T(8,128)S(1)}, u32[]{:S(2)}, u32[]{:S(2)}) collective-permute-start(f32[4,320,128]{2,1,0:T(8,128)S(1)} %get-tuple-element.49), channel_id=1, source_target_pairs={{1,2},{2,1},{5,6},{6,5},{9,10},{10,9},{13,14},{14,13},{17,18},{18,... | collective-permute-start | bytes 1966088 | tf_op jit(solution)/shard_map/ppermute | solution.py:610
  40.6 7.4 %collective-permute-start.5 = (f32[4,64,640]{2,1,0:T(8,128)S(1)}, f32[4,64,640]{2,1,0:T(8,128)S(1)}, u32[]{:S(2)}, u32[]{:S(2)}) collective-permute-start(f32[4,64,640]{2,1,0:T(8,128)S(1)} %get-tuple-element.53), channel_id=1, source_target_pairs={{0,4},{1,5},{2,6},{3,7},{4,0},{5,1},{6,2},{7,3},{8,12},{9,13},{10,... | collective-permute-start | bytes 1966088 | tf_op jit(solution)/shard_map/ppermute | solution.py:610
  40.7 7.3 %collective-permute-start.6 = (f32[4,64,128]{2,1,0:T(8,128)S(1)}, f32[4,64,128]{2,1,0:T(8,128)S(1)}, u32[]{:S(2)}, u32[]{:S(2)}) collective-permute-start(f32[4,64,128]{2,1,0:T(8,128)S(1)} %get-tuple-element.54), channel_id=1, source_target_pairs={{4,8},{5,9},{6,10},{7,11},{8,4},{9,5},{10,6},{11,7},{12,16},{13,17... | collective-permute-start | bytes 393224 | tf_op jit(solution)/shard_map/ppermute | solution.py:610
  44.2 15.9 %collective-permute-start.9 = (f32[4,64,512]{2,1,0:T(8,128)S(1)}, f32[4,64,512]{2,1,0:T(8,128)S(1)}, u32[]{:S(2)}, u32[]{:S(2)}) collective-permute-start(f32[4,64,512]{2,1,0:T(8,128)S(1)} %get-tuple-element.57), channel_id=1, source_target_pairs={{4,8},{5,9},{6,10},{7,11},{8,4},{9,5},{10,6},{11,7},{12,16},{13,17... | collective-permute-start | bytes 1572872 | tf_op jit(solution)/shard_map/ppermute | solution.py:610
  48.2 14.0 %collective-permute-start.7 = (f32[4,256,128]{2,1,0:T(8,128)S(1)}, f32[4,256,128]{2,1,0:T(8,128)S(1)}, u32[]{:S(2)}, u32[]{:S(2)}) collective-permute-start(f32[4,256,128]{2,1,0:T(8,128)S(1)} %get-tuple-element.55), channel_id=1, source_target_pairs={{0,1},{1,0},{2,3},{3,2},{4,5},{5,4},{6,7},{7,6},{8,9},{9,8},{10,11... | collective-permute-start | bytes 1572872 | tf_op jit(solution)/shard_map/ppermute | solution.py:610
  48.2 15.7 %collective-permute-start.8 = (f32[4,256,128]{2,1,0:T(8,128)S(1)}, f32[4,256,128]{2,1,0:T(8,128)S(1)}, u32[]{:S(2)}, u32[]{:S(2)}) collective-permute-start(f32[4,256,128]{2,1,0:T(8,128)S(1)} %get-tuple-element.56), channel_id=1, source_target_pairs={{1,2},{2,1},{5,6},{6,5},{9,10},{10,9},{13,14},{14,13},{17,18},{18,... | collective-permute-start | bytes 1572872 | tf_op jit(solution)/shard_map/ppermute | solution.py:610

commit v7 on v6

--- a/solution.py
+++ b/solution.py
@@ -222,31 +222,29 @@
     )(objects)
 
 
-def extend_body(ze_in, zo_in, re, co, ze, zo):
+def extend_body(re, co, ze, zo):
     even = here()[1] == 0
-    half, last = ze_in.shape[1], re.shape[2] - LANES
+    last = re.shape[2] - LANES
     lane = low_lanes()
     for ch in range(ze.shape[0]):
-        ze[ch, :half] = ze_in[ch]
-        zo[ch, :half] = zo_in[ch]
         rows = jnp.where(lane, re[ch, :, :LANES], re[ch, :, last:])
         low = jnp.where(lane, rows, pltpu.roll(co[ch], HALO, 1))
         high = jnp.where(lane, pltpu.roll(rows, HALO, 1), co[ch])
-        zo[ch, half:] = jnp.where(even, low, high)
-        ze[ch, half:] = jnp.where(even, high, low)
-
-
-def extend(ze, zo, re, co):
-    strip = floats(ze.shape[0], ze.shape[1] + HALO, LANES)
+        zo[ch] = jnp.where(even, low, high)
+        ze[ch] = jnp.where(even, high, low)
+
+
+def extend(re, co):
+    corner = floats(*co.shape)
     return pl.pallas_call(
         extend_body,
-        out_shape=(strip, strip),
-        in_specs=[WHOLE] * 4,
+        out_shape=(corner, corner),
+        in_specs=[WHOLE] * 2,
         out_specs=[WHOLE] * 2,
         compiler_params=pltpu.CompilerParams(vmem_limit_bytes=SMALL),
         cost_estimate=cost(6, 2 * LANES),
         name="extend",
-    )(ze, zo, re, co)
+    )(re, co)
 
 
 def gather_body(ze_in, zo_in, re, co, ze, zo):
@@ -310,7 +308,7 @@
     return outer, inner
 
 
-def assemble(padded, ze, zo, tile):
+def assemble(padded, ze, zo, ke, ko, tile):
     row, col = here()
     even = col == 0
     half = tile // 2
@@ -320,10 +318,13 @@
             strip = jnp.where(even, (zo, ze)[side][ch], (ze, zo)[side][ch])
             turned = pltpu.roll(strip, HALO, 1)
             first, second = (turned, strip) if side == 0 else (strip, turned)
-            padded[ch, at, HALO : HALO + half] = first[:half]
-            padded[ch, at, HALO + half : HALO + tile] = second[:half]
-            padded[ch, at, pl.ds(inner, HALO)] = first[half:]
-            padded[ch, at, pl.ds(outer, HALO)] = second[half:]
+            padded[ch, at, HALO : HALO + half] = first
+            padded[ch, at, HALO + half : HALO + tile] = second
+            corner = jnp.where(even, (ko, ke)[side][ch], (ke, ko)[side][ch])
+            turned = pltpu.roll(corner, HALO, 1)
+            near, far = (turned, corner) if side == 0 else (corner, turned)
+            padded[ch, at, pl.ds(inner, HALO)] = near
+            padded[ch, at, pl.ds(outer, HALO)] = far
 
 
 def harvest(gradient, ze, zo, re, ro, co):
@@ -454,12 +455,12 @@
 
 
 def late_body(
-    offsets, padded_in, gradient_in, ze, zo, probe, spectrum, amplitudes, tables,
+    offsets, padded_in, gradient_in, ze, zo, ke, ko, probe, spectrum, amplitudes, tables,
     padded, gradient, gze, gzo, gre, gro, gco, order,
 ):
     tile, width = gro.shape[2], probe.shape[1]
     first = sort_positions(offsets, order, tile - width)
-    assemble(padded, ze, zo, tile)
+    assemble(padded, ze, zo, ke, ko, tile)
     group = group_of(offsets.shape[1])
     run_groups(
         first // group, offsets.shape[1] // group, offsets, order,
@@ -519,9 +520,9 @@
     )(offsets, padded, gradient, re, ro, *fixed)
 
 
-def late(offsets, padded, gradient, ze, zo, fixed):
+def late(offsets, padded, gradient, sides, fixed):
     count, width = fixed[2].shape[:2]
-    channels, half = ze.shape[0], ze.shape[1] - HALO
+    channels, half = sides[0].shape[:2]
     strip, rows = floats(channels, half, LANES), floats(channels, HALO, 2 * half)
     wide, corner = floats(channels, HALO, 2 * half + LANES), floats(channels, HALO, LANES)
     return pl.pallas_call(
@@ -529,14 +530,14 @@
         out_shape=[
             floats(*padded.shape), floats(*gradient.shape), strip, strip, wide, rows, corner
         ],
-        in_specs=[SCALARS] + [WHOLE] * 8,
+        in_specs=[SCALARS] + [WHOLE] * 10,
         out_specs=[WHOLE] * 7,
         scratch_shapes=[pltpu.SMEM((count + 1,), jnp.int32)],
         input_output_aliases={1: 0, 2: 1},
         compiler_params=pltpu.CompilerParams(vmem_limit_bytes=VMEM),
         cost_estimate=cost(count, width),
         name="late",
-    )(offsets, padded, gradient, ze, zo, *fixed)
+    )(offsets, padded, gradient, *sides, *fixed)
 
 
 def settle_body(gradient_in, ze, zo, re, ro, gradient, out, sems):
@@ -619,16 +620,15 @@
     )
     tables = pltpu.with_memory_space_constraint(tables, pltpu.HBM)
     padded, ze, zo, re, ro, co = pack(objects)
-    re, co = swap(re, 1, 0), swap(co, -1, 0)
-    ro = swap(ro, -1, 0)
-    ze, zo = extend(ze, zo, re, co)
-    ze, zo, padded = lax.optimization_barrier((ze, zo, padded))
-    ze, zo = swap(ze, 0, 1), swap(zo, 0, -1)
+    ze, zo, re, co, ro = swap(ze, 0, 1), swap(zo, 0, -1), swap(re, 1, 0), swap(co, -1, 0), swap(ro, -1, 0)
+    ke, ko = extend(re, co)
+    ke, ko, padded = lax.optimization_barrier((ke, ko, padded))
+    sides = (ze, zo, swap(ke, 0, 1), swap(ko, 0, -1))
     gradient, *fixed = prepare(padded, probe, kernel, measured, tables)
     probe, tables, spectrum, amplitudes = fixed
     fixed = (probe, spectrum, amplitudes, tables)
     padded, gradient = early(offsets, padded, gradient, re, ro, fixed)
-    _, gradient, ze, zo, re, ro, co = late(offsets, padded, gradient, ze, zo, fixed)
+    _, gradient, ze, zo, re, ro, co = late(offsets, padded, gradient, sides, fixed)
     re, co, ro = swap(re, 1, 0), swap(co, -1, 0), swap(ro, -1, 0)
     ze, zo = gather(ze, zo, re, co)
     ze, zo = swap(ze, 0, 1), swap(zo, 0, -1)

time: 66.9 us -> 66.3 us (level)
  waiting for transfers between devices: 19.1 us -> 15.7 us
  starting transfers between devices: 22 us -> 24.8 us
    ppermute x10 -> x12, waiting for transfers between devices: 19.1 us -> 15.7 us  [swap(): return lax.ppermute(x, ('row', 'col'), pairs)]
    ppermute x10 -> x12, starting transfers between devices: 22 us -> 24.8 us  [swap(): return lax.ppermute(x, ('row', 'col'), pairs)]
  transfers between devices with their start and end apart: 10 -> 12, of which waited for: 7 -> 6; matrix products, arithmetic and copies ran while one was open for 0% -> 0% of each run, Pallas kernels for 14% -> 14%
where the time goes in v7:
time: 66.3 us; the launch traced here: 65.5 us
  starting transfers between devices  24.8 us (37%)
  Pallas kernels  24.7 us (37%)
  waiting for transfers between devices  15.7 us (24%)
    ppermute x12, starting transfers between devices, swap(): return lax.ppermute(x, ('row', 'col'), pairs)  24.8 us
    ppermute x12, waiting for transfers between devices, swap(): return lax.ppermute(x, ('row', 'col'), pairs)  15.7 us
    pallas_call x1, Pallas kernels, late(): pl.pallas_call(late_body, out_shape=[floats(*padded.shape), floats(*gradi...  11.1 us
    pallas_call x1, Pallas kernels, early(): pl.pallas_call(early_body, out_shape=[floats(*padded.shape), floats(*grad...  5.42 us
    pallas_call x1, Pallas kernels, prepare(): pl.pallas_call(prepare_body, out_shape=[floats(*padded.shape), floats(*pr...  3.41 us
    pallas_call x1, Pallas kernels, pack(): pl.pallas_call(pack_body, out_shape=(extended, strip, strip, rows, rows,...  2.4 us
    pallas_call x1, Pallas kernels, settle(): pl.pallas_call(settle_body, out_shape=[jax.ShapeDtypeStruct(gradient.shap...  2.08 us
  transfers between devices with their start and end apart: 12, of which 6 were waited for; matrix products, arithmetic and copies ran while one was open for 0% of the time, Pallas kernels for 14%

profile of v7, /device:TPU:11, one launch (start us, length us, event | category | flops | bytes accessed | tf_op | source)
XLA Modules:
  0.0 65.5 jit_solution(11693849478470865998)
XLA Ops:
  0.0 2.4 %pack.1 = (f32[4,6,648,128]{3,2,1,0:T(8,128)S(1)}, f32[4,256,128]{2,1,0:T(8,128)S(1)}, f32[4,256,128]{2,1,0:T(8,128)S(1)}, f32[4,64,512]{2,1,0:T(8,128)S(1)}, f3...) custom-call(f32[4,512,512]{2,1,0:T(8,128)} %objects.1), custom_call_target="tpu_custom_call" | custom-call | tf_op jit(solution)/shard_map/pack/pallas_call | solution.py:214
  2.4 0.7 %collective-permute-start = (f32[4,64,512]{2,1,0:T(8,128)S(1)}, f32[4,64,512]{2,1,0:T(8,128)S(1)}, u32[]{:S(2)}, u32[]{:S(2)}) collective-permute-start(f32[4,64,512]{2,1,0:T(8,128)S(1)} %get-tuple-element.32), channel_id=1, source_target_pairs={{0,4},{1,5},{2,6},{3,7},{4,0},{5,1},{6,2},{7,3},{8,12},{9,13},{10,... | collective-permute-start | bytes 1572872 | tf_op jit(solution)/shard_map/ppermute | solution.py:611
  3.2 3.0 %collective-permute-start.1 = (f32[4,64,128]{2,1,0:T(8,128)S(1)}, f32[4,64,128]{2,1,0:T(8,128)S(1)}, u32[]{:S(2)}, u32[]{:S(2)}) collective-permute-start(f32[4,64,128]{2,1,0:T(8,128)S(1)} %get-tuple-element.33), channel_id=1, source_target_pairs={{4,8},{5,9},{6,10},{7,11},{8,4},{9,5},{10,6},{11,7},{12,16},{13,17... | collective-permute-start | bytes 393224 | tf_op jit(solution)/shard_map/ppermute | solution.py:611
  6.2 3.4 %collective-permute-start.2 = (f32[4,64,512]{2,1,0:T(8,128)S(1)}, f32[4,64,512]{2,1,0:T(8,128)S(1)}, u32[]{:S(2)}, u32[]{:S(2)}) collective-permute-start(f32[4,64,512]{2,1,0:T(8,128)S(1)} %get-tuple-element.39), channel_id=1, source_target_pairs={{4,8},{5,9},{6,10},{7,11},{8,4},{9,5},{10,6},{11,7},{12,16},{13,17... | collective-permute-start | bytes 1572872 | tf_op jit(solution)/shard_map/ppermute | solution.py:611
  9.6 0.2 collective-permute-start.3
  9.9 4.3 %collective-permute-start.4 = (f32[4,256,128]{2,1,0:T(8,128)S(1)}, f32[4,256,128]{2,1,0:T(8,128)S(1)}, u32[]{:S(2)}, u32[]{:S(2)}) collective-permute-start(f32[4,256,128]{2,1,0:T(8,128)S(1)} %get-tuple-element.47), channel_id=1, source_target_pairs={{1,2},{2,1},{5,6},{6,5},{9,10},{10,9},{13,14},{14,13},{17,18},{18,... | collective-permute-start | bytes 1572872 | tf_op jit(solution)/shard_map/ppermute | solution.py:611
  14.2 0.1 extend.1
  14.4 1.9 %collective-permute-start.6 = (f32[4,64,128]{2,1,0:T(8,128)S(1)}, f32[4,64,128]{2,1,0:T(8,128)S(1)}, u32[]{:S(2)}, u32[]{:S(2)}) collective-permute-start(f32[4,64,128]{2,1,0:T(8,128)S(1)} %get-tuple-element.49), channel_id=1, source_target_pairs={{1,2},{2,1},{5,6},{6,5},{9,10},{10,9},{13,14},{14,13},{17,18},{18,... | collective-permute-start | bytes 393224 | tf_op jit(solution)/shard_map/ppermute | solution.py:611
  16.4 3.4 %prepare.1 = (f32[4,6,648,128]{3,2,1,0:T(8,128)S(1)}, f32[2,256,256]{2,1,0:T(8,128)S(1)}, bf16[6,256,256]{2,1,0:T(8,128)(2,1)S(1)}, f32[2,256,256]{2,1,0:T(8,128)S(1)}, f32[9,256,256]{2,1,0:T(8,128)S(1)}) custom-call(f32[4,6,648,128]{3,2,1,0:T(8,128)S(1)} %get-tuple-element.37.padded.padded_in, f32[2,256,256]{2,1,0:T(8,128)} %probe_in.1, ...), custom_call_target="tpu_custom_call" | custom-call | flops 1610612736 | bytes 524288 | tf_op jit(solution)/shard_map/prepare/pallas_call | solution.py:485
  19.8 2.6 %collective-permute-done.2.ro = f32[4,64,512]{2,1,0:T(8,128)S(1)} collective-permute-done((f32[4,64,512]{2,1,0:T(8,128)S(1)}, f32[4,64,512]{2,1,0:T(8,128)S(1)}, u32[]{:S(2)}, u32[]{:S(2)}) %collective-permute-start.2) | collective-permute-done | bytes 524320 | tf_op jit(solution)/shard_map/ppermute | solution.py:611
  22.4 5.4 %early.1 = (f32[4,6,648,128]{3,2,1,0:T(8,128)S(1)}, f32[4,6,648,128]{3,2,1,0:T(8,128)S(1)}) custom-call(s32[2,9]{1,0:T(2,128)S(1)} %bitcast.4, f32[4,6,648,128]{3,2,1,0:T(8,128)S(1)} %get-tuple-element.37.padded.padded_in, f32[4,6,648,128]{3,2,1,0:T(8,128)S(1)} %get-tuple-element.38.gradient_in, ...), custom_call_target="tpu_custom_call", output_to_operand_aliasing={{0}: (1, {}), {1}: (2, {})} | custom-call | flops 2415919104 | bytes 786432 | tf_op jit(solution)/shard_map/early/pallas_call | solution.py:510
  27.8 0.9 %collective-permute-done.6.ko = f32[4,64,128]{2,1,0:T(8,128)S(1)} collective-permute-done((f32[4,64,128]{2,1,0:T(8,128)S(1)}, f32[4,64,128]{2,1,0:T(8,128)S(1)}, u32[]{:S(2)}, u32[]{:S(2)}) %collective-permute-start.6) | collective-permute-done | bytes 131104 | tf_op jit(solution)/shard_map/ppermute | solution.py:611
  28.7 11.1 %late.1 = (f32[4,6,648,128]{3,2,1,0:T(8,128)S(1)}, f32[4,6,648,128]{3,2,1,0:T(8,128)S(1)}, f32[4,256,128]{2,1,0:T(8,128)S(1)}, f32[4,256,128]{2,1,0:T(8,128)S(1)...) custom-call(s32[2,9]{1,0:T(2,128)S(1)} %bitcast.5, ...), custom_call_target="tpu_custom_call", output_to_operand_aliasing={{0}: (1, {}), {1}: (2, {})} | custom-call | flops 7247757312 | bytes 2359296 | tf_op jit(solution)/shard_map/late/pallas_call | solution.py:528
  39.8 0.4 collective-permute-start.7
  40.2 2.7 %collective-permute-start.8 = (f32[4,64,128]{2,1,0:T(8,128)S(1)}, f32[4,64,128]{2,1,0:T(8,128)S(1)}, u32[]{:S(2)}, u32[]{:S(2)}) collective-permute-start(f32[4,64,128]{2,1,0:T(8,128)S(1)} %get-tuple-element.54), channel_id=1, source_target_pairs={{4,8},{5,9},{6,10},{7,11},{8,4},{9,5},{10,6},{11,7},{12,16},{13,17... | collective-permute-start | bytes 393224 | tf_op jit(solution)/shard_map/ppermute | solution.py:611
  42.9 3.7 %collective-permute-start.11 = (f32[4,64,512]{2,1,0:T(8,128)S(1)}, f32[4,64,512]{2,1,0:T(8,128)S(1)}, u32[]{:S(2)}, u32[]{:S(2)}) collective-permute-start(f32[4,64,512]{2,1,0:T(8,128)S(1)} %get-tuple-element.57), channel_id=1, source_target_pairs={{4,8},{5,9},{6,10},{7,11},{8,4},{9,5},{10,6},{11,7},{12,16},{13,17... | collective-permute-start | bytes 1572872 | tf_op jit(solution)/shard_map/ppermute | solution.py:611
  46.7 0.7 %collective-permute-done.8.co = f32[4,64,128]{2,1,0:T(8,128)S(1)} collective-permute-done((f32[4,64,128]{2,1,0:T(8,128)S(1)}, f32[4,64,128]{2,1,0:T(8,128)S(1)}, u32[]{:S(2)}, u32[]{:S(2)}) %collective-permute-start.8) | collective-permute-done | bytes 131104 | tf_op jit(solution)/shard_map/ppermute | solution.py:611
  47.4 0.1 gather.1
  47.5 0.1 collective-permute-start.9
  47.6 4.2 %collective-permute-start.10 = (f32[4,256,128]{2,1,0:T(8,128)S(1)}, f32[4,256,128]{2,1,0:T(8,128)S(1)}, u32[]{:S(2)}, u32[]{:S(2)}) collective-permute-start(f32[4,256,128]{2,1,0:T(8,128)S(1)} %get-tuple-element.56), channel_id=1, source_target_pairs={{1,2},{2,1},{5,6},{6,5},{9,10},{10,9},{13,14},{14,13},{17,18},{18,... | collective-permute-start | bytes 1572872 | tf_op jit(solution)/shard_map/ppermute | solution.py:611
  51.8 7.1 %collective-permute-done.11.ro = f32[4,64,512]{2,1,0:T(8,128)S(1)} collective-permute-done((f32[4,64,512]{2,1,0:T(8,128)S(1)}, f32[4,64,512]{2,1,0:T(8,128)S(1)}, u32[]{:S(2)}, u32[]{:S(2)}) %collective-permute-start.11) | collective-permute-done | bytes 524320 | tf_op jit(solution)/shard_map/ppermute | solution.py:611
  58.8 2.4 %collective-permute-done.9.ze = f32[4,256,128]{2,1,0:T(8,128)S(1)} collective-permute-done((f32[4,256,128]{2,1,0:T(8,128)S(1)}, f32[4,256,128]{2,1,0:T(8,128)S(1)}, u32[]{:S(2)}, u32[]{:S(2)}) %collective-permute-start.9) | collective-permute-done | bytes 524320 | tf_op jit(solution)/shard_map/ppermute | solution.py:611
  61.3 2.0 %collective-permute-done.10.zo = f32[4,256,128]{2,1,0:T(8,128)S(1)} collective-permute-done((f32[4,256,128]{2,1,0:T(8,128)S(1)}, f32[4,256,128]{2,1,0:T(8,128)S(1)}, u32[]{:S(2)}, u32[]{:S(2)}) %collective-permute-start.10) | collective-permute-done | bytes 524320 | tf_op jit(solution)/shard_map/ppermute | solution.py:611
  63.3 2.1 %settle.1 = (f32[4,6,648,128]{3,2,1,0:T(8,128)S(1)}, f32[4,512,512]{2,1,0:T(8,128)}) custom-call(f32[4,6,648,128]{3,2,1,0:T(8,128)S(1)} %get-tuple-element.50.gradient_in, f32[4,256,128]{2,1,0:T(8,128)S(1)} %collective-permute-done.9.ze, f32[4,256,128]{2,1,0:T(8,128)S(1)} %collective-permute-done.10.zo, ...), custom_call_target="tpu_custom_call", output_to_operand_aliasing={{0}: (0, {})} | custom-call | tf_op jit(solution)/shard_map/settle/pallas_call | solution.py:584
  (9 shorter events, 0.1 us)
Async XLA Ops:
  2.4 11.8 %collective-permute-start = (f32[4,64,512]{2,1,0:T(8,128)S(1)}, f32[4,64,512]{2,1,0:T(8,128)S(1)}, u32[]{:S(2)}, u32[]{:S(2)}) collective-permute-start(f32[4,64,512]{2,1,0:T(8,128)S(1)} %get-tuple-element.32), channel_id=1, source_target_pairs={{0,4},{1,5},{2,6},{3,7},{4,0},{5,1},{6,2},{7,3},{8,12},{9,13},{10,... | collective-permute-start | bytes 1572872 | tf_op jit(solution)/shard_map/ppermute | solution.py:611
  3.2 11.0 %collective-permute-start.1 = (f32[4,64,128]{2,1,0:T(8,128)S(1)}, f32[4,64,128]{2,1,0:T(8,128)S(1)}, u32[]{:S(2)}, u32[]{:S(2)}) collective-permute-start(f32[4,64,128]{2,1,0:T(8,128)S(1)} %get-tuple-element.33), channel_id=1, source_target_pairs={{4,8},{5,9},{6,10},{7,11},{8,4},{9,5},{10,6},{11,7},{12,16},{13,17... | collective-permute-start | bytes 393224 | tf_op jit(solution)/shard_map/ppermute | solution.py:611
  6.2 16.2 %collective-permute-start.2 = (f32[4,64,512]{2,1,0:T(8,128)S(1)}, f32[4,64,512]{2,1,0:T(8,128)S(1)}, u32[]{:S(2)}, u32[]{:S(2)}) collective-permute-start(f32[4,64,512]{2,1,0:T(8,128)S(1)} %get-tuple-element.39), channel_id=1, source_target_pairs={{4,8},{5,9},{6,10},{7,11},{8,4},{9,5},{10,6},{11,7},{12,16},{13,17... | collective-permute-start | bytes 1572872 | tf_op jit(solution)/shard_map/ppermute | solution.py:611
  9.6 18.2 %collective-permute-start.3 = (f32[4,256,128]{2,1,0:T(8,128)S(1)}, f32[4,256,128]{2,1,0:T(8,128)S(1)}, u32[]{:S(2)}, u32[]{:S(2)}) collective-permute-start(f32[4,256,128]{2,1,0:T(8,128)S(1)} %get-tuple-element.46), channel_id=1, source_target_pairs={{0,1},{1,0},{2,3},{3,2},{4,5},{5,4},{6,7},{7,6},{8,9},{9,8},{10,11... | collective-permute-start | bytes 1572872 | tf_op jit(solution)/shard_map/ppermute | solution.py:611
  9.9 18.0 %collective-permute-start.4 = (f32[4,256,128]{2,1,0:T(8,128)S(1)}, f32[4,256,128]{2,1,0:T(8,128)S(1)}, u32[]{:S(2)}, u32[]{:S(2)}) collective-permute-start(f32[4,256,128]{2,1,0:T(8,128)S(1)} %get-tuple-element.47), channel_id=1, source_target_pairs={{1,2},{2,1},{5,6},{6,5},{9,10},{10,9},{13,14},{14,13},{17,18},{18,... | collective-permute-start | bytes 1572872 | tf_op jit(solution)/shard_map/ppermute | solution.py:611
  14.3 8.0 %copy-start = (s32[1,1,9,2]{2,3,1,0:T(2,128)S(1)}, s32[1,1,9,2]{2,3,1,0:T(2,128)}, u32[]{:S(2)}) copy-start(s32[1,1,9,2]{2,3,1,0:T(2,128)} %param.10) | copy-start | bytes 220
  14.4 13.5 %collective-permute-start.5 = (f32[4,64,128]{2,1,0:T(8,128)S(1)}, f32[4,64,128]{2,1,0:T(8,128)S(1)}, u32[]{:S(2)}, u32[]{:S(2)}) collective-permute-start(f32[4,64,128]{2,1,0:T(8,128)S(1)} %get-tuple-element.48), channel_id=1, source_target_pairs={{0,1},{1,0},{2,3},{3,2},{4,5},{5,4},{6,7},{7,6},{8,9},{9,8},{10,11... | collective-permute-start | bytes 393224 | tf_op jit(solution)/shard_map/ppermute | solution.py:611
  14.4 14.3 %collective-permute-start.6 = (f32[4,64,128]{2,1,0:T(8,128)S(1)}, f32[4,64,128]{2,1,0:T(8,128)S(1)}, u32[]{:S(2)}, u32[]{:S(2)}) collective-permute-start(f32[4,64,128]{2,1,0:T(8,128)S(1)} %get-tuple-element.49), channel_id=1, source_target_pairs={{1,2},{2,1},{5,6},{6,5},{9,10},{10,9},{13,14},{14,13},{17,18},{18,... | collective-permute-start | bytes 393224 | tf_op jit(solution)/shard_map/ppermute | solution.py:611
  39.8 7.6 %collective-permute-start.7 = (f32[4,64,640]{2,1,0:T(8,128)S(1)}, f32[4,64,640]{2,1,0:T(8,128)S(1)}, u32[]{:S(2)}, u32[]{:S(2)}) collective-permute-start(f32[4,64,640]{2,1,0:T(8,128)S(1)} %get-tuple-element.53), channel_id=1, source_target_pairs={{0,4},{1,5},{2,6},{3,7},{4,0},{5,1},{6,2},{7,3},{8,12},{9,13},{10,... | collective-permute-start | bytes 1966088 | tf_op jit(solution)/shard_map/ppermute | solution.py:611
  40.2 7.2 %collective-permute-start.8 = (f32[4,64,128]{2,1,0:T(8,128)S(1)}, f32[4,64,128]{2,1,0:T(8,128)S(1)}, u32[]{:S(2)}, u32[]{:S(2)}) collective-permute-start(f32[4,64,128]{2,1,0:T(8,128)S(1)} %get-tuple-element.54), channel_id=1, source_target_pairs={{4,8},{5,9},{6,10},{7,11},{8,4},{9,5},{10,6},{11,7},{12,16},{13,17... | collective-permute-start | bytes 393224 | tf_op jit(solution)/shard_map/ppermute | solution.py:611
  42.9 15.9 %collective-permute-start.11 = (f32[4,64,512]{2,1,0:T(8,128)S(1)}, f32[4,64,512]{2,1,0:T(8,128)S(1)}, u32[]{:S(2)}, u32[]{:S(2)}) collective-permute-start(f32[4,64,512]{2,1,0:T(8,128)S(1)} %get-tuple-element.57), channel_id=1, source_target_pairs={{4,8},{5,9},{6,10},{7,11},{8,4},{9,5},{10,6},{11,7},{12,16},{13,17... | collective-permute-start | bytes 1572872 | tf_op jit(solution)/shard_map/ppermute | solution.py:611
  47.5 13.8 %collective-permute-start.9 = (f32[4,256,128]{2,1,0:T(8,128)S(1)}, f32[4,256,128]{2,1,0:T(8,128)S(1)}, u32[]{:S(2)}, u32[]{:S(2)}) collective-permute-start(f32[4,256,128]{2,1,0:T(8,128)S(1)} %get-tuple-element.55), channel_id=1, source_target_pairs={{0,1},{1,0},{2,3},{3,2},{4,5},{5,4},{6,7},{7,6},{8,9},{9,8},{10,11... | collective-permute-start | bytes 1572872 | tf_op jit(solution)/shard_map/ppermute | solution.py:611
  47.6 15.7 %collective-permute-start.10 = (f32[4,256,128]{2,1,0:T(8,128)S(1)}, f32[4,256,128]{2,1,0:T(8,128)S(1)}, u32[]{:S(2)}, u32[]{:S(2)}) collective-permute-start(f32[4,256,128]{2,1,0:T(8,128)S(1)} %get-tuple-element.56), channel_id=1, source_target_pairs={{1,2},{2,1},{5,6},{6,5},{9,10},{10,9},{13,14},{14,13},{17,18},{18,... | collective-permute-start | bytes 1572872 | tf_op jit(solution)/shard_map/ppermute | solution.py:611

commit v8 on v7

v8 whole, which is shorter than its diff:
```python
import itertools
import jax
import jax.numpy as jnp
import numpy as np
from jax import lax
from jax.experimental import pallas as pl
from jax.experimental.pallas import tpu as pltpu
from jax.sharding import PartitionSpec as P

HALO = 64
RATE = 0.5
LANES = 128
ROWS = 8
STEP = 32
GROUPS = (3, 2, 1)
VMEM = 24 * 1024 * 1024
SMALL = 12 * 1024 * 1024
LARGE = 24 * 1024 * 1024
WHOLE = pl.BlockSpec(memory_space=pltpu.VMEM)
SCALARS = pl.BlockSpec(memory_space=pltpu.SMEM)


def make_tables(width):
    half = width // 2
    index = np.arange(width)
    angle = 2.0 * np.pi / width * (index[:, None] * index[None, :] % width)
    cosine = np.cos(angle) / np.sqrt(width)
    sine = np.sin(angle) / np.sqrt(width)

    def block(parity):
        c, s = cosine[parity::2, :half], sine[parity::2, :half]
        return np.block([[c, s], [-s, c]])

    even, odd = block(0), block(1)
    order = np.zeros((width, width))
    order[index[0::2], np.arange(half)] = 1.0
    order[index[1::2], half + np.arange(half)] = 1.0
    return np.stack([even, odd, even.T, odd.T, order, RATE * order]).astype(jnp.bfloat16)


def dot(a, b):
    return jnp.dot(a, b, preferred_element_type=jnp.float32)


def steps(length):
    return range(0, length, STEP)


def rows_at(x, at):
    return x[at : at + STEP]


def narrow(*parts):
    return jnp.concatenate(parts, 1).astype(jnp.bfloat16)


def stack(parts):
    return jnp.concatenate(parts, 0)


def forward(x, half, tables):
    le, lo, re, ro = tables[0], tables[1], tables[2], tables[3]
    ur, ui, vr, vi = [], [], [], []
    for at in steps(half):
        (ar, ai), (br, bi) = x(at), x(half + at)
        for out, value in ((ur, ar + br), (ui, ai + bi), (vr, ar - br), (vi, ai - bi)):
            out.append(value.astype(jnp.bfloat16))
    e = dot(le, stack(ur + ui))
    o = dot(lo, stack(vr + vi))
    yield
    plus, minus = [], []
    for parts in (e, o):
        for at in steps(half):
            fr, fi = rows_at(parts, at), rows_at(parts, half + at)
            plus.append(narrow(fr[:, :half] + fr[:, half:], fi[:, :half] + fi[:, half:]))
            minus.append(narrow(fr[:, :half] - fr[:, half:], fi[:, :half] - fi[:, half:]))
    y = dot(stack(plus), re)
    z = dot(stack(minus), ro)
    yield

    def result(at):
        p, m = rows_at(y, at), rows_at(z, at)
        return (
            jnp.concatenate([p[:, :half], m[:, :half]], 1),
            jnp.concatenate([p[:, half:], m[:, half:]], 1),
        )

    return result


def inverse(x, half, tables):
    le, lo, re, ro = tables[2], tables[3], tables[0], tables[1]
    parities = []
    for first in (0, half):
        xr, xi = [], []
        for at in steps(half):
            r, i = x(first + at)
            xr.append(r.astype(jnp.bfloat16))
            xi.append(i.astype(jnp.bfloat16))
        parities.append(stack(xr + xi))
    e, o = dot(le, parities[0]), dot(lo, parities[1])
    yield
    low, high = [], []
    for sign in (1, -1):
        for at in steps(half):
            er, ei = rows_at(e, at), rows_at(e, half + at)
            fr, fi = rows_at(o, at), rows_at(o, half + at)
            r, i = (er + fr, ei + fi) if sign > 0 else (er - fr, ei - fi)
            low.append(narrow(r[:, :half], i[:, :half]))
            high.append(narrow(r[:, half:], i[:, half:]))
    y = dot(stack(low), re)
    z = dot(stack(high), ro)
    yield

    def result(at):
        p, m = rows_at(y, at), rows_at(z, at)
        s, d = p + m, p - m
        return (
            jnp.concatenate([s[:, :half], d[:, :half]], 1),
            jnp.concatenate([s[:, half:], d[:, half:]], 1),
        )

    return result


def reorder(x, order, stage):
    half = x.shape[0] // 2
    high = x.astype(jnp.bfloat16)
    low = (x - high.astype(jnp.float32)).astype(jnp.bfloat16)
    columns = dot(high, order) + dot(low, order)
    parts = []
    for k in range(2):
        stage[k] = columns[:, k * LANES : (k + 1) * LANES]
        parts.append(
            jnp.concatenate([stage[k, pl.ds(0, half, 2), :], stage[k, pl.ds(1, half, 2), :]], 0)
        )
    return jnp.concatenate(parts, 1)


def rolled(x, down, right):
    return pltpu.roll(pltpu.roll(x, down, 0), right, 1)


def masks(down, right):
    sub = lax.broadcasted_iota(jnp.int32, (ROWS, LANES), 0) >= down
    lane = lax.broadcasted_iota(jnp.int32, (1, LANES), 1) >= right
    return sub, lane


def window(ref, channel, row, tile, down, right, width, at):
    sub, lane = masks(down, right)
    parts = []
    for k in range(3):
        part = ref[channel, tile + k, pl.ds(row + at, STEP), :]
        if at == 0:
            after = ref[channel, tile + k, pl.ds(row + width, ROWS), :]
            part = jnp.concatenate([jnp.where(sub, part[:ROWS], after), part[ROWS:]], 0)
        parts.append(part)
    return jnp.concatenate([jnp.where(lane, parts[0], parts[2]), parts[1]], 1)


def accumulate(ref, channel, row, tile, down, right, width, at, value):
    sub, lane = masks(down, right)
    first = value[:, :LANES]
    for k, part in enumerate(
        (jnp.where(lane, first, 0.0), value[:, LANES:], jnp.where(lane, 0.0, first))
    ):
        if at == 0:
            head = part[:ROWS]
            ref[channel, tile + k, pl.ds(row, ROWS), :] += jnp.where(sub, head, 0.0)
            ref[channel, tile + k, pl.ds(row + ROWS, STEP - ROWS), :] += part[ROWS:]
            ref[channel, tile + k, pl.ds(row + width, ROWS), :] += jnp.where(sub, 0.0, head)
        else:
            ref[channel, tile + k, pl.ds(row + at, STEP), :] += part


def fold_pair(a, b, low_first):
    lane = lax.broadcasted_iota(jnp.int32, (1, LANES), 1) < HALO
    if low_first:
        return jnp.where(lane, a, pltpu.roll(b, HALO, 1))
    return jnp.where(lane, pltpu.roll(a, HALO, 1), b)


def here():
    return lax.axis_index("row") % 2, lax.axis_index("col") % 2


def low_lanes():
    return lax.broadcasted_iota(jnp.int32, (1, LANES), 1) < HALO


def pack_body(objects, padded, ze, zo, re, ro, co, sems):
    tile = objects.shape[2]
    tiles = tile // LANES
    half = ze.shape[1]
    row, col = here()
    even = col == 0
    outer = pl.multiple_of(HALO + row * (tile - HALO), HALO)
    inner = pl.multiple_of(HALO + (1 - row) * (tile - HALO), HALO)
    lane = low_lanes()
    edges = (0, tiles - 1)
    copies = [
        pltpu.make_async_copy(
            objects.at[:, :, pl.ds(k * LANES, LANES)],
            padded.at[:, k + 1, pl.ds(HALO, tile), :],
            sems.at[n],
        )
        for n, k in enumerate(edges)
    ] + [
        pltpu.make_async_copy(objects.at[:, pl.ds(rows - HALO, HALO), :], target, sems.at[2 + n])
        for n, (rows, target) in enumerate(((inner, re), (outer, ro)))
    ]
    for copy in copies:
        copy.start()
    for copy in copies[:2]:
        copy.wait()
    for ch in range(ze.shape[0]):
        low, high = (
            fold_pair(
                padded[ch, k + 1, HALO : HALO + half],
                padded[ch, k + 1, HALO + half : HALO + tile],
                k == 0,
            )
            for k in edges
        )
        zo[ch], ze[ch] = jnp.where(even, low, high), jnp.where(even, high, low)
        first, last = (padded[ch, k + 1, pl.ds(outer, HALO)] for k in edges)
        co[ch] = jnp.where(lane, first, last)
    for copy in copies[2:]:
        copy.wait()


def floats(*shape):
    return jax.ShapeDtypeStruct(shape, jnp.float32)


def pack(objects):
    channels, tile = objects.shape[:2]
    strip, rows = floats(channels, tile // 2, LANES), floats(channels, HALO, tile)
    extended = pltpu.VMEM(
        (channels, tile // LANES + 2, tile + 2 * HALO + ROWS, LANES), jnp.float32
    )
    return pl.pallas_call(
        pack_body,
        out_shape=(extended, strip, strip, rows, rows, floats(channels, HALO, LANES)),
        in_specs=[pl.BlockSpec(memory_space=pltpu.HBM)],
        out_specs=[WHOLE] * 6,
        scratch_shapes=[pltpu.SemaphoreType.DMA((4,))],
        compiler_params=pltpu.CompilerParams(vmem_limit_bytes=LARGE),
        name="pack",
    )(objects)


def extend_body(re, co, ze, zo):
    even = here()[1] == 0
    last = re.shape[2] - LANES
    lane = low_lanes()
    for ch in range(ze.shape[0]):
        rows = jnp.where(lane, re[ch, :, :LANES], re[ch, :, last:])
        low = jnp.where(lane, rows, pltpu.roll(co[ch], HALO, 1))
        high = jnp.where(lane, pltpu.roll(rows, HALO, 1), co[ch])
        zo[ch] = jnp.where(even, low, high)
        ze[ch] = jnp.where(even, high, low)


def extend(re, co):
    corner = floats(*co.shape)
    return pl.pallas_call(
        extend_body,
        out_shape=(corner, corner),
        in_specs=[WHOLE] * 2,
        out_specs=[WHOLE] * 2,
        compiler_params=pltpu.CompilerParams(vmem_limit_bytes=SMALL),
        cost_estimate=cost(1, 2 * LANES),
        name="extend",
    )(re, co)


def gather_body(ze_in, zo_in, re, co, ze, zo):
    row, col = here()
    below, even = row == 0, col == 0
    lane = low_lanes()
    half = ze.shape[1]
    first, last = slice(0, HALO), slice(half - HALO, half)
    for ch in range(ze.shape[0]):
        ce = re[ch, :, re.shape[2] - LANES :]
        top = jnp.where(below, co[ch], ce)
        bottom = jnp.where(below, ce, co[ch])
        left = (jnp.where(lane, pltpu.roll(top, HALO, 1), 0.0), jnp.where(lane, 0.0, bottom))
        right = (jnp.where(lane, top, 0.0), jnp.where(lane, 0.0, pltpu.roll(bottom, HALO, 1)))
        for rows, low, high in zip((first, last), left, right):
            zo[ch, rows] += jnp.where(even, low, high)
            ze[ch, rows] += jnp.where(even, high, low)


def gather(ze, zo, re, co):
    strip = floats(*ze.shape)
    return pl.pallas_call(
        gather_body,
        out_shape=(strip, strip),
        in_specs=[WHOLE] * 4,
        out_specs=[WHOLE] * 2,
        input_output_aliases={0: 0, 1: 1},
        compiler_params=pltpu.CompilerParams(vmem_limit_bytes=SMALL),
        cost_estimate=cost(1, 2 * LANES),
        name="gather",
    )(ze, zo, re, co)


def place_of(offsets, which):
    top = offsets[0, which] + HALO
    left = offsets[1, which] + LANES
    down, right = top % ROWS, left % LANES
    return pl.multiple_of(top - down, ROWS), left // LANES, down, right


def chain(spot, padded, probe, spectrum, measured, tables, gradient):
    width = probe.shape[1]
    half = width // 2
    held = {}

    def fixed(ref, at):
        return ref[0, pl.ds(at, STEP), :], ref[1, pl.ds(at, STEP), :]

    def windows(channel, at):
        return (window(padded, channel + part, *spot, width, at) for part in range(2))

    def illuminated(at):
        (pr, pim), (o1r, o1i) = fixed(probe, at), windows(0, at)
        return pr * o1r - pim * o1i, pr * o1i + pim * o1r

    f = yield from forward(illuminated, half, tables)

    def propagated(at):
        (kr, kim), (fr, fi) = fixed(spectrum, at), f(at)
        return kr * fr - kim * fi, kr * fi + kim * fr

    s = yield from inverse(propagated, half, tables)

    def leaving(at):
        held[at] = s(at)
        (sr, si), (o2r, o2i) = held[at], windows(2, at)
        return sr * o2r - si * o2i, sr * o2i + si * o2r

    z = yield from forward(leaving, half, tables)

    def residual(at):
        zr, zi = z(at)
        factor = measured[pl.ds(at, STEP), :] * lax.rsqrt(zr * zr + zi * zi + 1.0) - RATE
        return zr * factor, zi * factor

    g = yield from inverse(residual, half, tables)

    def back(at):
        (gr, gi), (sr, si), (o2r, o2i) = g(at), held[at], windows(2, at)
        accumulate(gradient, 2, *spot, width, at, sr * gr + si * gi)
        accumulate(gradient, 3, *spot, width, at, sr * gi - si * gr)
        return o2r * gr + o2i * gi, o2r * gi - o2i * gr

    u = yield from forward(back, half, tables)

    def returned(at):
        (kr, kim), (ur, ui) = fixed(spectrum, at), u(at)
        return kr * ur + kim * ui, kr * ui - kim * ur

    w = yield from inverse(returned, half, tables)
    for at in steps(width):
        (pr, pim), (wr, wi) = fixed(probe, at), w(at)
        accumulate(gradient, 0, *spot, width, at, pr * wr + pim * wi)
        accumulate(gradient, 1, *spot, width, at, pr * wi - pim * wr)


def rows_of(row, tile):
    outer = pl.multiple_of(row * (tile + HALO), HALO)
    inner = pl.multiple_of((1 - row) * (tile + HALO), HALO)
    return outer, inner


def write_columns(padded, ze, zo, tile):
    even = here()[1] == 0
    half = tile // 2
    for ch in range(ze.shape[0]):
        for side, at in ((0, 0), (1, padded.shape[1] - 1)):
            strip = jnp.where(even, (zo, ze)[side][ch], (ze, zo)[side][ch])
            turned = pltpu.roll(strip, HALO, 1)
            first, second = (turned, strip) if side == 0 else (strip, turned)
            padded[ch, at, HALO : HALO + half] = first
            padded[ch, at, HALO + half : HALO + tile] = second


def write_rows(padded, ke, ko, re, ro, tile):
    row, col = here()
    even = col == 0
    outer, inner = rows_of(row, tile)
    for ch in range(ke.shape[0]):
        for side, at in ((0, 0), (1, padded.shape[1] - 1)):
            corner = jnp.where(even, (ko, ke)[side][ch], (ke, ko)[side][ch])
            turned = pltpu.roll(corner, HALO, 1)
            near, far = (turned, corner) if side == 0 else (corner, turned)
            padded[ch, at, pl.ds(inner, HALO)] = near
            padded[ch, at, pl.ds(outer, HALO)] = far
        for k in range(tile // LANES):
            lanes = slice(k * LANES, (k + 1) * LANES)
            padded[ch, k + 1, pl.ds(inner, HALO)] = re[ch, :, lanes]
            padded[ch, k + 1, pl.ds(outer, HALO)] = ro[ch, :, lanes]


def harvest(gradient, ze, zo, re, ro, co):
    tile = ro.shape[2]
    tiles = tile // LANES
    half = ze.shape[1]
    row, col = here()
    even = col == 0
    lane = low_lanes()
    outer, inner = rows_of(row, tile)
    for ch in range(re.shape[0]):
        re[ch, :, tile:], co[ch] = (
            jnp.where(
                lane, gradient[ch, tiles + 1, pl.ds(rows, HALO)], gradient[ch, 0, pl.ds(rows, HALO)]
            )
            for rows in (inner, outer)
        )
        left, right = (
            fold_pair(
                gradient[ch, at, HALO : HALO + half],
                gradient[ch, at, HALO + half : HALO + tile],
                at > 0,
            )
            for at in (0, tiles + 1)
        )
        ze[ch] = jnp.where(even, right, left)
        zo[ch] = jnp.where(even, left, right)
        for k in range(tiles):
            lanes = slice(k * LANES, (k + 1) * LANES)
            re[ch, :, lanes] = gradient[ch, k + 1, pl.ds(inner, HALO)]
            ro[ch, :, lanes] = gradient[ch, k + 1, pl.ds(outer, HALO)]


def sort_positions(offsets, order, inside):
    count = offsets.shape[1]
    needs = [(offsets[0, i] >= 0) & (offsets[0, i] <= inside) for i in range(count)]
    at = jnp.int32(0)
    for i in range(count):
        order[at] = i
        at += needs[i].astype(jnp.int32)
    first = at
    for i in range(count):
        order[at] = i
        at += 1 - needs[i].astype(jnp.int32)
    return first


def run_groups(begin, end, offsets, order, padded, probes, spectrum, measured, tables, gradient):
    group = group_of(offsets.shape[1])

    def one(g, carry):
        chains = []
        for k in range(group):
            which = order[g * group + k]
            chains.append(
                chain(
                    place_of(offsets, which),
                    padded,
                    probes.at[which],
                    spectrum,
                    measured.at[which],
                    tables,
                    gradient,
                )
            )
        for _ in itertools.zip_longest(*chains):
            pass
        return carry

    lax.fori_loop(begin, end, one, 0)


def prepare_body(
    offsets, padded_in, objects, probe_in, kernel, measured, tables_in,
    padded, gradient, probes, tables, spectrum, amplitudes, probe, held, patterns, stage, sems,
):
    tile = gradient.shape[2] - 2 * HALO - ROWS
    tiles = gradient.shape[1] - 2
    loads = [
        pltpu.make_async_copy(source, target, sems.at[n])
        for n, (source, target) in enumerate(
            ((tables_in, tables), (kernel, held), (probe_in, probe), (measured, patterns))
        )
    ]
    rows = pl.ds(HALO, tile)
    copies = [
        pltpu.make_async_copy(
            padded.at[:, k + 1, rows, :], gradient.at[:, k + 1, rows, :], sems.at[len(loads) + k]
        )
        for k in (0, tiles - 1)
    ] + [
        pltpu.make_async_copy(
            objects.at[:, :, pl.ds(k * LANES, LANES)],
            target.at[:, k + 1, rows, :],
            sems.at[len(loads) + k + n * tiles],
        )
        for n, target in enumerate((gradient, padded))
        for k in range(1, tiles - 1)
    ]
    for copy in loads + copies:
        copy.start()
    bottom = gradient.shape[2] - HALO - tile
    for ch in range(gradient.shape[0]):
        for at in (0, tiles + 1):
            gradient[ch, at] = jnp.zeros(gradient.shape[2:], jnp.float32)
        for k in range(tiles):
            gradient[ch, k + 1, :HALO] = jnp.zeros((HALO, LANES), jnp.float32)
            gradient[ch, k + 1, HALO + tile :] = jnp.zeros((bottom, LANES), jnp.float32)
    for copy in loads:
        copy.wait()
    for part in range(2):
        spectrum[part] = reorder(held[part], tables[4], stage.at[part])
    for which in range(patterns.shape[0]):
        amplitudes[which] = reorder(patterns[which], tables[5], stage.at[which % 2])
        _, _, down, right = place_of(offsets, which)
        for part in range(2):
            probes[which, part] = rolled(probe[part], down, right)
    for copy in copies:
        copy.wait()


def early_body(
    offsets, padded_in, gradient_in, ze, zo, probes, spectrum, amplitudes, tables,
    padded, gradient, order,
):
    tile, width = 2 * ze.shape[1], probes.shape[2]
    first = sort_positions(offsets, order, tile - width)
    write_columns(padded, ze, zo, tile)
    run_groups(
        0, first // group_of(offsets.shape[1]), offsets, order,
        padded, probes, spectrum, amplitudes, tables, gradient,
    )


def late_body(
    offsets, padded_in, gradient_in, ke, ko, re, ro, probes, spectrum, amplitudes, tables,
    padded, gradient, gze, gzo, gre, gro, gco, order,
):
    tile, width = ro.shape[2], probes.shape[2]
    first = sort_positions(offsets, order, tile - width)
    write_rows(padded, ke, ko, re, ro, tile)
    group = group_of(offsets.shape[1])
    run_groups(
        first // group, offsets.shape[1] // group, offsets, order,
        padded, probes, spectrum, amplitudes, tables, gradient,
    )
    harvest(gradient, gze, gzo, gre, gro, gco)


def group_of(count):
    return next(k for k in GROUPS if count % k == 0)


def cost(positions, width):
    return pl.CostEstimate(
        flops=positions * 6 * 8 * width**3, bytes_accessed=positions * 4 * width * width, transcendentals=0
    )


def prepare(offsets, padded, objects, probe, kernel, measured, tables):
    width = probe.shape[1]
    far = pl.BlockSpec(memory_space=pltpu.HBM)
    return pl.pallas_call(
        prepare_body,
        out_shape=[
            floats(*padded.shape),
            floats(*padded.shape),
            floats(measured.shape[0], *probe.shape),
            jax.ShapeDtypeStruct(tables.shape, tables.dtype),
            floats(*kernel.shape),
            floats(*measured.shape),
        ],
        in_specs=[SCALARS, WHOLE] + [far] * 5,
        out_specs=[WHOLE] * 6,
        input_output_aliases={1: 0},
        scratch_shapes=[
            pltpu.VMEM(probe.shape, jnp.float32),
            pltpu.VMEM(kernel.shape, jnp.float32),
            pltpu.VMEM(measured.shape, jnp.float32),
            pltpu.VMEM((2, 2, width, LANES), jnp.float32),
            pltpu.SemaphoreType.DMA((4 + 2 * (padded.shape[1] - 2),)),
        ],
        compiler_params=pltpu.CompilerParams(vmem_limit_bytes=VMEM),
        cost_estimate=cost(2, width),
        name="prepare",
    )(offsets, padded, objects, probe, kernel, measured, tables)


def early(offsets, padded, gradient, ze, zo, fixed):
    count, width = fixed[2].shape[:2]
    return pl.pallas_call(
        early_body,
        out_shape=[floats(*padded.shape), floats(*gradient.shape)],
        in_specs=[SCALARS] + [WHOLE] * 8,
        out_specs=[WHOLE] * 2,
        scratch_shapes=[pltpu.SMEM((count + 1,), jnp.int32)],
        input_output_aliases={1: 0, 2: 1},
        compiler_params=pltpu.CompilerParams(vmem_limit_bytes=VMEM),
        cost_estimate=cost(3, width),
        name="early",
    )(offsets, padded, gradient, ze, zo, *fixed)


def late(offsets, padded, gradient, sides, fixed):
    count, width = fixed[2].shape[:2]
    channels, half = sides[2].shape[0], sides[2].shape[2] // 2
    strip, rows = floats(channels, half, LANES), floats(channels, HALO, 2 * half)
    wide, corner = floats(channels, HALO, 2 * half + LANES), floats(channels, HALO, LANES)
    return pl.pallas_call(
        late_body,
        out_shape=[
            floats(*padded.shape), floats(*gradient.shape), strip, strip, wide, rows, corner
        ],
        in_specs=[SCALARS] + [WHOLE] * 10,
        out_specs=[WHOLE] * 7,
        scratch_shapes=[pltpu.SMEM((count + 1,), jnp.int32)],
        input_output_aliases={1: 0, 2: 1},
        compiler_params=pltpu.CompilerParams(vmem_limit_bytes=VMEM),
        cost_estimate=cost(count, width),
        name="late",
    )(offsets, padded, gradient, *sides, *fixed)


def tile_copy(gradient, out, sems, k):
    tile = out.shape[2]
    return pltpu.make_async_copy(
        gradient.at[:, k + 1, pl.ds(HALO, tile), :],
        out.at[:, :, pl.ds(k * LANES, LANES)],
        sems.at[k],
    )


def inside_body(gradient_in, re, ro, gradient, out, sems):
    tile = ro.shape[2]
    row = here()[0]
    outer = pl.multiple_of(HALO + row * (tile - HALO), HALO)
    inner = pl.multiple_of(HALO + (1 - row) * (tile - HALO), HALO)
    tiles = tile // LANES
    for k in [*range(1, tiles - 1), 0, tiles - 1]:
        lanes = slice(k * LANES, (k + 1) * LANES)
        for ch in range(ro.shape[0]):
            gradient[ch, k + 1, pl.ds(inner, HALO)] += re[ch, :, lanes]
            gradient[ch, k + 1, pl.ds(outer, HALO)] += ro[ch, :, lanes]
        if 0 < k < tiles - 1:
            tile_copy(gradient, out, sems, k).start()
    for k in range(1, tiles - 1):
        tile_copy(gradient, out, sems, k).wait()


def border_body(gradient_in, out_in, ze, zo, gradient, out, sems):
    tile = out.shape[2]
    tiles = tile // LANES
    half = ze.shape[1]
    even = here()[1] == 0
    lane = low_lanes()
    for side, k in enumerate((0, tiles - 1)):
        mask = lane if side == 0 else jnp.logical_not(lane)
        for ch in range(ze.shape[0]):
            strip = jnp.where(even, (zo, ze)[side][ch], (ze, zo)[side][ch])
            turned = pltpu.roll(strip, HALO, 1)
            first, second = (strip, turned) if side == 0 else (turned, strip)
            gradient[ch, k + 1, HALO : HALO + half] += jnp.where(mask, first, 0.0)
            gradient[ch, k + 1, HALO + half : HALO + tile] += jnp.where(mask, second, 0.0)
        tile_copy(gradient, out, sems, k).start()
    for k in (0, tiles - 1):
        tile_copy(gradient, out, sems, k).wait()


def settle(gradient, ze, zo, re, ro, tile):
    channels = gradient.shape[0]
    far = pl.BlockSpec(memory_space=pltpu.HBM)
    shapes = [floats(*gradient.shape), floats(channels, tile, tile)]
    common = dict(
        out_shape=shapes,
        out_specs=[WHOLE, far],
        scratch_shapes=[pltpu.SemaphoreType.DMA((tile // LANES,))],
        compiler_params=pltpu.CompilerParams(vmem_limit_bytes=VMEM),
    )
    gradient, out = pl.pallas_call(
        inside_body,
        in_specs=[WHOLE] * 3,
        input_output_aliases={0: 0},
        name="inside",
        **common,
    )(gradient, re, ro)
    return pl.pallas_call(
        border_body,
        in_specs=[WHOLE, far, WHOLE, WHOLE],
        input_output_aliases={0: 0, 1: 1},
        name="border",
        **common,
    )(gradient, out, ze, zo)[1]


def swap(x, row, col):
    rows, cols = lax.axis_size("row"), lax.axis_size("col")

    def partner(i, kind):
        return i + kind * (1 - 2 * (i % 2))

    pairs = [
        (r * cols + c, partner(r, row) * cols + partner(c, col))
        for r in range(rows)
        for c in range(cols)
        if 0 <= partner(r, row) < rows and 0 <= partner(c, col) < cols
    ]
    return lax.ppermute(x, ("row", "col"), pairs)


def per_device(objects, probe, kernel, measured, offsets):
    tile = objects.shape[1]
    tables = jnp.asarray(make_tables(probe.shape[1]))
    offsets, measured = offsets[0, 0].T, measured[0, 0]
    objects, probe, kernel, measured = (
        pltpu.with_memory_space_constraint(x, pltpu.HBM) for x in (objects, probe, kernel, measured)
    )
    tables = pltpu.with_memory_space_constraint(tables, pltpu.HBM)
    padded, ze, zo, re, ro, co = pack(objects)
    ze, zo, re, co, ro = swap(ze, 0, 1), swap(zo, 0, -1), swap(re, 1, 0), swap(co, -1, 0), swap(ro, -1, 0)
    ke, ko = extend(re, co)
    ke, ko, padded = lax.optimization_barrier((ke, ko, padded))
    sides = (swap(ke, 0, 1), swap(ko, 0, -1), re, ro)
    padded, gradient, *fixed = prepare(offsets, padded, objects, probe, kernel, measured, tables)
    probe, tables, spectrum, amplitudes = fixed
    fixed = (probe, spectrum, amplitudes, tables)
    padded, gradient = early(offsets, padded, gradient, ze, zo, fixed)
    _, gradient, ze, zo, re, ro, co = late(offsets, padded, gradient, sides, fixed)
    re, co, ro = swap(re, 1, 0), swap(co, -1, 0), swap(ro, -1, 0)
    ze, zo = gather(ze, zo, re, co)
    ze, zo = swap(ze, 0, 1), swap(zo, 0, -1)
    return settle(gradient, ze, zo, re, ro, tile)


def solution(mesh):
    return jax.shard_map(
        per_device,
        mesh=mesh,
        in_specs=(
            P(None, "row", "col"),
            P(),
            P(),
            P("row", "col", None, None, None),
            P("row", "col", None, None),
        ),
        out_specs=P(None, "row", "col"),
        check_vma=False,
    )
```

time: 66.3 us -> 65 us (0.980)
  waiting for transfers between devices: 15.7 us -> 13.9 us
  Pallas kernels: 24.7 us -> 26 us
  starting transfers between devices: 24.8 us -> 23.8 us
    pallas_call x2 -> x3, Pallas kernels: 5.5 us -> 8.25 us  [the longest x1 5.27 us: prepare(): pl.pallas_call(prepare_body, out_shape=[floats(*padded.shape), floats(*pa...]
    ppermute x12, waiting for transfers between devices: 15.7 us -> 13.9 us  [swap(): return lax.ppermute(x, ('row', 'col'), pairs)]
    ppermute x12, starting transfers between devices: 24.8 us -> 23.8 us  [swap(): return lax.ppermute(x, ('row', 'col'), pairs)]
    pallas_call x1, Pallas kernels: 11.1 us -> 10.1 us  [late(): pl.pallas_call(late_body, out_shape=[floats(*padded.shape), floats(*gradi...]
    unnamed x2, local copies, waits for them, and re-layouts: 0.01 us -> 0.67 us
  transfers between devices with their start and end apart: 12 -> 12, of which waited for: 6 -> 5; matrix products, arithmetic and copies ran while one was open for 0% -> 0% of each run, Pallas kernels for 14% -> 19%
where the time goes in v8:
time: 65 us; the launch traced here: 64.8 us
  Pallas kernels  26 us (40%)
  starting transfers between devices  23.8 us (37%)
  waiting for transfers between devices  13.9 us (21%)
  local copies, waits for them, and re-layouts  0.67 us (1%)
    ppermute x12, starting transfers between devices, swap(): return lax.ppermute(x, ('row', 'col'), pairs)  23.8 us
    ppermute x12, waiting for transfers between devices, swap(): return lax.ppermute(x, ('row', 'col'), pairs)  13.9 us
    pallas_call x1, Pallas kernels, late(): pl.pallas_call(late_body, out_shape=[floats(*padded.shape), floats(*gradi...  10.1 us
    pallas_call x1, Pallas kernels, early(): pl.pallas_call(early_body, out_shape=[floats(*padded.shape), floats(*grad...  5.36 us
    pallas_call x1, Pallas kernels, prepare(): pl.pallas_call(prepare_body, out_shape=[floats(*padded.shape), floats(*pa...  5.27 us
    pallas_call x1, Pallas kernels, pack(): pl.pallas_call(pack_body, out_shape=(extended, strip, strip, rows, rows,...  1.98 us
    pallas_call x1, Pallas kernels, settle(): pl.pallas_call(border_body, in_specs=[WHOLE, far, WHOLE, WHOLE], input_ou...  1.59 us
    pallas_call x1, Pallas kernels, settle(): pl.pallas_call(inside_body, in_specs=[WHOLE] * 3, input_output_aliases={0...  1.39 us
  transfers between devices with their start and end apart: 12, of which 5 were waited for; matrix products, arithmetic and copies ran while one was open for 0% of the time, Pallas kernels for 19%

profile of v8, /device:TPU:11, one launch (start us, length us, event | category | flops | bytes accessed | tf_op | source)
XLA Modules:
  0.0 64.8 jit_solution(18208218068053088124)
XLA Ops:
  0.0 2.0 %pack.1 = (f32[4,6,648,128]{3,2,1,0:T(8,128)S(1)}, f32[4,256,128]{2,1,0:T(8,128)S(1)}, f32[4,256,128]{2,1,0:T(8,128)S(1)}, f32[4,64,512]{2,1,0:T(8,128)S(1)}, f3...) custom-call(f32[4,512,512]{2,1,0:T(8,128)} %objects.3), custom_call_target="tpu_custom_call" | custom-call | tf_op jit(solution)/shard_map/pack/pallas_call | solution.py:243
  2.0 0.7 %collective-permute-start = (f32[4,64,512]{2,1,0:T(8,128)S(1)}, f32[4,64,512]{2,1,0:T(8,128)S(1)}, u32[]{:S(2)}, u32[]{:S(2)}) collective-permute-start(f32[4,64,512]{2,1,0:T(8,128)S(1)} %get-tuple-element.35), channel_id=1, source_target_pairs={{0,4},{1,5},{2,6},{3,7},{4,0},{5,1},{6,2},{7,3},{8,12},{9,13},{10,... | collective-permute-start | bytes 1572872 | tf_op jit(solution)/shard_map/ppermute | solution.py:712
  2.7 0.2 collective-permute-start.2
  2.9 4.3 %collective-permute-start.3 = (f32[4,256,128]{2,1,0:T(8,128)S(1)}, f32[4,256,128]{2,1,0:T(8,128)S(1)}, u32[]{:S(2)}, u32[]{:S(2)}) collective-permute-start(f32[4,256,128]{2,1,0:T(8,128)S(1)} %get-tuple-element.44), channel_id=1, source_target_pairs={{1,2},{2,1},{5,6},{6,5},{9,10},{10,9},{13,14},{14,13},{17,18},{18,... | collective-permute-start | bytes 1572872 | tf_op jit(solution)/shard_map/ppermute | solution.py:712
  7.2 3.6 %collective-permute-start.1 = (f32[4,64,128]{2,1,0:T(8,128)S(1)}, f32[4,64,128]{2,1,0:T(8,128)S(1)}, u32[]{:S(2)}, u32[]{:S(2)}) collective-permute-start(f32[4,64,128]{2,1,0:T(8,128)S(1)} %get-tuple-element.36), channel_id=1, source_target_pairs={{4,8},{5,9},{6,10},{7,11},{8,4},{9,5},{10,6},{11,7},{12,16},{13,17... | collective-permute-start | bytes 393224 | tf_op jit(solution)/shard_map/ppermute | solution.py:712
  10.9 2.8 %collective-permute-start.6 = (f32[4,64,512]{2,1,0:T(8,128)S(1)}, f32[4,64,512]{2,1,0:T(8,128)S(1)}, u32[]{:S(2)}, u32[]{:S(2)}) collective-permute-start(f32[4,64,512]{2,1,0:T(8,128)S(1)} %get-tuple-element.53), channel_id=1, source_target_pairs={{4,8},{5,9},{6,10},{7,11},{8,4},{9,5},{10,6},{11,7},{12,16},{13,17... | collective-permute-start | bytes 1572872 | tf_op jit(solution)/shard_map/ppermute | solution.py:712
  13.7 2.1 %collective-permute-done.1.co = f32[4,64,128]{2,1,0:T(8,128)S(1)} collective-permute-done((f32[4,64,128]{2,1,0:T(8,128)S(1)}, f32[4,64,128]{2,1,0:T(8,128)S(1)}, u32[]{:S(2)}, u32[]{:S(2)}) %collective-permute-start.1) | collective-permute-done | bytes 131104 | tf_op jit(solution)/shard_map/ppermute | solution.py:712
  15.8 0.1 extend.1
  16.1 1.9 %collective-permute-start.5 = (f32[4,64,128]{2,1,0:T(8,128)S(1)}, f32[4,64,128]{2,1,0:T(8,128)S(1)}, u32[]{:S(2)}, u32[]{:S(2)}) collective-permute-start(f32[4,64,128]{2,1,0:T(8,128)S(1)} %get-tuple-element.52), channel_id=1, source_target_pairs={{1,2},{2,1},{5,6},{6,5},{9,10},{10,9},{13,14},{14,13},{17,18},{18,... | collective-permute-start | bytes 393224 | tf_op jit(solution)/shard_map/ppermute | solution.py:712
  18.0 0.7 %copy-done = s32[1,1,9,2]{2,3,1,0:T(2,128)S(1)} copy-done((s32[1,1,9,2]{2,3,1,0:T(2,128)S(1)}, s32[1,1,9,2]{2,3,1,0:T(2,128)}, u32[]{:S(2)}) %copy-start) | copy-done | bytes 96
  18.7 5.3 %prepare.1 = (f32[4,6,648,128]{3,2,1,0:T(8,128)S(1)}, f32[4,6,648,128]{3,2,1,0:T(8,128)S(1)}, f32[9,2,256,256]{3,2,1,0:T(8,128)S(1)}, bf16[6,256,256]{2,1,0:T(8,...) custom-call(s32[2,9]{1,0:T(2,128)S(1)} %bitcast.4, ...), custom_call_target="tpu_custom_call", output_to_operand_aliasing={{0}: (1, {})} | custom-call | flops 1610612736 | bytes 524288 | tf_op jit(solution)/shard_map/prepare/pallas_call | solution.py:568
  24.0 5.4 %early.1 = (f32[4,6,648,128]{3,2,1,0:T(8,128)S(1)}, f32[4,6,648,128]{3,2,1,0:T(8,128)S(1)}) custom-call(s32[2,9]{1,0:T(2,128)S(1)} %bitcast.5, f32[4,6,648,128]{3,2,1,0:T(8,128)S(1)} %get-tuple-element.41.padded_in, f32[4,6,648,128]{3,2,1,0:T(8,128)S(1)} %get-tuple-element.42.gradient_in, ...), custom_call_target="tpu_custom_call", output_to_operand_aliasing={{0}: (1, {}), {1}: (2, {})} | custom-call | flops 2415919104 | bytes 786432 | tf_op jit(solution)/shard_map/early/pallas_call | solution.py:596
  29.4 10.1 %late.1 = (f32[4,6,648,128]{3,2,1,0:T(8,128)S(1)}, f32[4,6,648,128]{3,2,1,0:T(8,128)S(1)}, f32[4,256,128]{2,1,0:T(8,128)S(1)}, f32[4,256,128]{2,1,0:T(8,128)S(1)...) custom-call(s32[2,9]{1,0:T(2,128)S(1)} %bitcast.6, ...), custom_call_target="tpu_custom_call", output_to_operand_aliasing={{0}: (1, {}), {1}: (2, {})} | custom-call | flops 7247757312 | bytes 2359296 | tf_op jit(solution)/shard_map/late/pallas_call | solution.py:614
  39.6 3.0 %collective-permute-start.9 = (f32[4,64,128]{2,1,0:T(8,128)S(1)}, f32[4,64,128]{2,1,0:T(8,128)S(1)}, u32[]{:S(2)}, u32[]{:S(2)}) collective-permute-start(f32[4,64,128]{2,1,0:T(8,128)S(1)} %get-tuple-element.61), channel_id=1, source_target_pairs={{4,8},{5,9},{6,10},{7,11},{8,4},{9,5},{10,6},{11,7},{12,16},{13,17... | collective-permute-start | bytes 393224 | tf_op jit(solution)/shard_map/ppermute | solution.py:712
  42.6 3.5 %collective-permute-start.8 = (f32[4,64,512]{2,1,0:T(8,128)S(1)}, f32[4,64,512]{2,1,0:T(8,128)S(1)}, u32[]{:S(2)}, u32[]{:S(2)}) collective-permute-start(f32[4,64,512]{2,1,0:T(8,128)S(1)} %get-tuple-element.56), channel_id=1, source_target_pairs={{4,8},{5,9},{6,10},{7,11},{8,4},{9,5},{10,6},{11,7},{12,16},{13,17... | collective-permute-start | bytes 1572872 | tf_op jit(solution)/shard_map/ppermute | solution.py:712
  46.1 1.3 %collective-permute-done.9.co = f32[4,64,128]{2,1,0:T(8,128)S(1)} collective-permute-done((f32[4,64,128]{2,1,0:T(8,128)S(1)}, f32[4,64,128]{2,1,0:T(8,128)S(1)}, u32[]{:S(2)}, u32[]{:S(2)}) %collective-permute-start.9) | collective-permute-done | bytes 131104 | tf_op jit(solution)/shard_map/ppermute | solution.py:712
  47.3 0.2 gather.1
  47.5 0.8 %collective-permute-start.10 = (f32[4,256,128]{2,1,0:T(8,128)S(1)}, f32[4,256,128]{2,1,0:T(8,128)S(1)}, u32[]{:S(2)}, u32[]{:S(2)}) collective-permute-start(f32[4,256,128]{2,1,0:T(8,128)S(1)} %get-tuple-element.62), channel_id=1, source_target_pairs={{0,1},{1,0},{2,3},{3,2},{4,5},{5,4},{6,7},{7,6},{8,9},{9,8},{10,11... | collective-permute-start | bytes 1572872 | tf_op jit(solution)/shard_map/ppermute | solution.py:712
  48.3 2.8 %collective-permute-start.11 = (f32[4,256,128]{2,1,0:T(8,128)S(1)}, f32[4,256,128]{2,1,0:T(8,128)S(1)}, u32[]{:S(2)}, u32[]{:S(2)}) collective-permute-start(f32[4,256,128]{2,1,0:T(8,128)S(1)} %get-tuple-element.63), channel_id=1, source_target_pairs={{1,2},{2,1},{5,6},{6,5},{9,10},{10,9},{13,14},{14,13},{17,18},{18,... | collective-permute-start | bytes 1572872 | tf_op jit(solution)/shard_map/ppermute | solution.py:712
  51.1 7.5 %collective-permute-done.8.ro = f32[4,64,512]{2,1,0:T(8,128)S(1)} collective-permute-done((f32[4,64,512]{2,1,0:T(8,128)S(1)}, f32[4,64,512]{2,1,0:T(8,128)S(1)}, u32[]{:S(2)}, u32[]{:S(2)}) %collective-permute-start.8) | collective-permute-done | bytes 524320 | tf_op jit(solution)/shard_map/ppermute | solution.py:712
  58.6 1.4 %inside.1 = (f32[4,6,648,128]{3,2,1,0:T(8,128)S(1)}, f32[4,512,512]{2,1,0:T(8,128)}) custom-call(f32[4,6,648,128]{3,2,1,0:T(8,128)S(1)} %get-tuple-element.54.gradient_in, f32[4,64,640]{2,1,0:T(8,128)S(1)} %collective-permute-done.7.re, f32[4,64,512]{2,1,0:T(8,128)S(1)} %collective-permute-done.8.ro), custom_call_target="tpu_custom_call", output_to_operand_aliasing={{0}: (0, {})} | custom-call | tf_op jit(solution)/shard_map/inside/pallas_call | solution.py:684
  60.0 1.0 %collective-permute-done.10.ze = f32[4,256,128]{2,1,0:T(8,128)S(1)} collective-permute-done((f32[4,256,128]{2,1,0:T(8,128)S(1)}, f32[4,256,128]{2,1,0:T(8,128)S(1)}, u32[]{:S(2)}, u32[]{:S(2)}) %collective-permute-start.10) | collective-permute-done | bytes 524320 | tf_op jit(solution)/shard_map/ppermute | solution.py:712
  61.0 2.0 %collective-permute-done.11.zo = f32[4,256,128]{2,1,0:T(8,128)S(1)} collective-permute-done((f32[4,256,128]{2,1,0:T(8,128)S(1)}, f32[4,256,128]{2,1,0:T(8,128)S(1)}, u32[]{:S(2)}, u32[]{:S(2)}) %collective-permute-start.11) | collective-permute-done | bytes 524320 | tf_op jit(solution)/shard_map/ppermute | solution.py:712
  63.0 1.6 %border.1 = (f32[4,6,648,128]{3,2,1,0:T(8,128)S(1)}, f32[4,512,512]{2,1,0:T(8,128)}) custom-call(f32[4,6,648,128]{3,2,1,0:T(8,128)S(1)} %get-tuple-element.57.gradient_in, f32[4,512,512]{2,1,0:T(8,128)} %get-tuple-element.58.out_in, f32[4,256,128]{2,1,0:T(8,128)S(1)} %collective-permute-done.10.ze, ...), custom_call_target="tpu_custom_call", output_to_operand_aliasing={{0}: (0, {}), {1}: (1, {})} | custom-call | tf_op jit(solution)/shard_map/border/pallas_call | solution.py:691
  (10 shorter events, 0.2 us)
Async XLA Ops:
  2.0 13.8 %collective-permute-start = (f32[4,64,512]{2,1,0:T(8,128)S(1)}, f32[4,64,512]{2,1,0:T(8,128)S(1)}, u32[]{:S(2)}, u32[]{:S(2)}) collective-permute-start(f32[4,64,512]{2,1,0:T(8,128)S(1)} %get-tuple-element.35), channel_id=1, source_target_pairs={{0,4},{1,5},{2,6},{3,7},{4,0},{5,1},{6,2},{7,3},{8,12},{9,13},{10,... | collective-permute-start | bytes 1572872 | tf_op jit(solution)/shard_map/ppermute | solution.py:712
  2.7 21.2 %collective-permute-start.2 = (f32[4,256,128]{2,1,0:T(8,128)S(1)}, f32[4,256,128]{2,1,0:T(8,128)S(1)}, u32[]{:S(2)}, u32[]{:S(2)}) collective-permute-start(f32[4,256,128]{2,1,0:T(8,128)S(1)} %get-tuple-element.43), channel_id=1, source_target_pairs={{0,1},{1,0},{2,3},{3,2},{4,5},{5,4},{6,7},{7,6},{8,9},{9,8},{10,11... | collective-permute-start | bytes 1572872 | tf_op jit(solution)/shard_map/ppermute | solution.py:712
  2.9 21.0 %collective-permute-start.3 = (f32[4,256,128]{2,1,0:T(8,128)S(1)}, f32[4,256,128]{2,1,0:T(8,128)S(1)}, u32[]{:S(2)}, u32[]{:S(2)}) collective-permute-start(f32[4,256,128]{2,1,0:T(8,128)S(1)} %get-tuple-element.44), channel_id=1, source_target_pairs={{1,2},{2,1},{5,6},{6,5},{9,10},{10,9},{13,14},{14,13},{17,18},{18,... | collective-permute-start | bytes 1572872 | tf_op jit(solution)/shard_map/ppermute | solution.py:712
  7.2 8.6 %collective-permute-start.1 = (f32[4,64,128]{2,1,0:T(8,128)S(1)}, f32[4,64,128]{2,1,0:T(8,128)S(1)}, u32[]{:S(2)}, u32[]{:S(2)}) collective-permute-start(f32[4,64,128]{2,1,0:T(8,128)S(1)} %get-tuple-element.36), channel_id=1, source_target_pairs={{4,8},{5,9},{6,10},{7,11},{8,4},{9,5},{10,6},{11,7},{12,16},{13,17... | collective-permute-start | bytes 393224 | tf_op jit(solution)/shard_map/ppermute | solution.py:712
  10.9 18.5 %collective-permute-start.6 = (f32[4,64,512]{2,1,0:T(8,128)S(1)}, f32[4,64,512]{2,1,0:T(8,128)S(1)}, u32[]{:S(2)}, u32[]{:S(2)}) collective-permute-start(f32[4,64,512]{2,1,0:T(8,128)S(1)} %get-tuple-element.53), channel_id=1, source_target_pairs={{4,8},{5,9},{6,10},{7,11},{8,4},{9,5},{10,6},{11,7},{12,16},{13,17... | collective-permute-start | bytes 1572872 | tf_op jit(solution)/shard_map/ppermute | solution.py:712
  16.0 13.4 %collective-permute-start.4 = (f32[4,64,128]{2,1,0:T(8,128)S(1)}, f32[4,64,128]{2,1,0:T(8,128)S(1)}, u32[]{:S(2)}, u32[]{:S(2)}) collective-permute-start(f32[4,64,128]{2,1,0:T(8,128)S(1)} %get-tuple-element.51), channel_id=1, source_target_pairs={{0,1},{1,0},{2,3},{3,2},{4,5},{5,4},{6,7},{7,6},{8,9},{9,8},{10,11... | collective-permute-start | bytes 393224 | tf_op jit(solution)/shard_map/ppermute | solution.py:712
  16.1 13.3 %collective-permute-start.5 = (f32[4,64,128]{2,1,0:T(8,128)S(1)}, f32[4,64,128]{2,1,0:T(8,128)S(1)}, u32[]{:S(2)}, u32[]{:S(2)}) collective-permute-start(f32[4,64,128]{2,1,0:T(8,128)S(1)} %get-tuple-element.52), channel_id=1, source_target_pairs={{1,2},{2,1},{5,6},{6,5},{9,10},{10,9},{13,14},{14,13},{17,18},{18,... | collective-permute-start | bytes 393224 | tf_op jit(solution)/shard_map/ppermute | solution.py:712
  18.0 0.7 %copy-start = (s32[1,1,9,2]{2,3,1,0:T(2,128)S(1)}, s32[1,1,9,2]{2,3,1,0:T(2,128)}, u32[]{:S(2)}) copy-start(s32[1,1,9,2]{2,3,1,0:T(2,128)} %param.10) | copy-start | bytes 220
  39.5 7.8 %collective-permute-start.7 = (f32[4,64,640]{2,1,0:T(8,128)S(1)}, f32[4,64,640]{2,1,0:T(8,128)S(1)}, u32[]{:S(2)}, u32[]{:S(2)}) collective-permute-start(f32[4,64,640]{2,1,0:T(8,128)S(1)} %get-tuple-element.55), channel_id=1, source_target_pairs={{0,4},{1,5},{2,6},{3,7},{4,0},{5,1},{6,2},{7,3},{8,12},{9,13},{10,... | collective-permute-start | bytes 1966088 | tf_op jit(solution)/shard_map/ppermute | solution.py:712
  39.6 7.8 %collective-permute-start.9 = (f32[4,64,128]{2,1,0:T(8,128)S(1)}, f32[4,64,128]{2,1,0:T(8,128)S(1)}, u32[]{:S(2)}, u32[]{:S(2)}) collective-permute-start(f32[4,64,128]{2,1,0:T(8,128)S(1)} %get-tuple-element.61), channel_id=1, source_target_pairs={{4,8},{5,9},{6,10},{7,11},{8,4},{9,5},{10,6},{11,7},{12,16},{13,17... | collective-permute-start | bytes 393224 | tf_op jit(solution)/shard_map/ppermute | solution.py:712
  42.6 16.0 %collective-permute-start.8 = (f32[4,64,512]{2,1,0:T(8,128)S(1)}, f32[4,64,512]{2,1,0:T(8,128)S(1)}, u32[]{:S(2)}, u32[]{:S(2)}) collective-permute-start(f32[4,64,512]{2,1,0:T(8,128)S(1)} %get-tuple-element.56), channel_id=1, source_target_pairs={{4,8},{5,9},{6,10},{7,11},{8,4},{9,5},{10,6},{11,7},{12,16},{13,17... | collective-permute-start | bytes 1572872 | tf_op jit(solution)/shard_map/ppermute | solution.py:712
  47.5 13.5 %collective-permute-start.10 = (f32[4,256,128]{2,1,0:T(8,128)S(1)}, f32[4,256,128]{2,1,0:T(8,128)S(1)}, u32[]{:S(2)}, u32[]{:S(2)}) collective-permute-start(f32[4,256,128]{2,1,0:T(8,128)S(1)} %get-tuple-element.62), channel_id=1, source_target_pairs={{0,1},{1,0},{2,3},{3,2},{4,5},{5,4},{6,7},{7,6},{8,9},{9,8},{10,11... | collective-permute-start | bytes 1572872 | tf_op jit(solution)/shard_map/ppermute | solution.py:712
  48.3 14.7 %collective-permute-start.11 = (f32[4,256,128]{2,1,0:T(8,128)S(1)}, f32[4,256,128]{2,1,0:T(8,128)S(1)}, u32[]{:S(2)}, u32[]{:S(2)}) collective-permute-start(f32[4,256,128]{2,1,0:T(8,128)S(1)} %get-tuple-element.63), channel_id=1, source_target_pairs={{1,2},{2,1},{5,6},{6,5},{9,10},{10,9},{13,14},{14,13},{17,18},{18,... | collective-permute-start | bytes 1572872 | tf_op jit(solution)/shard_map/ppermute | solution.py:712

commit v9 on v8

--- a/solution.py
+++ b/solution.py
@@ -511,15 +511,17 @@
         for k in range(tiles):
             gradient[ch, k + 1, :HALO] = jnp.zeros((HALO, LANES), jnp.float32)
             gradient[ch, k + 1, HALO + tile :] = jnp.zeros((bottom, LANES), jnp.float32)
-    for copy in loads:
+    for copy in loads[:3]:
         copy.wait()
     for part in range(2):
         spectrum[part] = reorder(held[part], tables[4], stage.at[part])
     for which in range(patterns.shape[0]):
-        amplitudes[which] = reorder(patterns[which], tables[5], stage.at[which % 2])
         _, _, down, right = place_of(offsets, which)
         for part in range(2):
             probes[which, part] = rolled(probe[part], down, right)
+    loads[3].wait()
+    for which in range(patterns.shape[0]):
+        amplitudes[which] = reorder(patterns[which], tables[5], stage.at[which % 2])
     for copy in copies:
         copy.wait()
 

time: 65 us -> 64.7 us (level)
  transfers between devices with their start and end apart: 12 -> 12, of which waited for: 5 -> 5; matrix products, arithmetic and copies ran while one was open for 0% -> 0% of each run, Pallas kernels for 19% -> 18%
where the time goes in v9:
time: 64.7 us; the launch traced here: 64.5 us
  Pallas kernels  25.6 us (40%)
  starting transfers between devices  24.1 us (37%)
  waiting for transfers between devices  13.8 us (21%)
  local copies, waits for them, and re-layouts  0.67 us (1%)
    ppermute x12, starting transfers between devices, swap(): return lax.ppermute(x, ('row', 'col'), pairs)  24.1 us
    ppermute x12, waiting for transfers between devices, swap(): return lax.ppermute(x, ('row', 'col'), pairs)  13.8 us
    pallas_call x1, Pallas kernels, late(): pl.pallas_call(late_body, out_shape=[floats(*padded.shape), floats(*gradi...  10.1 us
    pallas_call x1, Pallas kernels, early(): pl.pallas_call(early_body, out_shape=[floats(*padded.shape), floats(*grad...  5.29 us
    pallas_call x1, Pallas kernels, prepare(): pl.pallas_call(prepare_body, out_shape=[floats(*padded.shape), floats(*pa...  4.88 us
    pallas_call x1, Pallas kernels, pack(): pl.pallas_call(pack_body, out_shape=(extended, strip, strip, rows, rows,...  1.98 us
    pallas_call x1, Pallas kernels, settle(): pl.pallas_call(border_body, in_specs=[WHOLE, far, WHOLE, WHOLE], input_ou...  1.59 us
    pallas_call x1, Pallas kernels, settle(): pl.pallas_call(inside_body, in_specs=[WHOLE] * 3, input_output_aliases={0...  1.39 us
  transfers between devices with their start and end apart: 12, of which 5 were waited for; matrix products, arithmetic and copies ran while one was open for 0% of the time, Pallas kernels for 18%

profile of v9, /device:TPU:11, one launch (start us, length us, event | category | flops | bytes accessed | tf_op | source)
XLA Modules:
  0.0 64.5 jit_solution(14955797513254788501)
XLA Ops:
  0.0 2.0 %pack.1 = (f32[4,6,648,128]{3,2,1,0:T(8,128)S(1)}, f32[4,256,128]{2,1,0:T(8,128)S(1)}, f32[4,256,128]{2,1,0:T(8,128)S(1)}, f32[4,64,512]{2,1,0:T(8,128)S(1)}, f3...) custom-call(f32[4,512,512]{2,1,0:T(8,128)} %objects.3), custom_call_target="tpu_custom_call" | custom-call | tf_op jit(solution)/shard_map/pack/pallas_call | solution.py:243
  2.0 0.7 %collective-permute-start = (f32[4,64,512]{2,1,0:T(8,128)S(1)}, f32[4,64,512]{2,1,0:T(8,128)S(1)}, u32[]{:S(2)}, u32[]{:S(2)}) collective-permute-start(f32[4,64,512]{2,1,0:T(8,128)S(1)} %get-tuple-element.35), channel_id=1, source_target_pairs={{0,4},{1,5},{2,6},{3,7},{4,0},{5,1},{6,2},{7,3},{8,12},{9,13},{10,... | collective-permute-start | bytes 1572872 | tf_op jit(solution)/shard_map/ppermute | solution.py:714
  2.7 0.2 collective-permute-start.2
  2.9 4.3 %collective-permute-start.3 = (f32[4,256,128]{2,1,0:T(8,128)S(1)}, f32[4,256,128]{2,1,0:T(8,128)S(1)}, u32[]{:S(2)}, u32[]{:S(2)}) collective-permute-start(f32[4,256,128]{2,1,0:T(8,128)S(1)} %get-tuple-element.44), channel_id=1, source_target_pairs={{1,2},{2,1},{5,6},{6,5},{9,10},{10,9},{13,14},{14,13},{17,18},{18,... | collective-permute-start | bytes 1572872 | tf_op jit(solution)/shard_map/ppermute | solution.py:714
  7.2 3.6 %collective-permute-start.1 = (f32[4,64,128]{2,1,0:T(8,128)S(1)}, f32[4,64,128]{2,1,0:T(8,128)S(1)}, u32[]{:S(2)}, u32[]{:S(2)}) collective-permute-start(f32[4,64,128]{2,1,0:T(8,128)S(1)} %get-tuple-element.36), channel_id=1, source_target_pairs={{4,8},{5,9},{6,10},{7,11},{8,4},{9,5},{10,6},{11,7},{12,16},{13,17... | collective-permute-start | bytes 393224 | tf_op jit(solution)/shard_map/ppermute | solution.py:714
  10.9 2.8 %collective-permute-start.6 = (f32[4,64,512]{2,1,0:T(8,128)S(1)}, f32[4,64,512]{2,1,0:T(8,128)S(1)}, u32[]{:S(2)}, u32[]{:S(2)}) collective-permute-start(f32[4,64,512]{2,1,0:T(8,128)S(1)} %get-tuple-element.53), channel_id=1, source_target_pairs={{4,8},{5,9},{6,10},{7,11},{8,4},{9,5},{10,6},{11,7},{12,16},{13,17... | collective-permute-start | bytes 1572872 | tf_op jit(solution)/shard_map/ppermute | solution.py:714
  13.7 2.1 %collective-permute-done.1.co = f32[4,64,128]{2,1,0:T(8,128)S(1)} collective-permute-done((f32[4,64,128]{2,1,0:T(8,128)S(1)}, f32[4,64,128]{2,1,0:T(8,128)S(1)}, u32[]{:S(2)}, u32[]{:S(2)}) %collective-permute-start.1) | collective-permute-done | bytes 131104 | tf_op jit(solution)/shard_map/ppermute | solution.py:714
  15.8 0.1 extend.1
  16.1 1.9 %collective-permute-start.5 = (f32[4,64,128]{2,1,0:T(8,128)S(1)}, f32[4,64,128]{2,1,0:T(8,128)S(1)}, u32[]{:S(2)}, u32[]{:S(2)}) collective-permute-start(f32[4,64,128]{2,1,0:T(8,128)S(1)} %get-tuple-element.52), channel_id=1, source_target_pairs={{1,2},{2,1},{5,6},{6,5},{9,10},{10,9},{13,14},{14,13},{17,18},{18,... | collective-permute-start | bytes 393224 | tf_op jit(solution)/shard_map/ppermute | solution.py:714
  18.0 0.7 %copy-done = s32[1,1,9,2]{2,3,1,0:T(2,128)S(1)} copy-done((s32[1,1,9,2]{2,3,1,0:T(2,128)S(1)}, s32[1,1,9,2]{2,3,1,0:T(2,128)}, u32[]{:S(2)}) %copy-start) | copy-done | bytes 96
  18.7 4.9 %prepare.1 = (f32[4,6,648,128]{3,2,1,0:T(8,128)S(1)}, f32[4,6,648,128]{3,2,1,0:T(8,128)S(1)}, f32[9,2,256,256]{3,2,1,0:T(8,128)S(1)}, bf16[6,256,256]{2,1,0:T(8,...) custom-call(s32[2,9]{1,0:T(2,128)S(1)} %bitcast.4, ...), custom_call_target="tpu_custom_call", output_to_operand_aliasing={{0}: (1, {})} | custom-call | flops 1610612736 | bytes 524288 | tf_op jit(solution)/shard_map/prepare/pallas_call | solution.py:570
  23.6 5.3 %early.1 = (f32[4,6,648,128]{3,2,1,0:T(8,128)S(1)}, f32[4,6,648,128]{3,2,1,0:T(8,128)S(1)}) custom-call(s32[2,9]{1,0:T(2,128)S(1)} %bitcast.5, f32[4,6,648,128]{3,2,1,0:T(8,128)S(1)} %get-tuple-element.41.padded_in, f32[4,6,648,128]{3,2,1,0:T(8,128)S(1)} %get-tuple-element.42.gradient_in, ...), custom_call_target="tpu_custom_call", output_to_operand_aliasing={{0}: (1, {}), {1}: (2, {})} | custom-call | flops 2415919104 | bytes 786432 | tf_op jit(solution)/shard_map/early/pallas_call | solution.py:598
  28.9 10.1 %late.1 = (f32[4,6,648,128]{3,2,1,0:T(8,128)S(1)}, f32[4,6,648,128]{3,2,1,0:T(8,128)S(1)}, f32[4,256,128]{2,1,0:T(8,128)S(1)}, f32[4,256,128]{2,1,0:T(8,128)S(1)...) custom-call(s32[2,9]{1,0:T(2,128)S(1)} %bitcast.6, ...), custom_call_target="tpu_custom_call", output_to_operand_aliasing={{0}: (1, {}), {1}: (2, {})} | custom-call | flops 7247757312 | bytes 2359296 | tf_op jit(solution)/shard_map/late/pallas_call | solution.py:616
  39.1 3.1 %collective-permute-start.9 = (f32[4,64,128]{2,1,0:T(8,128)S(1)}, f32[4,64,128]{2,1,0:T(8,128)S(1)}, u32[]{:S(2)}, u32[]{:S(2)}) collective-permute-start(f32[4,64,128]{2,1,0:T(8,128)S(1)} %get-tuple-element.61), channel_id=1, source_target_pairs={{4,8},{5,9},{6,10},{7,11},{8,4},{9,5},{10,6},{11,7},{12,16},{13,17... | collective-permute-start | bytes 393224 | tf_op jit(solution)/shard_map/ppermute | solution.py:714
  42.2 3.4 %collective-permute-start.8 = (f32[4,64,512]{2,1,0:T(8,128)S(1)}, f32[4,64,512]{2,1,0:T(8,128)S(1)}, u32[]{:S(2)}, u32[]{:S(2)}) collective-permute-start(f32[4,64,512]{2,1,0:T(8,128)S(1)} %get-tuple-element.56), channel_id=1, source_target_pairs={{4,8},{5,9},{6,10},{7,11},{8,4},{9,5},{10,6},{11,7},{12,16},{13,17... | collective-permute-start | bytes 1572872 | tf_op jit(solution)/shard_map/ppermute | solution.py:714
  45.6 1.3 %collective-permute-done.9.co = f32[4,64,128]{2,1,0:T(8,128)S(1)} collective-permute-done((f32[4,64,128]{2,1,0:T(8,128)S(1)}, f32[4,64,128]{2,1,0:T(8,128)S(1)}, u32[]{:S(2)}, u32[]{:S(2)}) %collective-permute-start.9) | collective-permute-done | bytes 131104 | tf_op jit(solution)/shard_map/ppermute | solution.py:714
  46.9 0.2 gather.1
  47.0 0.8 %collective-permute-start.10 = (f32[4,256,128]{2,1,0:T(8,128)S(1)}, f32[4,256,128]{2,1,0:T(8,128)S(1)}, u32[]{:S(2)}, u32[]{:S(2)}) collective-permute-start(f32[4,256,128]{2,1,0:T(8,128)S(1)} %get-tuple-element.62), channel_id=1, source_target_pairs={{0,1},{1,0},{2,3},{3,2},{4,5},{5,4},{6,7},{7,6},{8,9},{9,8},{10,11... | collective-permute-start | bytes 1572872 | tf_op jit(solution)/shard_map/ppermute | solution.py:714
  47.9 3.0 %collective-permute-start.11 = (f32[4,256,128]{2,1,0:T(8,128)S(1)}, f32[4,256,128]{2,1,0:T(8,128)S(1)}, u32[]{:S(2)}, u32[]{:S(2)}) collective-permute-start(f32[4,256,128]{2,1,0:T(8,128)S(1)} %get-tuple-element.63), channel_id=1, source_target_pairs={{1,2},{2,1},{5,6},{6,5},{9,10},{10,9},{13,14},{14,13},{17,18},{18,... | collective-permute-start | bytes 1572872 | tf_op jit(solution)/shard_map/ppermute | solution.py:714
  50.9 7.3 %collective-permute-done.8.ro = f32[4,64,512]{2,1,0:T(8,128)S(1)} collective-permute-done((f32[4,64,512]{2,1,0:T(8,128)S(1)}, f32[4,64,512]{2,1,0:T(8,128)S(1)}, u32[]{:S(2)}, u32[]{:S(2)}) %collective-permute-start.8) | collective-permute-done | bytes 524320 | tf_op jit(solution)/shard_map/ppermute | solution.py:714
  58.1 1.4 %inside.1 = (f32[4,6,648,128]{3,2,1,0:T(8,128)S(1)}, f32[4,512,512]{2,1,0:T(8,128)}) custom-call(f32[4,6,648,128]{3,2,1,0:T(8,128)S(1)} %get-tuple-element.54.gradient_in, f32[4,64,640]{2,1,0:T(8,128)S(1)} %collective-permute-done.7.re, f32[4,64,512]{2,1,0:T(8,128)S(1)} %collective-permute-done.8.ro), custom_call_target="tpu_custom_call", output_to_operand_aliasing={{0}: (0, {})} | custom-call | tf_op jit(solution)/shard_map/inside/pallas_call | solution.py:686
  59.5 1.0 %collective-permute-done.10.ze = f32[4,256,128]{2,1,0:T(8,128)S(1)} collective-permute-done((f32[4,256,128]{2,1,0:T(8,128)S(1)}, f32[4,256,128]{2,1,0:T(8,128)S(1)}, u32[]{:S(2)}, u32[]{:S(2)}) %collective-permute-start.10) | collective-permute-done | bytes 524320 | tf_op jit(solution)/shard_map/ppermute | solution.py:714
  60.5 2.2 %collective-permute-done.11.zo = f32[4,256,128]{2,1,0:T(8,128)S(1)} collective-permute-done((f32[4,256,128]{2,1,0:T(8,128)S(1)}, f32[4,256,128]{2,1,0:T(8,128)S(1)}, u32[]{:S(2)}, u32[]{:S(2)}) %collective-permute-start.11) | collective-permute-done | bytes 524320 | tf_op jit(solution)/shard_map/ppermute | solution.py:714
  62.7 1.6 %border.1 = (f32[4,6,648,128]{3,2,1,0:T(8,128)S(1)}, f32[4,512,512]{2,1,0:T(8,128)}) custom-call(f32[4,6,648,128]{3,2,1,0:T(8,128)S(1)} %get-tuple-element.57.gradient_in, f32[4,512,512]{2,1,0:T(8,128)} %get-tuple-element.58.out_in, f32[4,256,128]{2,1,0:T(8,128)S(1)} %collective-permute-done.10.ze, ...), custom_call_target="tpu_custom_call", output_to_operand_aliasing={{0}: (0, {}), {1}: (1, {})} | custom-call | tf_op jit(solution)/shard_map/border/pallas_call | solution.py:693
  (10 shorter events, 0.2 us)
Async XLA Ops:
  2.0 13.8 %collective-permute-start = (f32[4,64,512]{2,1,0:T(8,128)S(1)}, f32[4,64,512]{2,1,0:T(8,128)S(1)}, u32[]{:S(2)}, u32[]{:S(2)}) collective-permute-start(f32[4,64,512]{2,1,0:T(8,128)S(1)} %get-tuple-element.35), channel_id=1, source_target_pairs={{0,4},{1,5},{2,6},{3,7},{4,0},{5,1},{6,2},{7,3},{8,12},{9,13},{10,... | collective-permute-start | bytes 1572872 | tf_op jit(solution)/shard_map/ppermute | solution.py:714
  2.7 20.8 %collective-permute-start.2 = (f32[4,256,128]{2,1,0:T(8,128)S(1)}, f32[4,256,128]{2,1,0:T(8,128)S(1)}, u32[]{:S(2)}, u32[]{:S(2)}) collective-permute-start(f32[4,256,128]{2,1,0:T(8,128)S(1)} %get-tuple-element.43), channel_id=1, source_target_pairs={{0,1},{1,0},{2,3},{3,2},{4,5},{5,4},{6,7},{7,6},{8,9},{9,8},{10,11... | collective-permute-start | bytes 1572872 | tf_op jit(solution)/shard_map/ppermute | solution.py:714
  2.9 20.6 %collective-permute-start.3 = (f32[4,256,128]{2,1,0:T(8,128)S(1)}, f32[4,256,128]{2,1,0:T(8,128)S(1)}, u32[]{:S(2)}, u32[]{:S(2)}) collective-permute-start(f32[4,256,128]{2,1,0:T(8,128)S(1)} %get-tuple-element.44), channel_id=1, source_target_pairs={{1,2},{2,1},{5,6},{6,5},{9,10},{10,9},{13,14},{14,13},{17,18},{18,... | collective-permute-start | bytes 1572872 | tf_op jit(solution)/shard_map/ppermute | solution.py:714
  7.2 8.6 %collective-permute-start.1 = (f32[4,64,128]{2,1,0:T(8,128)S(1)}, f32[4,64,128]{2,1,0:T(8,128)S(1)}, u32[]{:S(2)}, u32[]{:S(2)}) collective-permute-start(f32[4,64,128]{2,1,0:T(8,128)S(1)} %get-tuple-element.36), channel_id=1, source_target_pairs={{4,8},{5,9},{6,10},{7,11},{8,4},{9,5},{10,6},{11,7},{12,16},{13,17... | collective-permute-start | bytes 393224 | tf_op jit(solution)/shard_map/ppermute | solution.py:714
  10.9 18.0 %collective-permute-start.6 = (f32[4,64,512]{2,1,0:T(8,128)S(1)}, f32[4,64,512]{2,1,0:T(8,128)S(1)}, u32[]{:S(2)}, u32[]{:S(2)}) collective-permute-start(f32[4,64,512]{2,1,0:T(8,128)S(1)} %get-tuple-element.53), channel_id=1, source_target_pairs={{4,8},{5,9},{6,10},{7,11},{8,4},{9,5},{10,6},{11,7},{12,16},{13,17... | collective-permute-start | bytes 1572872 | tf_op jit(solution)/shard_map/ppermute | solution.py:714
  16.0 12.9 %collective-permute-start.4 = (f32[4,64,128]{2,1,0:T(8,128)S(1)}, f32[4,64,128]{2,1,0:T(8,128)S(1)}, u32[]{:S(2)}, u32[]{:S(2)}) collective-permute-start(f32[4,64,128]{2,1,0:T(8,128)S(1)} %get-tuple-element.51), channel_id=1, source_target_pairs={{0,1},{1,0},{2,3},{3,2},{4,5},{5,4},{6,7},{7,6},{8,9},{9,8},{10,11... | collective-permute-start | bytes 393224 | tf_op jit(solution)/shard_map/ppermute | solution.py:714
  16.1 12.8 %collective-permute-start.5 = (f32[4,64,128]{2,1,0:T(8,128)S(1)}, f32[4,64,128]{2,1,0:T(8,128)S(1)}, u32[]{:S(2)}, u32[]{:S(2)}) collective-permute-start(f32[4,64,128]{2,1,0:T(8,128)S(1)} %get-tuple-element.52), channel_id=1, source_target_pairs={{1,2},{2,1},{5,6},{6,5},{9,10},{10,9},{13,14},{14,13},{17,18},{18,... | collective-permute-start | bytes 393224 | tf_op jit(solution)/shard_map/ppermute | solution.py:714
  18.0 0.7 %copy-start = (s32[1,1,9,2]{2,3,1,0:T(2,128)S(1)}, s32[1,1,9,2]{2,3,1,0:T(2,128)}, u32[]{:S(2)}) copy-start(s32[1,1,9,2]{2,3,1,0:T(2,128)} %param.10) | copy-start | bytes 220
  39.0 7.8 %collective-permute-start.7 = (f32[4,64,640]{2,1,0:T(8,128)S(1)}, f32[4,64,640]{2,1,0:T(8,128)S(1)}, u32[]{:S(2)}, u32[]{:S(2)}) collective-permute-start(f32[4,64,640]{2,1,0:T(8,128)S(1)} %get-tuple-element.55), channel_id=1, source_target_pairs={{0,4},{1,5},{2,6},{3,7},{4,0},{5,1},{6,2},{7,3},{8,12},{9,13},{10,... | collective-permute-start | bytes 1966088 | tf_op jit(solution)/shard_map/ppermute | solution.py:714
  39.1 7.7 %collective-permute-start.9 = (f32[4,64,128]{2,1,0:T(8,128)S(1)}, f32[4,64,128]{2,1,0:T(8,128)S(1)}, u32[]{:S(2)}, u32[]{:S(2)}) collective-permute-start(f32[4,64,128]{2,1,0:T(8,128)S(1)} %get-tuple-element.61), channel_id=1, source_target_pairs={{4,8},{5,9},{6,10},{7,11},{8,4},{9,5},{10,6},{11,7},{12,16},{13,17... | collective-permute-start | bytes 393224 | tf_op jit(solution)/shard_map/ppermute | solution.py:714
  42.2 15.9 %collective-permute-start.8 = (f32[4,64,512]{2,1,0:T(8,128)S(1)}, f32[4,64,512]{2,1,0:T(8,128)S(1)}, u32[]{:S(2)}, u32[]{:S(2)}) collective-permute-start(f32[4,64,512]{2,1,0:T(8,128)S(1)} %get-tuple-element.56), channel_id=1, source_target_pairs={{4,8},{5,9},{6,10},{7,11},{8,4},{9,5},{10,6},{11,7},{12,16},{13,17... | collective-permute-start | bytes 1572872 | tf_op jit(solution)/shard_map/ppermute | solution.py:714
  47.0 13.5 %collective-permute-start.10 = (f32[4,256,128]{2,1,0:T(8,128)S(1)}, f32[4,256,128]{2,1,0:T(8,128)S(1)}, u32[]{:S(2)}, u32[]{:S(2)}) collective-permute-start(f32[4,256,128]{2,1,0:T(8,128)S(1)} %get-tuple-element.62), channel_id=1, source_target_pairs={{0,1},{1,0},{2,3},{3,2},{4,5},{5,4},{6,7},{7,6},{8,9},{9,8},{10,11... | collective-permute-start | bytes 1572872 | tf_op jit(solution)/shard_map/ppermute | solution.py:714
  47.9 14.8 %collective-permute-start.11 = (f32[4,256,128]{2,1,0:T(8,128)S(1)}, f32[4,256,128]{2,1,0:T(8,128)S(1)}, u32[]{:S(2)}, u32[]{:S(2)}) collective-permute-start(f32[4,256,128]{2,1,0:T(8,128)S(1)} %get-tuple-element.63), channel_id=1, source_target_pairs={{1,2},{2,1},{5,6},{6,5},{9,10},{10,9},{13,14},{14,13},{17,18},{18,... | collective-permute-start | bytes 1572872 | tf_op jit(solution)/shard_map/ppermute | solution.py:714
